TPU v7x, 128 devices: a whole 4x4x4 slice. The times are simulated.
128 devices in a mesh: seq: 32 (over z_lo, y, x), head: 4 (over z_hi, core).
Axes of the slice: x: 4, y: 4, z: 4 (z_hi: 2, z_lo: 2; z = z_hi * 2 + z_lo), core: 2. Of those that a mesh axis runs over, the one named last changes fastest.
Arguments:
- query: bfloat16 [4096, 96, 128], P(('seq', 'head')), may hold values from -15.6 to 15.6
- key_new: bfloat16 [4096, 8, 128], P('seq', 'head'), may hold values from -6 to 6
- value_new: bfloat16 [4096, 8, 128], P('seq', 'head'), may hold values from -6 to 6
- key_old: bfloat16 [4096, 8, 128], P('seq', 'head'), may hold values from -6 to 6
- value_old: bfloat16 [4096, 8, 128], P('seq', 'head'), may hold values from -6 to 6
- offset: int32 [1], replicated, may hold values from 0 to 4095
- windows: int32 [8], P('head'), may hold values from 2048 to 4096, as said below
- grad_out: bfloat16 [4096, 96, 128], P(('seq', 'head')), may hold values from -6 to 6
Outputs:
- grad_query: float32 [4096, 96, 128], P(('seq', 'head'))
- grad_key_new: float32 [4096, 8, 128], P('seq', 'head')
- grad_value_new: float32 [4096, 8, 128], P('seq', 'head')
- grad_key_old: float32 [4096, 8, 128], P('seq', 'head')
- grad_value_old: float32 [4096, 8, 128], P('seq', 'head')
Inputs may be any that keep to these rules, and one draw needn't show every extreme that they name: `windows`: one key-value head has a window of exactly 4096 tokens and another of exactly 2048.
All inputs are finite; a program needn't handle non-finite values.
Results may differ from a plain program's by a relative error of at most 0.003.
Values may be sent and summed in bfloat16 or wider, within the bound.
No kernel may reach another device: no remote copies, remote signals or barrier semaphores. Data moves between devices by JAX's collectives and lax.ppermute only.
A program may use at most 128 MiB of HBM per device.

v0:
```python
import math

import jax
import jax.numpy as jnp
from jax import lax
from jax.sharding import PartitionSpec as P


def from_behind(block, axis, distance):
    devices = range(lax.axis_size(axis))
    route = [((i - distance) % len(devices), i) for i in devices]
    return lax.ppermute(block, axis, route)


def score_tile(operand, partner):
    return jnp.einsum("qgjd,kgd->qgjk", operand, partner, preferred_element_type=jnp.float32)


def visible_mask(key_pos, query_pos, reaches):
    key_row = key_pos[None, None, None, :]
    query_col = query_pos[:, None, None, None]
    return (key_row <= query_col) & (key_row > query_col - reaches[None, :, None, None])


def shards(query, key_new, value_new, key_old, value_old, offset, windows, grad_out):
    queries, out_grads = (
        lax.all_to_all(query, "head", split_axis=1, concat_axis=0, tiled=True),
        lax.all_to_all(grad_out, "head", split_axis=1, concat_axis=0, tiled=True),
    )
    tok_rows, head_count, head_width = queries.shape
    group_count = key_new.shape[1]
    per_group = head_count // group_count
    seq_count = lax.axis_size("seq")
    seq_rank = lax.axis_index("seq")
    total_rows = tok_rows * seq_count
    score_scale = 1.0 / math.sqrt(head_width)
    queries = queries.reshape(tok_rows, group_count, per_group, head_width)
    out_grads = out_grads.reshape(tok_rows, group_count, per_group, head_width)
    first_query = seq_rank * tok_rows
    last_query = first_query + tok_rows - 1
    row_iota = jnp.arange(tok_rows, dtype=jnp.int32)
    query_pos = first_query + row_iota
    widest = jnp.max(windows)
    shift_at = offset[0]
    stored_pair = jnp.stack([key_old, value_old])
    new_home = jnp.stack([key_new, value_new])
    home_kv = jnp.concatenate([new_home, stored_pair])

    def old_positions(row_start, length):
        slot_index = row_start + jnp.arange(length, dtype=jnp.int32)
        return (slot_index - shift_at) % total_rows - total_rows

    def guarded(update, held_state, tile_pair, key_pos, allowed=True):
        touched = jnp.logical_and(
            allowed, jnp.any((key_pos <= last_query) & (key_pos > first_query - widest))
        )
        return lax.cond(
            touched,
            lambda state_in: update(state_in, tile_pair, key_pos),
            lambda state_in: state_in,
            held_state,
        )

    def stats_tile(held_state, tile_pair, key_pos):
        row_top, row_total, row_weighted = held_state
        seen = visible_mask(key_pos, query_pos, windows)
        masked = jnp.where(seen, score_scale * score_tile(queries, tile_pair[0]), -jnp.inf)
        weight_grad = score_tile(out_grads, tile_pair[1])
        new_top = jnp.maximum(row_top, jnp.max(masked, axis=-1))
        anchor = jnp.where(new_top == -jnp.inf, 0.0, new_top)
        shifted_exp = jnp.exp(masked - anchor[..., None])
        factor = jnp.exp(row_top - anchor)
        return (
            new_top,
            row_total * factor + jnp.sum(shifted_exp, axis=-1),
            row_weighted * factor + jnp.sum(shifted_exp * weight_grad, axis=-1),
        )

    def step_positions(step_index):
        owner_rows = (seq_rank - step_index) % seq_count * tok_rows
        return (owner_rows + row_iota, old_positions(owner_rows, tok_rows))

    def advance_keys(moving_kv):
        return from_behind(moving_kv, "seq", 1)

    def advance_sums(moving_grads):
        return from_behind(moving_grads, "seq", 1)

    def travel_stats(running, step_index, moving_kv):
        new_pos, old_pos = step_positions(step_index)
        running = guarded(stats_tile, running, moving_kv[0:2], new_pos)
        return guarded(stats_tile, running, moving_kv[2:4], old_pos)

    stat_shape = (tok_rows, group_count, per_group)
    empty_stats = (
        jnp.full(stat_shape, -jnp.inf, jnp.float32),
        jnp.zeros(stat_shape, jnp.float32),
        jnp.zeros(stat_shape, jnp.float32),
    )
    running = travel_stats(empty_stats, 0, home_kv)

    def pass_one(step_index, carried):
        moving_kv = advance_keys(carried[1])
        return (travel_stats(carried[0], step_index, moving_kv), moving_kv)

    running = lax.fori_loop(1, seq_count, pass_one, (running, home_kv))[0]
    log_total = running[0] + jnp.log(running[1])
    row_delta = running[2] / running[1]

    def grad_tile(held_state, tile_pair, key_pos):
        query_grad, held_sums = held_state
        seen = visible_mask(key_pos, query_pos, windows)
        weights = jnp.where(
            seen,
            jnp.exp(score_scale * score_tile(queries, tile_pair[0]) - log_total[..., None]),
            0.0,
        )
        weight_grad = score_tile(out_grads, tile_pair[1])
        dscore = (weights * (weight_grad - row_delta[..., None])).astype(jnp.bfloat16)
        weights_low = weights.astype(jnp.bfloat16)
        query_grad = query_grad + score_scale * jnp.einsum(
            "qgjk,kgd->qgjd", dscore, tile_pair[0], preferred_element_type=jnp.float32
        )
        key_part = score_scale * jnp.einsum(
            "qgjk,qgjd->kgd", dscore, queries, preferred_element_type=jnp.float32
        )
        value_part = jnp.einsum(
            "qgjk,qgjd->kgd", weights_low, out_grads, preferred_element_type=jnp.float32
        )
        return (query_grad, held_sums + jnp.stack([key_part, value_part]))

    def travel_grads(held_state, step_index, moving_kv):
        query_grad, moving_grads = held_state
        new_pos, old_pos = step_positions(step_index)
        query_grad, low_sums = guarded(
            grad_tile, (query_grad, moving_grads[0:2]), moving_kv[0:2], new_pos
        )
        query_grad, high_sums = guarded(
            grad_tile, (query_grad, moving_grads[2:4]), moving_kv[2:4], old_pos
        )
        return (query_grad, jnp.concatenate([low_sums, high_sums]))

    zero_query = jnp.zeros(queries.shape, jnp.float32)
    held_state = travel_grads((zero_query, jnp.zeros(home_kv.shape, jnp.float32)), 0, home_kv)

    def pass_two(step_index, carried):
        moving_kv = advance_keys(carried[1])
        moved_state = (carried[0][0], advance_sums(carried[0][1]))
        return (travel_grads(moved_state, step_index, moving_kv), moving_kv)

    held_state = lax.fori_loop(1, seq_count, pass_two, (held_state, home_kv))[0]
    held_state = (held_state[0], advance_sums(held_state[1]))
    query_grad, moving_grads = held_state
    old_grads = moving_grads[2:4]
    grad_query = lax.all_to_all(
        query_grad.reshape(tok_rows, head_count, head_width),
        "head",
        split_axis=0,
        concat_axis=1,
        tiled=True,
    )
    return (grad_query, moving_grads[0], moving_grads[1], old_grads[0], old_grads[1])


def solution(mesh):
    placed = (
        P(("seq", "head"), None, None),
        P("seq", "head", None),
        P("seq", "head", None),
        P("seq", "head", None),
        P("seq", "head", None),
        P(),
        P("head"),
        P(("seq", "head"), None, None),
    )
    return jax.shard_map(
        shards,
        mesh=mesh,
        in_specs=placed,
        out_specs=(
            P(("seq", "head"), None, None),
            P("seq", "head", None),
            P("seq", "head", None),
            P("seq", "head", None),
            P("seq", "head", None),
        ),
        check_vma=False,
    )
```

profile of v0, /device:TPU:32, one launch (start us, length us, event | category | flops | bytes accessed | tf_op | source)
XLA Modules:
  0.0 1434.0 jit_solution(16103889782191165589)
XLA Ops:
  25.1 12.1 all-to-all-done.1
  44.1 454.4 %while.44 = (s32[]{:T(128)}, f32[128,2,12]{0,2,1:T(8,128)}, f32[128,2,12]{0,2,1:T(8,128)S(1)}, f32[128,2,12]{0,2,1:T(8,128)S(1)}, bf16[4,128,2,128]{3,1,2,0:T(8,...) while((s32[]{:T(128)}, f32[128,2,12]{0,2,1:T(8,128)}, ...), condition=%wide.region_26.27_spmd.clone, body=%wide.region_13.26_spmd.clone.sunk | while | flops 409155072 | bytes 15362158 | solution.py:106
  61.7 8.2 collective-permute-done
  76.7 8.2 collective-permute-done
  91.6 8.2 collective-permute-done
  106.6 8.2 collective-permute-done
  121.5 8.2 collective-permute-done
  136.5 8.6 collective-permute-done
  151.9 9.8 collective-permute-done
  168.5 10.9 collective-permute-done
  186.2 10.1 collective-permute-done
  203.1 9.3 collective-permute-done
  219.1 8.4 collective-permute-done
  234.3 8.2 collective-permute-done
  249.2 8.2 collective-permute-done
  264.2 8.2 collective-permute-done
  279.1 8.2 collective-permute-done
  294.1 9.9 collective-permute-done
  307.4 9.0 collective-permute-done
  319.9 8.2 collective-permute-done
  331.4 8.2 collective-permute-done
  343.0 8.2 collective-permute-done
  354.6 8.2 collective-permute-done
  366.2 8.2 collective-permute-done
  377.7 9.2 collective-permute-done
  393.8 8.3 collective-permute-done
  408.8 8.2 collective-permute-done
  423.8 8.2 collective-permute-done
  438.8 8.2 collective-permute-done
  453.8 8.2 collective-permute-done
  468.7 10.7 collective-permute-done
  506.9 898.5 %while.45 = (s32[]{:T(128)}, f32[128,2,12,128]{3,0,2,1:T(8,128)S(1)}, f32[4,128,2,128]{3,1,2,0:T(8,128)}, bf16[4,128,2,128]{3,1,2,0:T(8,128)(2,1)}, s32[]{:T(128...) while((s32[]{:T(128)}, ...), condition=%wide.region_38.39_spmd.clone, body=%wide.region_31.38_spmd.clone.sunk | while | flops 1014337024 | bytes 40503600 | solution.py:151
  509.5 17.2 %collective-permute-done.2 = bf16[4,128,2,128]{3,1,2,0:T(8,128)(2,1)S(1)} collective-permute-done((bf16[4,128,2,128]{3,1,2,0:T(8,128)(2,1)}, bf16[4,128,2,128]{3,1,2,0:T(8,128)(2,1)S(1)}, u32[]{:S(2)}, u32[]{:S(2)}) %collective-permute-start.2) | collective-permute-done | bytes 262176 | tf_op jit(solution)/shard_map/while/body/eval_jaxpr/ppermute | solution.py:12
  538.5 18.3 %collective-permute-done.2 = bf16[4,128,2,128]{3,1,2,0:T(8,128)(2,1)S(1)} collective-permute-done((bf16[4,128,2,128]{3,1,2,0:T(8,128)(2,1)}, bf16[4,128,2,128]{3,1,2,0:T(8,128)(2,1)S(1)}, u32[]{:S(2)}, u32[]{:S(2)}) %collective-permute-start.2) | collective-permute-done | bytes 262176 | tf_op jit(solution)/shard_map/while/body/eval_jaxpr/ppermute | solution.py:12
  568.6 19.4 %collective-permute-done.2 = bf16[4,128,2,128]{3,1,2,0:T(8,128)(2,1)S(1)} collective-permute-done((bf16[4,128,2,128]{3,1,2,0:T(8,128)(2,1)}, bf16[4,128,2,128]{3,1,2,0:T(8,128)(2,1)S(1)}, u32[]{:S(2)}, u32[]{:S(2)}) %collective-permute-start.2) | collective-permute-done | bytes 262176 | tf_op jit(solution)/shard_map/while/body/eval_jaxpr/ppermute | solution.py:12
  599.7 20.5 %collective-permute-done.2 = bf16[4,128,2,128]{3,1,2,0:T(8,128)(2,1)S(1)} collective-permute-done((bf16[4,128,2,128]{3,1,2,0:T(8,128)(2,1)}, bf16[4,128,2,128]{3,1,2,0:T(8,128)(2,1)S(1)}, u32[]{:S(2)}, u32[]{:S(2)}) %collective-permute-start.2) | collective-permute-done | bytes 262176 | tf_op jit(solution)/shard_map/while/body/eval_jaxpr/ppermute | solution.py:12
  632.0 21.7 %collective-permute-done.2 = bf16[4,128,2,128]{3,1,2,0:T(8,128)(2,1)S(1)} collective-permute-done((bf16[4,128,2,128]{3,1,2,0:T(8,128)(2,1)}, bf16[4,128,2,128]{3,1,2,0:T(8,128)(2,1)S(1)}, u32[]{:S(2)}, u32[]{:S(2)}) %collective-permute-start.2) | collective-permute-done | bytes 262176 | tf_op jit(solution)/shard_map/while/body/eval_jaxpr/ppermute | solution.py:12
  665.4 21.6 %collective-permute-done.2 = bf16[4,128,2,128]{3,1,2,0:T(8,128)(2,1)S(1)} collective-permute-done((bf16[4,128,2,128]{3,1,2,0:T(8,128)(2,1)}, bf16[4,128,2,128]{3,1,2,0:T(8,128)(2,1)S(1)}, u32[]{:S(2)}, u32[]{:S(2)}) %collective-permute-start.2) | collective-permute-done | bytes 262176 | tf_op jit(solution)/shard_map/while/body/eval_jaxpr/ppermute | solution.py:12
  698.8 20.8 %collective-permute-done.2 = bf16[4,128,2,128]{3,1,2,0:T(8,128)(2,1)S(1)} collective-permute-done((bf16[4,128,2,128]{3,1,2,0:T(8,128)(2,1)}, bf16[4,128,2,128]{3,1,2,0:T(8,128)(2,1)S(1)}, u32[]{:S(2)}, u32[]{:S(2)}) %collective-permute-start.2) | collective-permute-done | bytes 262176 | tf_op jit(solution)/shard_map/while/body/eval_jaxpr/ppermute | solution.py:12
  731.4 19.9 %collective-permute-done.2 = bf16[4,128,2,128]{3,1,2,0:T(8,128)(2,1)S(1)} collective-permute-done((bf16[4,128,2,128]{3,1,2,0:T(8,128)(2,1)}, bf16[4,128,2,128]{3,1,2,0:T(8,128)(2,1)S(1)}, u32[]{:S(2)}, u32[]{:S(2)}) %collective-permute-start.2) | collective-permute-done | bytes 262176 | tf_op jit(solution)/shard_map/while/body/eval_jaxpr/ppermute | solution.py:12
  763.0 19.0 %collective-permute-done.2 = bf16[4,128,2,128]{3,1,2,0:T(8,128)(2,1)S(1)} collective-permute-done((bf16[4,128,2,128]{3,1,2,0:T(8,128)(2,1)}, bf16[4,128,2,128]{3,1,2,0:T(8,128)(2,1)S(1)}, u32[]{:S(2)}, u32[]{:S(2)}) %collective-permute-start.2) | collective-permute-done | bytes 262176 | tf_op jit(solution)/shard_map/while/body/eval_jaxpr/ppermute | solution.py:12
  793.8 18.1 %collective-permute-done.2 = bf16[4,128,2,128]{3,1,2,0:T(8,128)(2,1)S(1)} collective-permute-done((bf16[4,128,2,128]{3,1,2,0:T(8,128)(2,1)}, bf16[4,128,2,128]{3,1,2,0:T(8,128)(2,1)S(1)}, u32[]{:S(2)}, u32[]{:S(2)}) %collective-permute-start.2) | collective-permute-done | bytes 262176 | tf_op jit(solution)/shard_map/while/body/eval_jaxpr/ppermute | solution.py:12
  823.7 17.3 %collective-permute-done.2 = bf16[4,128,2,128]{3,1,2,0:T(8,128)(2,1)S(1)} collective-permute-done((bf16[4,128,2,128]{3,1,2,0:T(8,128)(2,1)}, bf16[4,128,2,128]{3,1,2,0:T(8,128)(2,1)S(1)}, u32[]{:S(2)}, u32[]{:S(2)}) %collective-permute-start.2) | collective-permute-done | bytes 262176 | tf_op jit(solution)/shard_map/while/body/eval_jaxpr/ppermute | solution.py:12
  852.7 16.5 %collective-permute-done.2 = bf16[4,128,2,128]{3,1,2,0:T(8,128)(2,1)S(1)} collective-permute-done((bf16[4,128,2,128]{3,1,2,0:T(8,128)(2,1)}, bf16[4,128,2,128]{3,1,2,0:T(8,128)(2,1)S(1)}, u32[]{:S(2)}, u32[]{:S(2)}) %collective-permute-start.2) | collective-permute-done | bytes 262176 | tf_op jit(solution)/shard_map/while/body/eval_jaxpr/ppermute | solution.py:12
  881.0 15.7 %collective-permute-done.2 = bf16[4,128,2,128]{3,1,2,0:T(8,128)(2,1)S(1)} collective-permute-done((bf16[4,128,2,128]{3,1,2,0:T(8,128)(2,1)}, bf16[4,128,2,128]{3,1,2,0:T(8,128)(2,1)S(1)}, u32[]{:S(2)}, u32[]{:S(2)}) %collective-permute-start.2) | collective-permute-done | bytes 262176 | tf_op jit(solution)/shard_map/while/body/eval_jaxpr/ppermute | solution.py:12
  908.5 14.9 %collective-permute-done.2 = bf16[4,128,2,128]{3,1,2,0:T(8,128)(2,1)S(1)} collective-permute-done((bf16[4,128,2,128]{3,1,2,0:T(8,128)(2,1)}, bf16[4,128,2,128]{3,1,2,0:T(8,128)(2,1)S(1)}, u32[]{:S(2)}, u32[]{:S(2)}) %collective-permute-start.2) | collective-permute-done | bytes 262176 | tf_op jit(solution)/shard_map/while/body/eval_jaxpr/ppermute | solution.py:12
  935.1 14.1 collective-permute-done.2
  960.9 16.3 %collective-permute-done.2 = bf16[4,128,2,128]{3,1,2,0:T(8,128)(2,1)S(1)} collective-permute-done((bf16[4,128,2,128]{3,1,2,0:T(8,128)(2,1)}, bf16[4,128,2,128]{3,1,2,0:T(8,128)(2,1)S(1)}, u32[]{:S(2)}, u32[]{:S(2)}) %collective-permute-start.2) | collective-permute-done | bytes 262176 | tf_op jit(solution)/shard_map/while/body/eval_jaxpr/ppermute | solution.py:12
  989.0 22.2 %collective-permute-done.2 = bf16[4,128,2,128]{3,1,2,0:T(8,128)(2,1)S(1)} collective-permute-done((bf16[4,128,2,128]{3,1,2,0:T(8,128)(2,1)}, bf16[4,128,2,128]{3,1,2,0:T(8,128)(2,1)S(1)}, u32[]{:S(2)}, u32[]{:S(2)}) %collective-permute-start.2) | collective-permute-done | bytes 262176 | tf_op jit(solution)/shard_map/while/body/eval_jaxpr/ppermute | solution.py:12
  1018.5 21.1 %collective-permute-done.2 = bf16[4,128,2,128]{3,1,2,0:T(8,128)(2,1)S(1)} collective-permute-done((bf16[4,128,2,128]{3,1,2,0:T(8,128)(2,1)}, bf16[4,128,2,128]{3,1,2,0:T(8,128)(2,1)S(1)}, u32[]{:S(2)}, u32[]{:S(2)}) %collective-permute-start.2) | collective-permute-done | bytes 262176 | tf_op jit(solution)/shard_map/while/body/eval_jaxpr/ppermute | solution.py:12
  1046.5 20.5 %collective-permute-done.2 = bf16[4,128,2,128]{3,1,2,0:T(8,128)(2,1)S(1)} collective-permute-done((bf16[4,128,2,128]{3,1,2,0:T(8,128)(2,1)}, bf16[4,128,2,128]{3,1,2,0:T(8,128)(2,1)S(1)}, u32[]{:S(2)}, u32[]{:S(2)}) %collective-permute-start.2) | collective-permute-done | bytes 262176 | tf_op jit(solution)/shard_map/while/body/eval_jaxpr/ppermute | solution.py:12
  1074.0 19.6 %collective-permute-done.2 = bf16[4,128,2,128]{3,1,2,0:T(8,128)(2,1)S(1)} collective-permute-done((bf16[4,128,2,128]{3,1,2,0:T(8,128)(2,1)}, bf16[4,128,2,128]{3,1,2,0:T(8,128)(2,1)S(1)}, u32[]{:S(2)}, u32[]{:S(2)}) %collective-permute-start.2) | collective-permute-done | bytes 262176 | tf_op jit(solution)/shard_map/while/body/eval_jaxpr/ppermute | solution.py:12
  1100.7 18.7 %collective-permute-done.2 = bf16[4,128,2,128]{3,1,2,0:T(8,128)(2,1)S(1)} collective-permute-done((bf16[4,128,2,128]{3,1,2,0:T(8,128)(2,1)}, bf16[4,128,2,128]{3,1,2,0:T(8,128)(2,1)S(1)}, u32[]{:S(2)}, u32[]{:S(2)}) %collective-permute-start.2) | collective-permute-done | bytes 262176 | tf_op jit(solution)/shard_map/while/body/eval_jaxpr/ppermute | solution.py:12
  1126.3 21.4 %collective-permute-done.2 = bf16[4,128,2,128]{3,1,2,0:T(8,128)(2,1)S(1)} collective-permute-done((bf16[4,128,2,128]{3,1,2,0:T(8,128)(2,1)}, bf16[4,128,2,128]{3,1,2,0:T(8,128)(2,1)S(1)}, u32[]{:S(2)}, u32[]{:S(2)}) %collective-permute-start.2) | collective-permute-done | bytes 262176 | tf_op jit(solution)/shard_map/while/body/eval_jaxpr/ppermute | solution.py:12
  1154.7 20.4 %collective-permute-done.2 = bf16[4,128,2,128]{3,1,2,0:T(8,128)(2,1)S(1)} collective-permute-done((bf16[4,128,2,128]{3,1,2,0:T(8,128)(2,1)}, bf16[4,128,2,128]{3,1,2,0:T(8,128)(2,1)S(1)}, u32[]{:S(2)}, u32[]{:S(2)}) %collective-permute-start.2) | collective-permute-done | bytes 262176 | tf_op jit(solution)/shard_map/while/body/eval_jaxpr/ppermute | solution.py:12
  1182.1 18.0 %collective-permute-done.2 = bf16[4,128,2,128]{3,1,2,0:T(8,128)(2,1)S(1)} collective-permute-done((bf16[4,128,2,128]{3,1,2,0:T(8,128)(2,1)}, bf16[4,128,2,128]{3,1,2,0:T(8,128)(2,1)S(1)}, u32[]{:S(2)}, u32[]{:S(2)}) %collective-permute-start.2) | collective-permute-done | bytes 262176 | tf_op jit(solution)/shard_map/while/body/eval_jaxpr/ppermute | solution.py:12
  1210.6 19.1 %collective-permute-done.2 = bf16[4,128,2,128]{3,1,2,0:T(8,128)(2,1)S(1)} collective-permute-done((bf16[4,128,2,128]{3,1,2,0:T(8,128)(2,1)}, bf16[4,128,2,128]{3,1,2,0:T(8,128)(2,1)S(1)}, u32[]{:S(2)}, u32[]{:S(2)}) %collective-permute-start.2) | collective-permute-done | bytes 262176 | tf_op jit(solution)/shard_map/while/body/eval_jaxpr/ppermute | solution.py:12
  1240.1 20.2 %collective-permute-done.2 = bf16[4,128,2,128]{3,1,2,0:T(8,128)(2,1)S(1)} collective-permute-done((bf16[4,128,2,128]{3,1,2,0:T(8,128)(2,1)}, bf16[4,128,2,128]{3,1,2,0:T(8,128)(2,1)S(1)}, u32[]{:S(2)}, u32[]{:S(2)}) %collective-permute-start.2) | collective-permute-done | bytes 262176 | tf_op jit(solution)/shard_map/while/body/eval_jaxpr/ppermute | solution.py:12
  1270.8 21.3 %collective-permute-done.2 = bf16[4,128,2,128]{3,1,2,0:T(8,128)(2,1)S(1)} collective-permute-done((bf16[4,128,2,128]{3,1,2,0:T(8,128)(2,1)}, bf16[4,128,2,128]{3,1,2,0:T(8,128)(2,1)S(1)}, u32[]{:S(2)}, u32[]{:S(2)}) %collective-permute-start.2) | collective-permute-done | bytes 262176 | tf_op jit(solution)/shard_map/while/body/eval_jaxpr/ppermute | solution.py:12
  1302.6 22.0 %collective-permute-done.2 = bf16[4,128,2,128]{3,1,2,0:T(8,128)(2,1)S(1)} collective-permute-done((bf16[4,128,2,128]{3,1,2,0:T(8,128)(2,1)}, bf16[4,128,2,128]{3,1,2,0:T(8,128)(2,1)S(1)}, u32[]{:S(2)}, u32[]{:S(2)}) %collective-permute-start.2) | collective-permute-done | bytes 262176 | tf_op jit(solution)/shard_map/while/body/eval_jaxpr/ppermute | solution.py:12
  1335.0 13.8 collective-permute-done.2
  1359.3 13.9 collective-permute-done.2
  1383.6 13.9 collective-permute-done.2
  1411.6 18.5 %collective-permute-done.3 = f32[4,128,2,128]{3,2,1,0:T(2,128)S(1)} collective-permute-done((f32[4,128,2,128]{3,2,1,0:T(2,128)S(1)}, f32[4,128,2,128]{3,2,1,0:T(2,128)S(1)}, u32[]{:S(2)}, u32[]{:S(2)}) %collective-permute-start.3) | collective-permute-done | bytes 524320 | tf_op jit(solution)/shard_map/ppermute | solution.py:12
  (1216 shorter events, 685.5 us)
Async XLA Ops:
  3.0 17.5 %all-to-all-start = ((bf16[32,96,128]{2,0,1:T(8,128)(2,1)}), bf16[32,96,128]{2,0,1:T(8,128)(2,1)S(1)}, u32[]{:S(2)}, u32[]{:S(2)}) async-start(bf16[32,96,128]{2,0,1:T(8,128)(2,1)} %copy.77), calls=%async_computation | async-start | bytes 1572864 | tf_op jit(solution)/shard_map/all_to_all | solution.py:27
  20.6 16.6 %all-to-all-start.1 = ((bf16[32,96,128]{2,0,1:T(8,128)(2,1)}), bf16[32,96,128]{2,0,1:T(8,128)(2,1)S(1)}, u32[]{:S(2)}, u32[]{:S(2)}) async-start(bf16[32,96,128]{2,0,1:T(8,128)(2,1)} %copy.79), calls=%async_computation.1 | async-start | bytes 1572864 | tf_op jit(solution)/shard_map/all_to_all | solution.py:28
  506.9 20.7 %collective-permute-start.1 = (f32[4,128,2,128]{3,1,2,0:T(8,128)}, f32[4,128,2,128]{3,1,2,0:T(8,128)}, u32[]{:S(2)}, u32[]{:S(2)}) collective-permute-start(f32[4,128,2,128]{3,1,2,0:T(8,128)} %get-tuple-element.1780), channel_id=1, source_target_pairs={{124,0},{0,4},{4,8},{8,12},{12,16},{16,20},{20,24},{24,28},{28,32}... | collective-permute-start | bytes 1572872 | tf_op jit(solution)/shard_map/while/body/eval_jaxpr/ppermute | solution.py:12
  506.9 19.9 %collective-permute-start.2 = (bf16[4,128,2,128]{3,1,2,0:T(8,128)(2,1)}, bf16[4,128,2,128]{3,1,2,0:T(8,128)(2,1)S(1)}, u32[]{:S(2)}, u32[]{:S(2)}) collective-permute-start(bf16[4,128,2,128]{3,1,2,0:T(8,128)(2,1)} %get-tuple-element.1781), channel_id=1, source_target_pairs={{124,0},{0,4},{4,8},{8,12},{12,16},{16,20},{20,24},{24,28},{28,32}... | collective-permute-start | bytes 786440 | tf_op jit(solution)/shard_map/while/body/eval_jaxpr/ppermute | solution.py:12
  535.9 21.8 %collective-permute-start.1 = (f32[4,128,2,128]{3,1,2,0:T(8,128)}, f32[4,128,2,128]{3,1,2,0:T(8,128)}, u32[]{:S(2)}, u32[]{:S(2)}) collective-permute-start(f32[4,128,2,128]{3,1,2,0:T(8,128)} %get-tuple-element.1780), channel_id=1, source_target_pairs={{124,0},{0,4},{4,8},{8,12},{12,16},{16,20},{20,24},{24,28},{28,32}... | collective-permute-start | bytes 1572872 | tf_op jit(solution)/shard_map/while/body/eval_jaxpr/ppermute | solution.py:12
  535.9 20.9 %collective-permute-start.2 = (bf16[4,128,2,128]{3,1,2,0:T(8,128)(2,1)}, bf16[4,128,2,128]{3,1,2,0:T(8,128)(2,1)S(1)}, u32[]{:S(2)}, u32[]{:S(2)}) collective-permute-start(bf16[4,128,2,128]{3,1,2,0:T(8,128)(2,1)} %get-tuple-element.1781), channel_id=1, source_target_pairs={{124,0},{0,4},{4,8},{8,12},{12,16},{16,20},{20,24},{24,28},{28,32}... | collective-permute-start | bytes 786440 | tf_op jit(solution)/shard_map/while/body/eval_jaxpr/ppermute | solution.py:12
  566.0 22.8 %collective-permute-start.1 = (f32[4,128,2,128]{3,1,2,0:T(8,128)}, f32[4,128,2,128]{3,1,2,0:T(8,128)}, u32[]{:S(2)}, u32[]{:S(2)}) collective-permute-start(f32[4,128,2,128]{3,1,2,0:T(8,128)} %get-tuple-element.1780), channel_id=1, source_target_pairs={{124,0},{0,4},{4,8},{8,12},{12,16},{16,20},{20,24},{24,28},{28,32}... | collective-permute-start | bytes 1572872 | tf_op jit(solution)/shard_map/while/body/eval_jaxpr/ppermute | solution.py:12
  566.0 22.0 %collective-permute-start.2 = (bf16[4,128,2,128]{3,1,2,0:T(8,128)(2,1)}, bf16[4,128,2,128]{3,1,2,0:T(8,128)(2,1)S(1)}, u32[]{:S(2)}, u32[]{:S(2)}) collective-permute-start(bf16[4,128,2,128]{3,1,2,0:T(8,128)(2,1)} %get-tuple-element.1781), channel_id=1, source_target_pairs={{124,0},{0,4},{4,8},{8,12},{12,16},{16,20},{20,24},{24,28},{28,32}... | collective-permute-start | bytes 786440 | tf_op jit(solution)/shard_map/while/body/eval_jaxpr/ppermute | solution.py:12
  597.1 23.9 %collective-permute-start.1 = (f32[4,128,2,128]{3,1,2,0:T(8,128)}, f32[4,128,2,128]{3,1,2,0:T(8,128)}, u32[]{:S(2)}, u32[]{:S(2)}) collective-permute-start(f32[4,128,2,128]{3,1,2,0:T(8,128)} %get-tuple-element.1780), channel_id=1, source_target_pairs={{124,0},{0,4},{4,8},{8,12},{12,16},{16,20},{20,24},{24,28},{28,32}... | collective-permute-start | bytes 1572872 | tf_op jit(solution)/shard_map/while/body/eval_jaxpr/ppermute | solution.py:12
  597.1 23.1 %collective-permute-start.2 = (bf16[4,128,2,128]{3,1,2,0:T(8,128)(2,1)}, bf16[4,128,2,128]{3,1,2,0:T(8,128)(2,1)S(1)}, u32[]{:S(2)}, u32[]{:S(2)}) collective-permute-start(bf16[4,128,2,128]{3,1,2,0:T(8,128)(2,1)} %get-tuple-element.1781), channel_id=1, source_target_pairs={{124,0},{0,4},{4,8},{8,12},{12,16},{16,20},{20,24},{24,28},{28,32}... | collective-permute-start | bytes 786440 | tf_op jit(solution)/shard_map/while/body/eval_jaxpr/ppermute | solution.py:12
  629.4 25.1 %collective-permute-start.1 = (f32[4,128,2,128]{3,1,2,0:T(8,128)}, f32[4,128,2,128]{3,1,2,0:T(8,128)}, u32[]{:S(2)}, u32[]{:S(2)}) collective-permute-start(f32[4,128,2,128]{3,1,2,0:T(8,128)} %get-tuple-element.1780), channel_id=1, source_target_pairs={{124,0},{0,4},{4,8},{8,12},{12,16},{16,20},{20,24},{24,28},{28,32}... | collective-permute-start | bytes 1572872 | tf_op jit(solution)/shard_map/while/body/eval_jaxpr/ppermute | solution.py:12
  629.4 24.3 %collective-permute-start.2 = (bf16[4,128,2,128]{3,1,2,0:T(8,128)(2,1)}, bf16[4,128,2,128]{3,1,2,0:T(8,128)(2,1)S(1)}, u32[]{:S(2)}, u32[]{:S(2)}) collective-permute-start(bf16[4,128,2,128]{3,1,2,0:T(8,128)(2,1)} %get-tuple-element.1781), channel_id=1, source_target_pairs={{124,0},{0,4},{4,8},{8,12},{12,16},{16,20},{20,24},{24,28},{28,32}... | collective-permute-start | bytes 786440 | tf_op jit(solution)/shard_map/while/body/eval_jaxpr/ppermute | solution.py:12
  662.8 25.1 %collective-permute-start.1 = (f32[4,128,2,128]{3,1,2,0:T(8,128)}, f32[4,128,2,128]{3,1,2,0:T(8,128)}, u32[]{:S(2)}, u32[]{:S(2)}) collective-permute-start(f32[4,128,2,128]{3,1,2,0:T(8,128)} %get-tuple-element.1780), channel_id=1, source_target_pairs={{124,0},{0,4},{4,8},{8,12},{12,16},{16,20},{20,24},{24,28},{28,32}... | collective-permute-start | bytes 1572872 | tf_op jit(solution)/shard_map/while/body/eval_jaxpr/ppermute | solution.py:12
  662.8 24.2 %collective-permute-start.2 = (bf16[4,128,2,128]{3,1,2,0:T(8,128)(2,1)}, bf16[4,128,2,128]{3,1,2,0:T(8,128)(2,1)S(1)}, u32[]{:S(2)}, u32[]{:S(2)}) collective-permute-start(bf16[4,128,2,128]{3,1,2,0:T(8,128)(2,1)} %get-tuple-element.1781), channel_id=1, source_target_pairs={{124,0},{0,4},{4,8},{8,12},{12,16},{16,20},{20,24},{24,28},{28,32}... | collective-permute-start | bytes 786440 | tf_op jit(solution)/shard_map/while/body/eval_jaxpr/ppermute | solution.py:12
  696.2 24.2 %collective-permute-start.1 = (f32[4,128,2,128]{3,1,2,0:T(8,128)}, f32[4,128,2,128]{3,1,2,0:T(8,128)}, u32[]{:S(2)}, u32[]{:S(2)}) collective-permute-start(f32[4,128,2,128]{3,1,2,0:T(8,128)} %get-tuple-element.1780), channel_id=1, source_target_pairs={{124,0},{0,4},{4,8},{8,12},{12,16},{16,20},{20,24},{24,28},{28,32}... | collective-permute-start | bytes 1572872 | tf_op jit(solution)/shard_map/while/body/eval_jaxpr/ppermute | solution.py:12
  696.2 23.4 %collective-permute-start.2 = (bf16[4,128,2,128]{3,1,2,0:T(8,128)(2,1)}, bf16[4,128,2,128]{3,1,2,0:T(8,128)(2,1)S(1)}, u32[]{:S(2)}, u32[]{:S(2)}) collective-permute-start(bf16[4,128,2,128]{3,1,2,0:T(8,128)(2,1)} %get-tuple-element.1781), channel_id=1, source_target_pairs={{124,0},{0,4},{4,8},{8,12},{12,16},{16,20},{20,24},{24,28},{28,32}... | collective-permute-start | bytes 786440 | tf_op jit(solution)/shard_map/while/body/eval_jaxpr/ppermute | solution.py:12
  728.8 23.3 %collective-permute-start.1 = (f32[4,128,2,128]{3,1,2,0:T(8,128)}, f32[4,128,2,128]{3,1,2,0:T(8,128)}, u32[]{:S(2)}, u32[]{:S(2)}) collective-permute-start(f32[4,128,2,128]{3,1,2,0:T(8,128)} %get-tuple-element.1780), channel_id=1, source_target_pairs={{124,0},{0,4},{4,8},{8,12},{12,16},{16,20},{20,24},{24,28},{28,32}... | collective-permute-start | bytes 1572872 | tf_op jit(solution)/shard_map/while/body/eval_jaxpr/ppermute | solution.py:12
  728.8 22.5 %collective-permute-start.2 = (bf16[4,128,2,128]{3,1,2,0:T(8,128)(2,1)}, bf16[4,128,2,128]{3,1,2,0:T(8,128)(2,1)S(1)}, u32[]{:S(2)}, u32[]{:S(2)}) collective-permute-start(bf16[4,128,2,128]{3,1,2,0:T(8,128)(2,1)} %get-tuple-element.1781), channel_id=1, source_target_pairs={{124,0},{0,4},{4,8},{8,12},{12,16},{16,20},{20,24},{24,28},{28,32}... | collective-permute-start | bytes 786440 | tf_op jit(solution)/shard_map/while/body/eval_jaxpr/ppermute | solution.py:12
  760.4 22.4 %collective-permute-start.1 = (f32[4,128,2,128]{3,1,2,0:T(8,128)}, f32[4,128,2,128]{3,1,2,0:T(8,128)}, u32[]{:S(2)}, u32[]{:S(2)}) collective-permute-start(f32[4,128,2,128]{3,1,2,0:T(8,128)} %get-tuple-element.1780), channel_id=1, source_target_pairs={{124,0},{0,4},{4,8},{8,12},{12,16},{16,20},{20,24},{24,28},{28,32}... | collective-permute-start | bytes 1572872 | tf_op jit(solution)/shard_map/while/body/eval_jaxpr/ppermute | solution.py:12
  760.4 21.6 %collective-permute-start.2 = (bf16[4,128,2,128]{3,1,2,0:T(8,128)(2,1)}, bf16[4,128,2,128]{3,1,2,0:T(8,128)(2,1)S(1)}, u32[]{:S(2)}, u32[]{:S(2)}) collective-permute-start(bf16[4,128,2,128]{3,1,2,0:T(8,128)(2,1)} %get-tuple-element.1781), channel_id=1, source_target_pairs={{124,0},{0,4},{4,8},{8,12},{12,16},{16,20},{20,24},{24,28},{28,32}... | collective-permute-start | bytes 786440 | tf_op jit(solution)/shard_map/while/body/eval_jaxpr/ppermute | solution.py:12
  791.1 21.6 %collective-permute-start.1 = (f32[4,128,2,128]{3,1,2,0:T(8,128)}, f32[4,128,2,128]{3,1,2,0:T(8,128)}, u32[]{:S(2)}, u32[]{:S(2)}) collective-permute-start(f32[4,128,2,128]{3,1,2,0:T(8,128)} %get-tuple-element.1780), channel_id=1, source_target_pairs={{124,0},{0,4},{4,8},{8,12},{12,16},{16,20},{20,24},{24,28},{28,32}... | collective-permute-start | bytes 1572872 | tf_op jit(solution)/shard_map/while/body/eval_jaxpr/ppermute | solution.py:12
  791.1 20.8 %collective-permute-start.2 = (bf16[4,128,2,128]{3,1,2,0:T(8,128)(2,1)}, bf16[4,128,2,128]{3,1,2,0:T(8,128)(2,1)S(1)}, u32[]{:S(2)}, u32[]{:S(2)}) collective-permute-start(bf16[4,128,2,128]{3,1,2,0:T(8,128)(2,1)} %get-tuple-element.1781), channel_id=1, source_target_pairs={{124,0},{0,4},{4,8},{8,12},{12,16},{16,20},{20,24},{24,28},{28,32}... | collective-permute-start | bytes 786440 | tf_op jit(solution)/shard_map/while/body/eval_jaxpr/ppermute | solution.py:12
  821.0 20.8 %collective-permute-start.1 = (f32[4,128,2,128]{3,1,2,0:T(8,128)}, f32[4,128,2,128]{3,1,2,0:T(8,128)}, u32[]{:S(2)}, u32[]{:S(2)}) collective-permute-start(f32[4,128,2,128]{3,1,2,0:T(8,128)} %get-tuple-element.1780), channel_id=1, source_target_pairs={{124,0},{0,4},{4,8},{8,12},{12,16},{16,20},{20,24},{24,28},{28,32}... | collective-permute-start | bytes 1572872 | tf_op jit(solution)/shard_map/while/body/eval_jaxpr/ppermute | solution.py:12
  821.0 19.9 %collective-permute-start.2 = (bf16[4,128,2,128]{3,1,2,0:T(8,128)(2,1)}, bf16[4,128,2,128]{3,1,2,0:T(8,128)(2,1)S(1)}, u32[]{:S(2)}, u32[]{:S(2)}) collective-permute-start(bf16[4,128,2,128]{3,1,2,0:T(8,128)(2,1)} %get-tuple-element.1781), channel_id=1, source_target_pairs={{124,0},{0,4},{4,8},{8,12},{12,16},{16,20},{20,24},{24,28},{28,32}... | collective-permute-start | bytes 786440 | tf_op jit(solution)/shard_map/while/body/eval_jaxpr/ppermute | solution.py:12
  850.1 20.0 %collective-permute-start.1 = (f32[4,128,2,128]{3,1,2,0:T(8,128)}, f32[4,128,2,128]{3,1,2,0:T(8,128)}, u32[]{:S(2)}, u32[]{:S(2)}) collective-permute-start(f32[4,128,2,128]{3,1,2,0:T(8,128)} %get-tuple-element.1780), channel_id=1, source_target_pairs={{124,0},{0,4},{4,8},{8,12},{12,16},{16,20},{20,24},{24,28},{28,32}... | collective-permute-start | bytes 1572872 | tf_op jit(solution)/shard_map/while/body/eval_jaxpr/ppermute | solution.py:12
  850.1 19.1 %collective-permute-start.2 = (bf16[4,128,2,128]{3,1,2,0:T(8,128)(2,1)}, bf16[4,128,2,128]{3,1,2,0:T(8,128)(2,1)S(1)}, u32[]{:S(2)}, u32[]{:S(2)}) collective-permute-start(bf16[4,128,2,128]{3,1,2,0:T(8,128)(2,1)} %get-tuple-element.1781), channel_id=1, source_target_pairs={{124,0},{0,4},{4,8},{8,12},{12,16},{16,20},{20,24},{24,28},{28,32}... | collective-permute-start | bytes 786440 | tf_op jit(solution)/shard_map/while/body/eval_jaxpr/ppermute | solution.py:12
  878.4 19.1 %collective-permute-start.1 = (f32[4,128,2,128]{3,1,2,0:T(8,128)}, f32[4,128,2,128]{3,1,2,0:T(8,128)}, u32[]{:S(2)}, u32[]{:S(2)}) collective-permute-start(f32[4,128,2,128]{3,1,2,0:T(8,128)} %get-tuple-element.1780), channel_id=1, source_target_pairs={{124,0},{0,4},{4,8},{8,12},{12,16},{16,20},{20,24},{24,28},{28,32}... | collective-permute-start | bytes 1572872 | tf_op jit(solution)/shard_map/while/body/eval_jaxpr/ppermute | solution.py:12
  878.4 18.3 %collective-permute-start.2 = (bf16[4,128,2,128]{3,1,2,0:T(8,128)(2,1)}, bf16[4,128,2,128]{3,1,2,0:T(8,128)(2,1)S(1)}, u32[]{:S(2)}, u32[]{:S(2)}) collective-permute-start(bf16[4,128,2,128]{3,1,2,0:T(8,128)(2,1)} %get-tuple-element.1781), channel_id=1, source_target_pairs={{124,0},{0,4},{4,8},{8,12},{12,16},{16,20},{20,24},{24,28},{28,32}... | collective-permute-start | bytes 786440 | tf_op jit(solution)/shard_map/while/body/eval_jaxpr/ppermute | solution.py:12
  905.9 18.3 %collective-permute-start.1 = (f32[4,128,2,128]{3,1,2,0:T(8,128)}, f32[4,128,2,128]{3,1,2,0:T(8,128)}, u32[]{:S(2)}, u32[]{:S(2)}) collective-permute-start(f32[4,128,2,128]{3,1,2,0:T(8,128)} %get-tuple-element.1780), channel_id=1, source_target_pairs={{124,0},{0,4},{4,8},{8,12},{12,16},{16,20},{20,24},{24,28},{28,32}... | collective-permute-start | bytes 1572872 | tf_op jit(solution)/shard_map/while/body/eval_jaxpr/ppermute | solution.py:12
  905.9 17.5 %collective-permute-start.2 = (bf16[4,128,2,128]{3,1,2,0:T(8,128)(2,1)}, bf16[4,128,2,128]{3,1,2,0:T(8,128)(2,1)S(1)}, u32[]{:S(2)}, u32[]{:S(2)}) collective-permute-start(bf16[4,128,2,128]{3,1,2,0:T(8,128)(2,1)} %get-tuple-element.1781), channel_id=1, source_target_pairs={{124,0},{0,4},{4,8},{8,12},{12,16},{16,20},{20,24},{24,28},{28,32}... | collective-permute-start | bytes 786440 | tf_op jit(solution)/shard_map/while/body/eval_jaxpr/ppermute | solution.py:12
  932.5 17.5 %collective-permute-start.1 = (f32[4,128,2,128]{3,1,2,0:T(8,128)}, f32[4,128,2,128]{3,1,2,0:T(8,128)}, u32[]{:S(2)}, u32[]{:S(2)}) collective-permute-start(f32[4,128,2,128]{3,1,2,0:T(8,128)} %get-tuple-element.1780), channel_id=1, source_target_pairs={{124,0},{0,4},{4,8},{8,12},{12,16},{16,20},{20,24},{24,28},{28,32}... | collective-permute-start | bytes 1572872 | tf_op jit(solution)/shard_map/while/body/eval_jaxpr/ppermute | solution.py:12
  932.5 16.7 %collective-permute-start.2 = (bf16[4,128,2,128]{3,1,2,0:T(8,128)(2,1)}, bf16[4,128,2,128]{3,1,2,0:T(8,128)(2,1)S(1)}, u32[]{:S(2)}, u32[]{:S(2)}) collective-permute-start(bf16[4,128,2,128]{3,1,2,0:T(8,128)(2,1)} %get-tuple-element.1781), channel_id=1, source_target_pairs={{124,0},{0,4},{4,8},{8,12},{12,16},{16,20},{20,24},{24,28},{28,32}... | collective-permute-start | bytes 786440 | tf_op jit(solution)/shard_map/while/body/eval_jaxpr/ppermute | solution.py:12
  958.3 19.7 %collective-permute-start.1 = (f32[4,128,2,128]{3,1,2,0:T(8,128)}, f32[4,128,2,128]{3,1,2,0:T(8,128)}, u32[]{:S(2)}, u32[]{:S(2)}) collective-permute-start(f32[4,128,2,128]{3,1,2,0:T(8,128)} %get-tuple-element.1780), channel_id=1, source_target_pairs={{124,0},{0,4},{4,8},{8,12},{12,16},{16,20},{20,24},{24,28},{28,32}... | collective-permute-start | bytes 1572872 | tf_op jit(solution)/shard_map/while/body/eval_jaxpr/ppermute | solution.py:12
  958.3 18.9 %collective-permute-start.2 = (bf16[4,128,2,128]{3,1,2,0:T(8,128)(2,1)}, bf16[4,128,2,128]{3,1,2,0:T(8,128)(2,1)S(1)}, u32[]{:S(2)}, u32[]{:S(2)}) collective-permute-start(bf16[4,128,2,128]{3,1,2,0:T(8,128)(2,1)} %get-tuple-element.1781), channel_id=1, source_target_pairs={{124,0},{0,4},{4,8},{8,12},{12,16},{16,20},{20,24},{24,28},{28,32}... | collective-permute-start | bytes 786440 | tf_op jit(solution)/shard_map/while/body/eval_jaxpr/ppermute | solution.py:12
  986.3 25.7 %collective-permute-start.1 = (f32[4,128,2,128]{3,1,2,0:T(8,128)}, f32[4,128,2,128]{3,1,2,0:T(8,128)}, u32[]{:S(2)}, u32[]{:S(2)}) collective-permute-start(f32[4,128,2,128]{3,1,2,0:T(8,128)} %get-tuple-element.1780), channel_id=1, source_target_pairs={{124,0},{0,4},{4,8},{8,12},{12,16},{16,20},{20,24},{24,28},{28,32}... | collective-permute-start | bytes 1572872 | tf_op jit(solution)/shard_map/while/body/eval_jaxpr/ppermute | solution.py:12
  986.4 24.8 %collective-permute-start.2 = (bf16[4,128,2,128]{3,1,2,0:T(8,128)(2,1)}, bf16[4,128,2,128]{3,1,2,0:T(8,128)(2,1)S(1)}, u32[]{:S(2)}, u32[]{:S(2)}) collective-permute-start(bf16[4,128,2,128]{3,1,2,0:T(8,128)(2,1)} %get-tuple-element.1781), channel_id=1, source_target_pairs={{124,0},{0,4},{4,8},{8,12},{12,16},{16,20},{20,24},{24,28},{28,32}... | collective-permute-start | bytes 786440 | tf_op jit(solution)/shard_map/while/body/eval_jaxpr/ppermute | solution.py:12
  1015.5 24.8 %collective-permute-start.1 = (f32[4,128,2,128]{3,1,2,0:T(8,128)}, f32[4,128,2,128]{3,1,2,0:T(8,128)}, u32[]{:S(2)}, u32[]{:S(2)}) collective-permute-start(f32[4,128,2,128]{3,1,2,0:T(8,128)} %get-tuple-element.1780), channel_id=1, source_target_pairs={{124,0},{0,4},{4,8},{8,12},{12,16},{16,20},{20,24},{24,28},{28,32}... | collective-permute-start | bytes 1572872 | tf_op jit(solution)/shard_map/while/body/eval_jaxpr/ppermute | solution.py:12
  1015.8 23.7 %collective-permute-start.2 = (bf16[4,128,2,128]{3,1,2,0:T(8,128)(2,1)}, bf16[4,128,2,128]{3,1,2,0:T(8,128)(2,1)S(1)}, u32[]{:S(2)}, u32[]{:S(2)}) collective-permute-start(bf16[4,128,2,128]{3,1,2,0:T(8,128)(2,1)} %get-tuple-element.1781), channel_id=1, source_target_pairs={{124,0},{0,4},{4,8},{8,12},{12,16},{16,20},{20,24},{24,28},{28,32}... | collective-permute-start | bytes 786440 | tf_op jit(solution)/shard_map/while/body/eval_jaxpr/ppermute | solution.py:12
  1043.9 24.0 %collective-permute-start.1 = (f32[4,128,2,128]{3,1,2,0:T(8,128)}, f32[4,128,2,128]{3,1,2,0:T(8,128)}, u32[]{:S(2)}, u32[]{:S(2)}) collective-permute-start(f32[4,128,2,128]{3,1,2,0:T(8,128)} %get-tuple-element.1780), channel_id=1, source_target_pairs={{124,0},{0,4},{4,8},{8,12},{12,16},{16,20},{20,24},{24,28},{28,32}... | collective-permute-start | bytes 1572872 | tf_op jit(solution)/shard_map/while/body/eval_jaxpr/ppermute | solution.py:12
  1043.9 23.2 %collective-permute-start.2 = (bf16[4,128,2,128]{3,1,2,0:T(8,128)(2,1)}, bf16[4,128,2,128]{3,1,2,0:T(8,128)(2,1)S(1)}, u32[]{:S(2)}, u32[]{:S(2)}) collective-permute-start(bf16[4,128,2,128]{3,1,2,0:T(8,128)(2,1)} %get-tuple-element.1781), channel_id=1, source_target_pairs={{124,0},{0,4},{4,8},{8,12},{12,16},{16,20},{20,24},{24,28},{28,32}... | collective-permute-start | bytes 786440 | tf_op jit(solution)/shard_map/while/body/eval_jaxpr/ppermute | solution.py:12
  1071.4 23.1 %collective-permute-start.1 = (f32[4,128,2,128]{3,1,2,0:T(8,128)}, f32[4,128,2,128]{3,1,2,0:T(8,128)}, u32[]{:S(2)}, u32[]{:S(2)}) collective-permute-start(f32[4,128,2,128]{3,1,2,0:T(8,128)} %get-tuple-element.1780), channel_id=1, source_target_pairs={{124,0},{0,4},{4,8},{8,12},{12,16},{16,20},{20,24},{24,28},{28,32}... | collective-permute-start | bytes 1572872 | tf_op jit(solution)/shard_map/while/body/eval_jaxpr/ppermute | solution.py:12
  1071.4 22.2 %collective-permute-start.2 = (bf16[4,128,2,128]{3,1,2,0:T(8,128)(2,1)}, bf16[4,128,2,128]{3,1,2,0:T(8,128)(2,1)S(1)}, u32[]{:S(2)}, u32[]{:S(2)}) collective-permute-start(bf16[4,128,2,128]{3,1,2,0:T(8,128)(2,1)} %get-tuple-element.1781), channel_id=1, source_target_pairs={{124,0},{0,4},{4,8},{8,12},{12,16},{16,20},{20,24},{24,28},{28,32}... | collective-permute-start | bytes 786440 | tf_op jit(solution)/shard_map/while/body/eval_jaxpr/ppermute | solution.py:12
  1098.0 22.1 %collective-permute-start.1 = (f32[4,128,2,128]{3,1,2,0:T(8,128)}, f32[4,128,2,128]{3,1,2,0:T(8,128)}, u32[]{:S(2)}, u32[]{:S(2)}) collective-permute-start(f32[4,128,2,128]{3,1,2,0:T(8,128)} %get-tuple-element.1780), channel_id=1, source_target_pairs={{124,0},{0,4},{4,8},{8,12},{12,16},{16,20},{20,24},{24,28},{28,32}... | collective-permute-start | bytes 1572872 | tf_op jit(solution)/shard_map/while/body/eval_jaxpr/ppermute | solution.py:12
  1098.0 21.3 %collective-permute-start.2 = (bf16[4,128,2,128]{3,1,2,0:T(8,128)(2,1)}, bf16[4,128,2,128]{3,1,2,0:T(8,128)(2,1)S(1)}, u32[]{:S(2)}, u32[]{:S(2)}) collective-permute-start(bf16[4,128,2,128]{3,1,2,0:T(8,128)(2,1)} %get-tuple-element.1781), channel_id=1, source_target_pairs={{124,0},{0,4},{4,8},{8,12},{12,16},{16,20},{20,24},{24,28},{28,32}... | collective-permute-start | bytes 786440 | tf_op jit(solution)/shard_map/while/body/eval_jaxpr/ppermute | solution.py:12
  1123.7 24.8 %collective-permute-start.1 = (f32[4,128,2,128]{3,1,2,0:T(8,128)}, f32[4,128,2,128]{3,1,2,0:T(8,128)}, u32[]{:S(2)}, u32[]{:S(2)}) collective-permute-start(f32[4,128,2,128]{3,1,2,0:T(8,128)} %get-tuple-element.1780), channel_id=1, source_target_pairs={{124,0},{0,4},{4,8},{8,12},{12,16},{16,20},{20,24},{24,28},{28,32}... | collective-permute-start | bytes 1572872 | tf_op jit(solution)/shard_map/while/body/eval_jaxpr/ppermute | solution.py:12
  1123.7 24.0 %collective-permute-start.2 = (bf16[4,128,2,128]{3,1,2,0:T(8,128)(2,1)}, bf16[4,128,2,128]{3,1,2,0:T(8,128)(2,1)S(1)}, u32[]{:S(2)}, u32[]{:S(2)}) collective-permute-start(bf16[4,128,2,128]{3,1,2,0:T(8,128)(2,1)} %get-tuple-element.1781), channel_id=1, source_target_pairs={{124,0},{0,4},{4,8},{8,12},{12,16},{16,20},{20,24},{24,28},{28,32}... | collective-permute-start | bytes 786440 | tf_op jit(solution)/shard_map/while/body/eval_jaxpr/ppermute | solution.py:12
  1152.1 23.9 %collective-permute-start.1 = (f32[4,128,2,128]{3,1,2,0:T(8,128)}, f32[4,128,2,128]{3,1,2,0:T(8,128)}, u32[]{:S(2)}, u32[]{:S(2)}) collective-permute-start(f32[4,128,2,128]{3,1,2,0:T(8,128)} %get-tuple-element.1780), channel_id=1, source_target_pairs={{124,0},{0,4},{4,8},{8,12},{12,16},{16,20},{20,24},{24,28},{28,32}... | collective-permute-start | bytes 1572872 | tf_op jit(solution)/shard_map/while/body/eval_jaxpr/ppermute | solution.py:12
  1152.1 23.0 %collective-permute-start.2 = (bf16[4,128,2,128]{3,1,2,0:T(8,128)(2,1)}, bf16[4,128,2,128]{3,1,2,0:T(8,128)(2,1)S(1)}, u32[]{:S(2)}, u32[]{:S(2)}) collective-permute-start(bf16[4,128,2,128]{3,1,2,0:T(8,128)(2,1)} %get-tuple-element.1781), channel_id=1, source_target_pairs={{124,0},{0,4},{4,8},{8,12},{12,16},{16,20},{20,24},{24,28},{28,32}... | collective-permute-start | bytes 786440 | tf_op jit(solution)/shard_map/while/body/eval_jaxpr/ppermute | solution.py:12
  1179.5 21.5 %collective-permute-start.1 = (f32[4,128,2,128]{3,1,2,0:T(8,128)}, f32[4,128,2,128]{3,1,2,0:T(8,128)}, u32[]{:S(2)}, u32[]{:S(2)}) collective-permute-start(f32[4,128,2,128]{3,1,2,0:T(8,128)} %get-tuple-element.1780), channel_id=1, source_target_pairs={{124,0},{0,4},{4,8},{8,12},{12,16},{16,20},{20,24},{24,28},{28,32}... | collective-permute-start | bytes 1572872 | tf_op jit(solution)/shard_map/while/body/eval_jaxpr/ppermute | solution.py:12
  1179.5 20.6 %collective-permute-start.2 = (bf16[4,128,2,128]{3,1,2,0:T(8,128)(2,1)}, bf16[4,128,2,128]{3,1,2,0:T(8,128)(2,1)S(1)}, u32[]{:S(2)}, u32[]{:S(2)}) collective-permute-start(bf16[4,128,2,128]{3,1,2,0:T(8,128)(2,1)} %get-tuple-element.1781), channel_id=1, source_target_pairs={{124,0},{0,4},{4,8},{8,12},{12,16},{16,20},{20,24},{24,28},{28,32}... | collective-permute-start | bytes 786440 | tf_op jit(solution)/shard_map/while/body/eval_jaxpr/ppermute | solution.py:12
  1208.0 22.6 %collective-permute-start.1 = (f32[4,128,2,128]{3,1,2,0:T(8,128)}, f32[4,128,2,128]{3,1,2,0:T(8,128)}, u32[]{:S(2)}, u32[]{:S(2)}) collective-permute-start(f32[4,128,2,128]{3,1,2,0:T(8,128)} %get-tuple-element.1780), channel_id=1, source_target_pairs={{124,0},{0,4},{4,8},{8,12},{12,16},{16,20},{20,24},{24,28},{28,32}... | collective-permute-start | bytes 1572872 | tf_op jit(solution)/shard_map/while/body/eval_jaxpr/ppermute | solution.py:12
  1208.0 21.7 %collective-permute-start.2 = (bf16[4,128,2,128]{3,1,2,0:T(8,128)(2,1)}, bf16[4,128,2,128]{3,1,2,0:T(8,128)(2,1)S(1)}, u32[]{:S(2)}, u32[]{:S(2)}) collective-permute-start(bf16[4,128,2,128]{3,1,2,0:T(8,128)(2,1)} %get-tuple-element.1781), channel_id=1, source_target_pairs={{124,0},{0,4},{4,8},{8,12},{12,16},{16,20},{20,24},{24,28},{28,32}... | collective-permute-start | bytes 786440 | tf_op jit(solution)/shard_map/while/body/eval_jaxpr/ppermute | solution.py:12
  1237.5 23.6 %collective-permute-start.1 = (f32[4,128,2,128]{3,1,2,0:T(8,128)}, f32[4,128,2,128]{3,1,2,0:T(8,128)}, u32[]{:S(2)}, u32[]{:S(2)}) collective-permute-start(f32[4,128,2,128]{3,1,2,0:T(8,128)} %get-tuple-element.1780), channel_id=1, source_target_pairs={{124,0},{0,4},{4,8},{8,12},{12,16},{16,20},{20,24},{24,28},{28,32}... | collective-permute-start | bytes 1572872 | tf_op jit(solution)/shard_map/while/body/eval_jaxpr/ppermute | solution.py:12
  1237.5 22.8 %collective-permute-start.2 = (bf16[4,128,2,128]{3,1,2,0:T(8,128)(2,1)}, bf16[4,128,2,128]{3,1,2,0:T(8,128)(2,1)S(1)}, u32[]{:S(2)}, u32[]{:S(2)}) collective-permute-start(bf16[4,128,2,128]{3,1,2,0:T(8,128)(2,1)} %get-tuple-element.1781), channel_id=1, source_target_pairs={{124,0},{0,4},{4,8},{8,12},{12,16},{16,20},{20,24},{24,28},{28,32}... | collective-permute-start | bytes 786440 | tf_op jit(solution)/shard_map/while/body/eval_jaxpr/ppermute | solution.py:12
  1268.2 24.8 %collective-permute-start.1 = (f32[4,128,2,128]{3,1,2,0:T(8,128)}, f32[4,128,2,128]{3,1,2,0:T(8,128)}, u32[]{:S(2)}, u32[]{:S(2)}) collective-permute-start(f32[4,128,2,128]{3,1,2,0:T(8,128)} %get-tuple-element.1780), channel_id=1, source_target_pairs={{124,0},{0,4},{4,8},{8,12},{12,16},{16,20},{20,24},{24,28},{28,32}... | collective-permute-start | bytes 1572872 | tf_op jit(solution)/shard_map/while/body/eval_jaxpr/ppermute | solution.py:12
  1268.2 24.0 %collective-permute-start.2 = (bf16[4,128,2,128]{3,1,2,0:T(8,128)(2,1)}, bf16[4,128,2,128]{3,1,2,0:T(8,128)(2,1)S(1)}, u32[]{:S(2)}, u32[]{:S(2)}) collective-permute-start(bf16[4,128,2,128]{3,1,2,0:T(8,128)(2,1)} %get-tuple-element.1781), channel_id=1, source_target_pairs={{124,0},{0,4},{4,8},{8,12},{12,16},{16,20},{20,24},{24,28},{28,32}... | collective-permute-start | bytes 786440 | tf_op jit(solution)/shard_map/while/body/eval_jaxpr/ppermute | solution.py:12
  1300.0 25.4 %collective-permute-start.1 = (f32[4,128,2,128]{3,1,2,0:T(8,128)}, f32[4,128,2,128]{3,1,2,0:T(8,128)}, u32[]{:S(2)}, u32[]{:S(2)}) collective-permute-start(f32[4,128,2,128]{3,1,2,0:T(8,128)} %get-tuple-element.1780), channel_id=1, source_target_pairs={{124,0},{0,4},{4,8},{8,12},{12,16},{16,20},{20,24},{24,28},{28,32}... | collective-permute-start | bytes 1572872 | tf_op jit(solution)/shard_map/while/body/eval_jaxpr/ppermute | solution.py:12
  1300.0 24.6 %collective-permute-start.2 = (bf16[4,128,2,128]{3,1,2,0:T(8,128)(2,1)}, bf16[4,128,2,128]{3,1,2,0:T(8,128)(2,1)S(1)}, u32[]{:S(2)}, u32[]{:S(2)}) collective-permute-start(bf16[4,128,2,128]{3,1,2,0:T(8,128)(2,1)} %get-tuple-element.1781), channel_id=1, source_target_pairs={{124,0},{0,4},{4,8},{8,12},{12,16},{16,20},{20,24},{24,28},{28,32}... | collective-permute-start | bytes 786440 | tf_op jit(solution)/shard_map/while/body/eval_jaxpr/ppermute | solution.py:12
  1332.4 17.3 %collective-permute-start.1 = (f32[4,128,2,128]{3,1,2,0:T(8,128)}, f32[4,128,2,128]{3,1,2,0:T(8,128)}, u32[]{:S(2)}, u32[]{:S(2)}) collective-permute-start(f32[4,128,2,128]{3,1,2,0:T(8,128)} %get-tuple-element.1780), channel_id=1, source_target_pairs={{124,0},{0,4},{4,8},{8,12},{12,16},{16,20},{20,24},{24,28},{28,32}... | collective-permute-start | bytes 1572872 | tf_op jit(solution)/shard_map/while/body/eval_jaxpr/ppermute | solution.py:12
  1356.7 17.3 %collective-permute-start.1 = (f32[4,128,2,128]{3,1,2,0:T(8,128)}, f32[4,128,2,128]{3,1,2,0:T(8,128)}, u32[]{:S(2)}, u32[]{:S(2)}) collective-permute-start(f32[4,128,2,128]{3,1,2,0:T(8,128)} %get-tuple-element.1780), channel_id=1, source_target_pairs={{124,0},{0,4},{4,8},{8,12},{12,16},{16,20},{20,24},{24,28},{28,32}... | collective-permute-start | bytes 1572872 | tf_op jit(solution)/shard_map/while/body/eval_jaxpr/ppermute | solution.py:12
  1381.0 17.4 %collective-permute-start.1 = (f32[4,128,2,128]{3,1,2,0:T(8,128)}, f32[4,128,2,128]{3,1,2,0:T(8,128)}, u32[]{:S(2)}, u32[]{:S(2)}) collective-permute-start(f32[4,128,2,128]{3,1,2,0:T(8,128)} %get-tuple-element.1780), channel_id=1, source_target_pairs={{124,0},{0,4},{4,8},{8,12},{12,16},{16,20},{20,24},{24,28},{28,32}... | collective-permute-start | bytes 1572872 | tf_op jit(solution)/shard_map/while/body/eval_jaxpr/ppermute | solution.py:12
  1381.0 16.5 %collective-permute-start.2 = (bf16[4,128,2,128]{3,1,2,0:T(8,128)(2,1)}, bf16[4,128,2,128]{3,1,2,0:T(8,128)(2,1)S(1)}, u32[]{:S(2)}, u32[]{:S(2)}) collective-permute-start(bf16[4,128,2,128]{3,1,2,0:T(8,128)(2,1)} %get-tuple-element.1781), channel_id=1, source_target_pairs={{124,0},{0,4},{4,8},{8,12},{12,16},{16,20},{20,24},{24,28},{28,32}... | collective-permute-start | bytes 786440 | tf_op jit(solution)/shard_map/while/body/eval_jaxpr/ppermute | solution.py:12
  1407.4 25.3 %all-to-all-start.2 = ((f32[128,24,128]{2,1,0:T(8,128)}), f32[128,24,128]{2,1,0:T(8,128)S(1)}, u32[]{:S(2)}, u32[]{:S(2)}) async-start(f32[128,24,128]{2,1,0:T(8,128)} %copy.93), calls=%async_computation.2 | async-start | bytes 3145728 | tf_op jit(solution)/shard_map/all_to_all | solution.py:155
  1411.5 18.6 %collective-permute-start.3 = (f32[4,128,2,128]{3,2,1,0:T(2,128)S(1)}, f32[4,128,2,128]{3,2,1,0:T(2,128)S(1)}, u32[]{:S(2)}, u32[]{:S(2)}) collective-permute-start(f32[4,128,2,128]{3,2,1,0:T(2,128)S(1)} %copy.95), channel_id=1, source_target_pairs={{124,0},{0,4},{4,8},{8,12},{12,16},{16,20},{20,24},{24,28},{28,32}... | collective-permute-start | bytes 1572872 | tf_op jit(solution)/shard_map/ppermute | solution.py:12
  (129 other events, 556.2 us)
where the time goes:
time: 1440 us; the launch traced here: 1430 us
  waiting for transfers between devices  883 us (61%)
  other arithmetic  202 us (14%)
  local copies, waits for them, and re-layouts  148 us (10%)
  matrix products  99.4 us (7%)
  loops' own time  84.7 us (6%)
    ppermute x94, waiting for transfers between devices, from_behind(): return lax.ppermute(block, axis, route)  862 us
    reduce_or x64, other arithmetic, guarded(): jnp.any((key_pos <= last_query) & (key_pos > first_query - widest))  83.9 us
    dot_general x104, matrix products, score_tile(): jnp.einsum('qgjd,kgd->qgjk', operand, partner, preferred_element_type=jnp...  62.6 us
    concatenate x32, other arithmetic, travel_grads(): return (query_grad, jnp.concatenate([low_sums, high_sums]))  56.6 us
    slice x31, local copies, waits for them, and re-layouts, travel_grads(): moving_grads[2:4]  54.9 us
    while x124, local copies, waits for them, and re-layouts  47.5 us
    another operation x1, loops' own time, shards(): held_state = lax.fori_loop(1, seq_count, pass_two, (held_state, home_kv))[0]  41 us
    another operation x1, loops' own time, shards(): running = lax.fori_loop(1, seq_count, pass_one, (running, home_kv))[0]  39.5 us
  transfers between devices with their start and end apart: 97, of which 66 were waited for; matrix products, arithmetic and copies ran while one was open for 8% of the time, Pallas kernels for 0%

commit v1 on v0

v1 whole, which is shorter than its diff:
```python
import functools
import math

import jax
import jax.numpy as jnp
from jax import lax
from jax.experimental import pallas as pl
from jax.experimental.pallas import tpu as pltpu
from jax.sharding import Mesh, PartitionSpec as P

BF, F4 = jnp.bfloat16, jnp.float32
NEG = -1e30
LOG2E = 1.4426950408889634
HD = 128
HEADS = 12
TOK = 128
SUB = 32
HALF = 2048
KB = 512
HPG = 6
ROWS = HPG * TOK
EXP_SCALE = LOG2E / math.sqrt(HD)
SCALE = 1.0 / math.sqrt(HD)
ALL = ("zl", "y", "x", "zh", "core")
COLUMN = ("zh", "core", "zl")


def nt(a, b):
    return lax.dot_general(a, b, (((1,), (1,)), ((), ())), preferred_element_type=F4)


def nn(a, b):
    return lax.dot_general(a, b, (((1,), (0,)), ((), ())), preferred_element_type=F4)


def block_plan(info, half, run):
    off, win, k = info[0] & (HALF - 1), info[1], info[2]
    t0 = run * HALF + k * TOK
    lo, hi = t0 - win + 1, t0 + TOK - 1
    new_base, old_base = HALF * half, HALF * half - 2 * HALF
    nblk = HALF // KB

    first = jnp.maximum(lo, new_base)
    last = jnp.minimum(hi, new_base + HALF - 1)
    new_first = (first - new_base) // KB
    n_new = jnp.where(last >= first, (last - new_base) // KB + 1 - new_first, 0)

    first_o = jnp.maximum(lo, old_base)
    last_o = jnp.minimum(hi, old_base + HALF - 1)
    start = (first_o - old_base + off) & (HALF - 1)
    old_first = start // KB
    n_old = jnp.where(
        last_o >= first_o,
        jnp.minimum((start - old_first * KB + last_o - first_o + KB) // KB, nblk),
        0,
    )

    def block(i):
        is_new = i < n_new
        ya = jnp.where(is_new, new_first + i, (old_first + i - n_new) & (nblk - 1))
        seg = jnp.where(is_new, 0, 1)
        wrap = off - ya * KB
        inside = (wrap > 0) & (wrap < KB)
        old_min = jnp.where(inside, 0, (ya * KB - off) & (HALF - 1)) + old_base
        pmin = jnp.where(is_new, new_base + ya * KB, old_min)
        pmax = jnp.where(is_new | ~inside, pmin + KB - 1, old_base + HALF - 1)
        full = (pmax <= t0) & (pmin > hi - win)

        def bias():
            r = lax.broadcasted_iota(jnp.int32, (KB, TOK), 0)
            res = ya * KB + r
            pos = jnp.where(is_new, new_base + res, ((res - off) & (HALF - 1)) + old_base)
            qp = t0 + lax.broadcasted_iota(jnp.int32, (KB, TOK), 1)
            b = jnp.where((pos <= qp) & (pos > qp - win), 0.0, NEG)
            return jnp.concatenate([b] * HPG, axis=1)

        return seg, ya, full, bias

    return n_new + n_old, block


def load_rows(qd_ref, which, run, hg, dst):
    for j in range(HPG):
        dst[pl.ds(j * TOK, TOK), :] = qd_ref[:, run, which, hg * HPG + j].reshape(TOK, HD)


def stats_kernel(half, first, info, qd_ref, kv_ref, *refs):
    if not first:
        prev, refs = refs[0], refs[1:]
    st_ref, q_s, do_s = refs

    def per_run(run, _):
        n_all, block = block_plan(info, half, run)

        def per_group(hg, _):
            load_rows(qd_ref, 0, run, hg, q_s)
            load_rows(qd_ref, 1, run, hg, do_s)

            def body(i, c):
                seg, yr, full, bias = block(i)
                k = kv_ref[pl.ds(4 * yr, 4), seg, 0].reshape(KB, HD)
                v = kv_ref[pl.ds(4 * yr, 4), seg, 1].reshape(KB, HD)

                def tile(masked, c):
                    m, l, t = c
                    s = nt(k, q_s[...]) * EXP_SCALE
                    if masked:
                        s = s + bias()
                    g3 = nt(v, do_s[...]).reshape(KB // 8, 8, ROWS)
                    s3 = s.reshape(KB // 8, 8, ROWS)
                    m2 = jnp.maximum(m, jnp.max(s3, axis=0))
                    al = jnp.exp2(m - m2)
                    e3 = jnp.exp2(s3 - m2[None])
                    return (m2, l * al + jnp.sum(e3, axis=0), t * al + jnp.sum(e3 * g3, axis=0))

                return lax.cond(full, functools.partial(tile, False), functools.partial(tile, True), c)

            if first:
                init = (jnp.full((8, ROWS), NEG, F4), jnp.zeros((8, ROWS), F4), jnp.zeros((8, ROWS), F4))
            else:
                init = tuple(prev[run, hg, j] for j in range(3))
            out = lax.fori_loop(0, n_all, body, init)
            for j in range(3):
                st_ref[run, hg, j] = out[j]
            return 0

        return lax.fori_loop(0, HEADS // HPG, per_group, 0)

    lax.fori_loop(0, 2, per_run, 0)


def grads_kernel(half, last, info, qd_ref, st_ref, kv_ref, *refs):
    if last:
        prev, refs = refs[0], refs[1:]
    dq_ref, out_ref, q_s, do_s, dqt_s, acc = refs

    def zero(i, _):
        acc[i] = jnp.zeros((2, 2, KB, HD), F4)
        return 0

    lax.fori_loop(0, 4, zero, 0)

    def per_run(run, _):
        n_all, block = block_plan(info, half, run)

        def per_group(hg, _):
            load_rows(qd_ref, 0, run, hg, q_s)
            load_rows(qd_ref, 1, run, hg, do_s)
            m, l, t = (st_ref[run, hg, j] for j in range(3))
            top = jnp.max(m, axis=0, keepdims=True)
            f = jnp.exp2(m - top)
            total = jnp.sum(l * f, axis=0, keepdims=True)
            lse = jnp.broadcast_to(top + jnp.log2(total), (8, ROWS))
            delta = jnp.broadcast_to(jnp.sum(t * f, axis=0, keepdims=True) / total, (8, ROWS))
            if last:
                dqt_s[...] = prev[run, hg]
            else:
                dqt_s[...] = jnp.zeros_like(dqt_s)

            def body(i, _):
                seg, yr, full, bias = block(i)

                def tile(masked):
                    k = kv_ref[pl.ds(4 * yr, 4), seg, 0].reshape(KB, HD)
                    v = kv_ref[pl.ds(4 * yr, 4), seg, 1].reshape(KB, HD)
                    s = nt(k, q_s[...]) * EXP_SCALE
                    if masked:
                        s = s + bias()
                    g3 = nt(v, do_s[...]).reshape(KB // 8, 8, ROWS)
                    p3 = jnp.exp2(s.reshape(KB // 8, 8, ROWS) - lse[None])
                    pb = p3.reshape(KB, ROWS).astype(BF)
                    ds = (p3 * (g3 - delta[None])).reshape(KB, ROWS).astype(BF)
                    acc[yr, seg, 1] += nn(pb, do_s[...])
                    acc[yr, seg, 0] += nn(ds, q_s[...])
                    dqt_s[...] += nn(jnp.transpose(k), ds)

                pl.when(full)(functools.partial(tile, False))
                pl.when(jnp.logical_not(full))(functools.partial(tile, True))
                return 0

            lax.fori_loop(0, n_all, body, 0)
            if last:
                dq = jnp.transpose(dqt_s[...]) * SCALE
                for j in range(HPG):
                    dq_ref[:, run, hg * HPG + j] = (
                        dq[j * TOK : (j + 1) * TOK].astype(dq_ref.dtype).reshape(TOK // SUB, SUB, HD)
                    )
            else:
                dq_ref[run, hg] = dqt_s[...]
            return 0

        return lax.fori_loop(0, HEADS // HPG, per_group, 0)

    lax.fori_loop(0, 2, per_run, 0)
    for yr in range(4):
        for seg in range(2):
            cols = pl.ds(4 * yr, 4)
            out_ref[cols, seg, 0] = (acc[yr, seg, 0] * SCALE).astype(BF).reshape(4, TOK, HD)
            out_ref[cols, seg, 1] = acc[yr, seg, 1].astype(BF).reshape(4, TOK, HD)


VM = pl.BlockSpec(memory_space=pltpu.VMEM)
SM = pl.BlockSpec(memory_space=pltpu.SMEM)
COMMON = (
    pltpu.VMEM((ROWS, HD), BF),
    pltpu.VMEM((ROWS, HD), BF),
)
STAT_SHAPE = (2, HEADS // HPG, 3, 8, ROWS)


def stats_call(half, first, info, qd, kv, prev=None):
    ops = [info, qd, kv] + ([] if first else [prev])
    return pl.pallas_call(
        functools.partial(stats_kernel, half, first),
        out_shape=jax.ShapeDtypeStruct(STAT_SHAPE, F4),
        in_specs=[SM, VM, VM] + ([] if first else [VM]),
        out_specs=VM,
        scratch_shapes=[*COMMON],
        compiler_params=pltpu.CompilerParams(vmem_limit_bytes=48 * 2**20),
        cost_estimate=pl.CostEstimate(flops=2 * 2 * 3072 * 2112 * HD * 2, bytes_accessed=4 << 20, transcendentals=3072 * 2112),
        name="stats%d" % half,
    )(*ops)


def grads_call(half, last, info, qd, stats, kv, prev=None):
    ops = [info, qd, stats, kv] + ([prev] if last else [])
    dq_shape = (
        jax.ShapeDtypeStruct((4, 2, HEADS, SUB, HD), BF)
        if last
        else jax.ShapeDtypeStruct((2, HEADS // HPG, HD, ROWS), F4)
    )
    outs = pl.pallas_call(
        functools.partial(grads_kernel, half, last),
        out_shape=(dq_shape, jax.ShapeDtypeStruct((16, 2, 2, TOK, HD), BF)),
        in_specs=[SM, VM, VM, VM] + ([VM] if last else []),
        out_specs=(VM, VM),
        scratch_shapes=[
            *COMMON,
            pltpu.VMEM((HD, ROWS), F4),
            pltpu.VMEM((4, 2, 2, KB, HD), F4),
        ],
        compiler_params=pltpu.CompilerParams(vmem_limit_bytes=48 * 2**20),
        cost_estimate=pl.CostEstimate(flops=5 * 2 * 3072 * 2112 * HD * 2, bytes_accessed=8 << 20, transcendentals=3072 * 2112),
        name="grads%d" % half,
    )(*ops)
    return outs


def gather_half(new, old):
    block = jnp.broadcast_to(jnp.stack([new, old])[None], (16, 2, 2, TOK, HD))
    return lax.all_to_all(block, ("y", "x"), 0, 0, tiled=True)


def reduce_half(blocks):
    return jnp.sum(lax.all_to_all(blocks, ("y", "x"), 0, 0, tiled=True).astype(F4), axis=0)


def shards(query, key_new, value_new, key_old, value_old, offset, windows, grad_out):
    zl, yy, xx = lax.axis_index("zl"), lax.axis_index("y"), lax.axis_index("x")
    col = 4 * yy + xx
    swap = lambda a: lax.ppermute(a, "zl", [(0, 1), (1, 0)])

    kv = jnp.stack([jnp.stack([key_new, value_new]), jnp.stack([key_old, value_old])])
    kv = jnp.moveaxis(kv, 3, 0)
    mine = jnp.where(zl == 0, kv[0], kv[1])
    theirs = swap(jnp.where(zl == 0, kv[1], kv[0]))
    z0 = jnp.where(zl == 0, mine, theirs)
    z1 = jnp.where(zl == 0, theirs, mine)
    slot = col * TOK + jnp.arange(TOK, dtype=jnp.int32)
    upper = (((slot - offset[0]) & (2 * HALF - 1)) >= HALF)[None, :, None]
    old_hi = jnp.where(upper, z0[1], z1[1])
    old_lo = jnp.where(upper, z1[1], z0[1])

    def rows_of(a):
        return jnp.swapaxes(a, 0, 1).reshape(8, 1, HEADS, SUB, HD)

    qd = jnp.concatenate([rows_of(query), rows_of(grad_out)], axis=1)
    qd = lax.all_to_all(qd, COLUMN, 0, 0, tiled=True).reshape(4, 2, 2, HEADS, SUB, HD)

    kv_hi = gather_half(z1[0], old_hi)
    new_lo, old_lo, kv_hi = lax.optimization_barrier((z0[0], old_lo, kv_hi))
    kv_lo = gather_half(new_lo, old_lo)

    win = jnp.where(zl == 0, windows[0], windows[1])
    zero = jnp.int32(0)
    info = jnp.stack([offset[0], win, col, zero]).astype(jnp.int32)

    stats = stats_call(1, True, info, qd, kv_hi)
    stats = stats_call(0, False, info, qd, kv_lo, stats)
    dq_part, blocks_hi = grads_call(1, False, info, qd, stats, kv_hi)
    sum_hi = reduce_half(blocks_hi)
    dq, blocks_lo = grads_call(0, True, info, qd, stats, kv_lo, dq_part)
    sum_lo = reduce_half(blocks_lo)

    dq = lax.all_to_all(dq.reshape(8, HEADS, SUB, HD), COLUMN, 0, 0, tiled=True)
    grad_query = jnp.swapaxes(dq.reshape(8 * HEADS, SUB, HD), 0, 1).astype(F4)

    r0 = jnp.stack([sum_lo[0], jnp.where(upper, sum_hi[1], sum_lo[1])])
    r1 = jnp.stack([sum_hi[0], jnp.where(upper, sum_lo[1], sum_hi[1])])
    keep = jnp.where(zl == 0, r0, r1)
    got = swap(jnp.where(zl == 0, r1, r0).astype(BF)).astype(F4)
    both = jnp.stack([jnp.where(zl == 0, keep, got), jnp.where(zl == 0, got, keep)], axis=3)
    return (grad_query, both[0, 0], both[0, 1], both[1, 0], both[1, 1])


def solution(mesh):
    fine = Mesh(mesh.devices.reshape(2, 4, 4, 2, 2), ALL)
    tokens = P(ALL, None, None)
    slots = P(("zl", "y", "x"), ("zh", "core"), None)
    return jax.shard_map(
        shards,
        mesh=fine,
        in_specs=(tokens, slots, slots, slots, slots, P(), P(("zh", "core")), tokens),
        out_specs=(tokens, slots, slots, slots, slots),
        check_vma=False,
    )
```

time: 1440 us -> 256 us (0.18)
  the two profiles are of different devices: /device:TPU:32 before, /device:TPU:0 now
where the time goes in v1:
time: 256 us; the launch traced here: 251 us
  waiting for transfers between devices  79.6 us (31%)
  Pallas kernels  62.9 us (25%)
  blocking collectives  61.6 us (24%)
  starting transfers between devices  29 us (11%)
  local copies, waits for them, and re-layouts  12.2 us (5%)
  other arithmetic  2.92 us (1%)
  between operations  2.79 us (1%)
    all_to_all x2, blocking collectives, reduce_half(): lax.all_to_all(blocks, ('y', 'x'), 0, 0, tiled=True).astype(F4)  61.6 us
    all_to_all x2, waiting for transfers between devices, gather_half(): return lax.all_to_all(block, ('y', 'x'), 0, 0, tiled=True)  45.6 us
    pallas_call x2, Pallas kernels, grads_call(): pl.pallas_call(functools.partial(grads_kernel, half, last), out_shape=(dq...  39.4 us
    pallas_call x2, Pallas kernels, stats_call(): pl.pallas_call(functools.partial(stats_kernel, half, first), out_shape=ja...  23.4 us
    all_to_all x1, waiting for transfers between devices, shards(): lax.all_to_all(qd, COLUMN, 0, 0, tiled=True)  21.6 us
    all_to_all x2, starting transfers between devices, gather_half(): return lax.all_to_all(block, ('y', 'x'), 0, 0, tiled=True)  11.7 us
    all_to_all x1, waiting for transfers between devices, shards(): dq = lax.all_to_all(dq.reshape(8, HEADS, SUB, HD), COLUMN, 0, 0, tiled=True)  9.46 us
    all_to_all x1, starting transfers between devices, shards(): dq = lax.all_to_all(dq.reshape(8, HEADS, SUB, HD), COLUMN, 0, 0, tiled=True)  8.22 us
  transfers between devices with their start and end apart: 6, of which 5 were waited for; matrix products, arithmetic and copies ran while one was open for 2% of the time, Pallas kernels for 5%

profile of v1, /device:TPU:0, one launch (start us, length us, event | category | flops | bytes accessed | tf_op | source)
XLA Modules:
  0.0 250.9 jit_solution(8186192203033295216)
XLA Ops:
  0.6 0.9 copy_bitcast_fusion.2
  1.6 0.9 copy_bitcast_fusion
  2.5 2.1 collective-permute-start
  5.3 2.8 %collective-permute-done = bf16[2,2,128,128]{3,2,1,0:T(8,128)(2,1)S(1)} collective-permute-done((bf16[2,2,128,128]{3,2,1,0:T(8,128)(2,1)S(1)}, bf16[2,2,128,128]{3,2,1,0:T(8,128)(2,1)S(1)}, u32[]{:S(2)}, u32[]{:S(2)}) %collective-permute-start) | collective-permute-done | bytes 131104 | tf_op jit(solution)/shard_map/ppermute | solution.py:261
  8.1 0.1 fusion.8
  8.3 1.9 broadcast_in_dim.37
  10.1 0.0 copy-start.2
  10.1 7.2 %all-to-all-start.1 = ((bf16[16,2,2,128,128]{4,3,2,1,0:T(8,128)(2,1)}), bf16[16,2,2,128,128]{4,3,2,1,0:T(8,128)(2,1)S(1)}, u32[]{:S(2)}, u32[]{:S(2)}) async-start(bf16[16,2,2,128,128]{4,3,2,1,0:T(8,128)(2,1)} %broadcast_in_dim.37), calls=%async_computation.1 | async-start | bytes 4194304 | tf_op jit(solution)/shard_map/all_to_all | solution.py:251
  17.3 0.0 copy-done.2
  17.3 0.0 copy-start.3
  17.3 0.3 copy.30
  17.6 0.8 copy-done.3
  18.4 0.3 copy.31
  18.7 0.1 pad_maximum_fusion
  18.9 1.4 copy.32
  20.3 27.1 %all-to-all-done.1.kv_ref = bf16[16,2,2,128,128]{4,3,2,1,0:T(8,128)(2,1)S(1)} async-done(((bf16[16,2,2,128,128]{4,3,2,1,0:T(8,128)(2,1)}), bf16[16,2,2,128,128]{4,3,2,1,0:T(8,128)(2,1)S(1)}, u32[]{:S(2)}, u32[]{:S(2)}) %all-to-all-start.1) | async-done | bytes 2097184 | tf_op jit(solution)/shard_map/all_to_all | solution.py:251
  47.4 0.0 copy-start
  47.4 4.8 %all-to-all-start = ((bf16[8,2,12,32,128]{4,3,2,1,0:T(8,128)(2,1)}), bf16[8,2,12,32,128]{4,3,2,1,0:T(8,128)(2,1)}, u32[]{:S(2)}, u32[]{:S(2)}) async-start(bf16[8,2,12,32,128]{4,3,2,1,0:T(8,128)(2,1)} %copy.32), calls=%async_computation | async-start | bytes 3145728 | tf_op jit(solution)/shard_map/all_to_all | solution.py:278
  52.2 0.1 bitcast_select_fusion.2
  52.4 21.6 %all-to-all-done = bf16[8,2,12,32,128]{4,3,2,1,0:T(8,128)(2,1)} async-done(((bf16[8,2,12,32,128]{4,3,2,1,0:T(8,128)(2,1)}), bf16[8,2,12,32,128]{4,3,2,1,0:T(8,128)(2,1)}, u32[]{:S(2)}, u32[]{:S(2)}) %all-to-all-start) | async-done | bytes 1572896 | tf_op jit(solution)/shard_map/all_to_all | solution.py:278
  74.0 1.9 broadcast_in_dim.38
  75.9 0.0 copy-start.4
  75.9 4.6 %all-to-all-start.2 = ((bf16[16,2,2,128,128]{4,3,2,1,0:T(8,128)(2,1)}), bf16[16,2,2,128,128]{4,3,2,1,0:T(8,128)(2,1)}, u32[]{:S(2)}, u32[]{:S(2)}) async-start(bf16[16,2,2,128,128]{4,3,2,1,0:T(8,128)(2,1)} %broadcast_in_dim.38), calls=%async_computation.2 | async-start | bytes 4194304 | tf_op jit(solution)/shard_map/all_to_all | solution.py:251
  80.4 0.0 copy-done.4
  80.4 0.6 fusion.9
  82.3 0.1 pad_add_fusion.info
  82.4 0.0 copy-done
  82.4 11.4 %stats1.1.refs_0_ = f32[2,2,3,8,768]{4,3,2,1,0:T(8,128)S(1)} custom-call(s32[4]{0:T(128)S(1)} %pad_add_fusion.info, bf16[4,2,2,12,32,128]{5,4,3,2,1,0:T(8,128)(2,1)} %bitcast.8.qd_ref, bf16[16,2,2,128,128]{4,3,2,1,0:T(8,128)(2,1)S(1)} %all-to-all-done.1.kv_ref), custom_call_target="tpu_custom_call" | custom-call | flops 6643777536 | bytes 4194304 | tf_op jit(solution)/shard_map/stats1/pallas_call | solution.py:213
  93.8 18.5 %all-to-all-done.2.kv_ref = bf16[16,2,2,128,128]{4,3,2,1,0:T(8,128)(2,1)} async-done(((bf16[16,2,2,128,128]{4,3,2,1,0:T(8,128)(2,1)}), bf16[16,2,2,128,128]{4,3,2,1,0:T(8,128)(2,1)}, u32[]{:S(2)}, u32[]{:S(2)}) %all-to-all-start.2) | async-done | bytes 2097184 | tf_op jit(solution)/shard_map/all_to_all | solution.py:251
  112.4 12.0 %stats0.1.st_ref = f32[2,2,3,8,768]{4,3,2,1,0:T(8,128)S(1)} custom-call(s32[4]{0:T(128)S(1)} %pad_add_fusion.info, bf16[4,2,2,12,32,128]{5,4,3,2,1,0:T(8,128)(2,1)} %bitcast.8.qd_ref, bf16[16,2,2,128,128]{4,3,2,1,0:T(8,128)(2,1)} %all-to-all-done.2.kv_ref, f32[2,2,3,8,768]{4,3,2,1,0:T(8,128)S(1)} %stats1.1.refs_0_), custom_call_target="tpu_custom_call" | custom-call | flops 6643777536 | bytes 4194304 | tf_op jit(solution)/shard_map/stats0/pallas_call | solution.py:213
  124.4 18.8 %grads1.1 = (f32[2,2,128,768]{3,2,1,0:T(8,128)S(1)}, bf16[16,2,2,128,128]{4,3,2,1,0:T(8,128)(2,1)S(1)}) custom-call(s32[4]{0:T(128)S(1)} %pad_add_fusion.info, bf16[4,2,2,12,32,128]{5,4,3,2,1,0:T(8,128)(2,1)} %bitcast.8.qd_ref, f32[2,2,3,8,768]{4,3,2,1,0:T(8,128)S(1)} %stats0.1.st_ref, bf16[16,2,2,128,128]{4,3,2,1,0:T(8,128)(2,1)} %copy-done), custom_call_target="tpu_custom_call" | custom-call | flops 16609443840 | bytes 8388608 | tf_op jit(solution)/shard_map/grads1/pallas_call | solution.py:232
  143.2 20.7 %grads0.1 = (bf16[4,2,12,32,128]{4,3,2,1,0:T(8,128)(2,1)}, bf16[16,2,2,128,128]{4,3,2,1,0:T(8,128)(2,1)}) custom-call(s32[4]{0:T(128)S(1)} %pad_add_fusion.info, bf16[4,2,2,12,32,128]{5,4,3,2,1,0:T(8,128)(2,1)} %bitcast.8.qd_ref, f32[2,2,3,8,768]{4,3,2,1,0:T(8,128)S(1)} %stats0.1.st_ref, bf16[16,2,2,128,128]{4,3,2,1,0:T(8,128)(2,1)} %all-to-all-done.2.kv_ref, ...), custom_call_target="tpu_custom_call" | custom-call | flops 16609443840 | bytes 8388608 | tf_op jit(solution)/shard_map/grads0/pallas_call | solution.py:232
  163.8 29.9 %all_to_all.30 = bf16[16,2,2,128,128]{4,3,2,1,0:T(8,128)(2,1)S(1)} all-to-all(bf16[16,2,2,128,128]{4,3,2,1,0:T(8,128)(2,1)} %get-tuple-element.17), channel_id=1, replica_groups=mesh['zl'=2,'y'=4,'x'=4,'zh'=2,'core'=2] {'y','x'}, dimensions={0} | all-to-all | bytes 4194304 | tf_op jit(solution)/shard_map/all_to_all | solution.py:255
  193.8 31.7 %all_to_all.31 = bf16[16,2,2,128,128]{4,3,2,1,0:T(8,128)(2,1)} all-to-all(bf16[16,2,2,128,128]{4,3,2,1,0:T(8,128)(2,1)S(1)} %get-tuple-element.18), channel_id=1, replica_groups=mesh['zl'=2,'y'=4,'x'=4,'zh'=2,'core'=2] {'y','x'}, dimensions={0} | all-to-all | bytes 4194304 | tf_op jit(solution)/shard_map/all_to_all | solution.py:255
  225.4 8.2 %all-to-all-start.3 = ((bf16[8,12,32,128]{3,2,1,0:T(8,128)(2,1)}), bf16[8,12,32,128]{3,2,1,0:T(8,128)(2,1)S(1)}, u32[]{:S(2)}, u32[]{:S(2)}) async-start(bf16[8,12,32,128]{3,2,1,0:T(8,128)(2,1)} %bitcast.24), calls=%async_computation.3 | async-start | bytes 1572864 | tf_op jit(solution)/shard_map/all_to_all | solution.py:295
  233.6 0.0 copy-start.1
  233.7 0.4 convert_reduce_fusion.1
  234.0 1.2 copy-done.1
  235.2 0.4 convert_reduce_fusion
  235.6 0.1 slice_select_fusion.1
  235.8 2.1 collective-permute-start.1
  237.9 9.5 %all-to-all-done.3 = bf16[8,12,32,128]{3,2,1,0:T(8,128)(2,1)S(1)} async-done(((bf16[8,12,32,128]{3,2,1,0:T(8,128)(2,1)}), bf16[8,12,32,128]{3,2,1,0:T(8,128)(2,1)S(1)}, u32[]{:S(2)}, u32[]{:S(2)}) %all-to-all-start.3) | async-done | bytes 786464 | tf_op jit(solution)/shard_map/all_to_all | solution.py:295
  247.3 0.3 convert_bitcast_fusion
  247.6 2.1 copy.38
  249.6 0.0 collective-permute-done.1
  249.7 1.2 fusion.4
  (10 shorter events, 0.2 us)
Async XLA Ops:
  2.5 5.6 %collective-permute-start = (bf16[2,2,128,128]{3,2,1,0:T(8,128)(2,1)S(1)}, bf16[2,2,128,128]{3,2,1,0:T(8,128)(2,1)S(1)}, u32[]{:S(2)}, u32[]{:S(2)}) collective-permute-start(bf16[2,2,128,128]{3,2,1,0:T(8,128)(2,1)S(1)} %select_bitcast_fusion), channel_id=1, source_target_pairs={{0,64},{64,0},{1,65},{65,1},{2,66},{66,2},{3,67},{67,3},{4,68},{68... | collective-permute-start | bytes 393224 | tf_op jit(solution)/shard_map/ppermute | solution.py:261
  10.1 7.2 %copy-start.2 = (bf16[32,96,128]{2,1,0:T(8,128)(2,1)S(1)}, bf16[32,96,128]{2,1,0:T(8,128)(2,1)}, u32[]{:S(2)}) copy-start(bf16[32,96,128]{2,1,0:T(8,128)(2,1)} %param.8) | copy-start | bytes 2359300
  10.1 37.3 %all-to-all-start.1 = ((bf16[16,2,2,128,128]{4,3,2,1,0:T(8,128)(2,1)}), bf16[16,2,2,128,128]{4,3,2,1,0:T(8,128)(2,1)S(1)}, u32[]{:S(2)}, u32[]{:S(2)}) async-start(bf16[16,2,2,128,128]{4,3,2,1,0:T(8,128)(2,1)} %broadcast_in_dim.37), calls=%async_computation.1 | async-start | bytes 4194304 | tf_op jit(solution)/shard_map/all_to_all | solution.py:251
  17.3 1.1 copy-start.3
  47.4 35.0 %copy-start = (bf16[16,2,2,128,128]{4,3,2,1,0:T(8,128)(2,1)}, bf16[16,2,2,128,128]{4,3,2,1,0:T(8,128)(2,1)S(1)}, u32[]{:S(2)}) copy-start(bf16[16,2,2,128,128]{4,3,2,1,0:T(8,128)(2,1)S(1)} %all-to-all-done.1.kv_ref) | copy-start | bytes 6291460
  47.4 26.6 %all-to-all-start = ((bf16[8,2,12,32,128]{4,3,2,1,0:T(8,128)(2,1)}), bf16[8,2,12,32,128]{4,3,2,1,0:T(8,128)(2,1)}, u32[]{:S(2)}, u32[]{:S(2)}) async-start(bf16[8,2,12,32,128]{4,3,2,1,0:T(8,128)(2,1)} %copy.32), calls=%async_computation | async-start | bytes 3145728 | tf_op jit(solution)/shard_map/all_to_all | solution.py:278
  75.9 4.6 %copy-start.4 = (s32[2]{0:T(128)S(1)}, s32[2]{0:T(128)}, u32[]{:S(2)}) copy-start(s32[2]{0:T(128)} %param.14) | copy-start | bytes 28
  75.9 36.5 %all-to-all-start.2 = ((bf16[16,2,2,128,128]{4,3,2,1,0:T(8,128)(2,1)}), bf16[16,2,2,128,128]{4,3,2,1,0:T(8,128)(2,1)}, u32[]{:S(2)}, u32[]{:S(2)}) async-start(bf16[16,2,2,128,128]{4,3,2,1,0:T(8,128)(2,1)} %broadcast_in_dim.38), calls=%async_computation.2 | async-start | bytes 4194304 | tf_op jit(solution)/shard_map/all_to_all | solution.py:251
  225.4 21.9 %all-to-all-start.3 = ((bf16[8,12,32,128]{3,2,1,0:T(8,128)(2,1)}), bf16[8,12,32,128]{3,2,1,0:T(8,128)(2,1)S(1)}, u32[]{:S(2)}, u32[]{:S(2)}) async-start(bf16[8,12,32,128]{3,2,1,0:T(8,128)(2,1)} %bitcast.24), calls=%async_computation.3 | async-start | bytes 1572864 | tf_op jit(solution)/shard_map/all_to_all | solution.py:295
  233.6 1.6 copy-start.1
  235.8 13.9 %collective-permute-start.1 = (bf16[2,2,128,128]{3,2,1,0:T(8,128)(2,1)S(1)}, bf16[2,2,128,128]{3,2,1,0:T(8,128)(2,1)S(1)}, u32[]{:S(2)}, u32[]{:S(2)}) collective-permute-start(bf16[2,2,128,128]{3,2,1,0:T(8,128)(2,1)S(1)} %select_convert_fusion), channel_id=1, source_target_pairs={{0,64},{64,0},{1,65},{65,1},{2,66},{66,2},{3,67},{67,3},{4,68},{68... | collective-permute-start | bytes 393224 | tf_op jit(solution)/shard_map/ppermute | solution.py:261

commit v2 on v1

v2 whole, which is shorter than its diff:
```python
import functools
import math

import jax
import jax.numpy as jnp
from jax import lax
from jax.experimental import pallas as pl
from jax.experimental.pallas import tpu as pltpu
from jax.sharding import Mesh, PartitionSpec as P

BF, F4 = jnp.bfloat16, jnp.float32
NEG = -1e30
LOG2E = 1.4426950408889634
HD = 128
HEADS = 12
TOK = 128
SUB = 32
HALF = 2048
KB = 512
PART = 64
ROWS = HEADS * PART
EXP_SCALE = LOG2E / math.sqrt(HD)
SCALE = 1.0 / math.sqrt(HD)
ALL = ("zl", "yh", "yp", "x", "zh", "core")
COLUMN = ("zh", "yp", "zl")
PLANE = ("yh", "core", "x")


def nt(a, b):
    return lax.dot_general(a, b, (((1,), (1,)), ((), ())), preferred_element_type=F4)


def nn(a, b):
    return lax.dot_general(a, b, (((1,), (0,)), ((), ())), preferred_element_type=F4)


def block_plan(info, half, run):
    off, win, col, core = info[0] & (HALF - 1), info[1], info[2], info[3]
    zl, yp = run // 2, run % 2
    t0 = zl * HALF + (col + 4 * yp) * TOK + core * SUB
    t1 = t0 + 2 * SUB + SUB - 1
    lo = t0 - win + 1
    new_base, old_base = HALF * half, HALF * half - 2 * HALF
    nblk = HALF // KB

    first = jnp.maximum(lo, new_base)
    last = jnp.minimum(t1, new_base + HALF - 1)
    new_first = (first - new_base) // KB
    n_new = jnp.where(last >= first, (last - new_base) // KB + 1 - new_first, 0)

    first_o = jnp.maximum(lo, old_base)
    last_o = jnp.minimum(t1, old_base + HALF - 1)
    start = (first_o - old_base + off) & (HALF - 1)
    old_first = start // KB
    n_old = jnp.where(
        last_o >= first_o,
        jnp.minimum((start - old_first * KB + last_o - first_o + KB) // KB, nblk),
        0,
    )

    def block(i):
        is_new = i < n_new
        ya = jnp.where(is_new, new_first + i, (old_first + i - n_new) & (nblk - 1))
        seg = jnp.where(is_new, 0, 1)
        wrap = off - ya * KB
        inside = (wrap > 0) & (wrap < KB)
        old_min = jnp.where(inside, 0, (ya * KB - off) & (HALF - 1)) + old_base
        pmin = jnp.where(is_new, new_base + ya * KB, old_min)
        pmax = jnp.where(is_new | ~inside, pmin + KB - 1, old_base + HALF - 1)
        full = (pmax <= t0) & (pmin > t1 - win)

        def bias():
            res = ya * KB + lax.broadcasted_iota(jnp.int32, (KB, TOK), 0)
            pos = jnp.where(is_new, new_base + res, ((res - off) & (HALF - 1)) + old_base)
            lane = lax.broadcasted_iota(jnp.int32, (KB, TOK), 1)
            qp = t0 + (lane & (SUB - 1)) + ((lane & SUB) << 1)
            b = jnp.where((pos <= qp) & (pos > qp - win), 0.0, NEG)
            return jnp.concatenate([b] * (ROWS // TOK), axis=1)

        place = ((ya & 1) ^ core, pl.ds(4 * (ya >> 1), 4))
        return seg, ya, place, full, bias

    return n_new + n_old, block


def load_rows(qd_ref, which, run, dst):
    for j in range(HEADS):
        dst[pl.ds(j * PART, PART), :] = qd_ref[:, run % 2, run // 2, which, j].reshape(PART, HD)


def fetch(srcs, kv_s, sem):
    copies = [pltpu.make_async_copy(s, kv_s.at[i], sem.at[i]) for i, s in enumerate(srcs)]
    for c in copies:
        c.start()
    for c in copies:
        c.wait()


def stats_kernel(info, qd_ref, own, other, st_ref, q_s, do_s, kv_s, sem):
    fetch((own, other), kv_s, sem)

    def per_run(run, _):
        load_rows(qd_ref, 0, run, q_s)
        load_rows(qd_ref, 1, run, do_s)
        c = (jnp.full((8, ROWS), NEG, F4), jnp.zeros((8, ROWS), F4), jnp.zeros((8, ROWS), F4))
        for half in (1, 0):
            n_all, block = block_plan(info, half, run)

            def body(i, c, half=half, block=block):
                seg, ya, (rel, cols), full, bias = block(i)
                k = kv_s[rel, cols, half, seg, 0].reshape(KB, HD)
                v = kv_s[rel, cols, half, seg, 1].reshape(KB, HD)

                def tile(masked, c):
                    m, l, t = c
                    s = nt(k, q_s[...]) * EXP_SCALE
                    if masked:
                        s = s + bias()
                    g3 = nt(v, do_s[...]).reshape(KB // 8, 8, ROWS)
                    s3 = s.reshape(KB // 8, 8, ROWS)
                    m2 = jnp.maximum(m, jnp.max(s3, axis=0))
                    al = jnp.exp2(m - m2)
                    e3 = jnp.exp2(s3 - m2[None])
                    return (m2, l * al + jnp.sum(e3, axis=0), t * al + jnp.sum(e3 * g3, axis=0))

                return lax.cond(full, functools.partial(tile, False), functools.partial(tile, True), c)

            c = lax.fori_loop(0, n_all, body, c)
        m, l, t = c
        top = jnp.max(m, axis=0, keepdims=True)
        f = jnp.exp2(m - top)
        total = jnp.sum(l * f, axis=0, keepdims=True)
        st_ref[run, 0] = jnp.broadcast_to(top + jnp.log2(total), (8, ROWS))
        st_ref[run, 1] = jnp.broadcast_to(jnp.sum(t * f, axis=0, keepdims=True) / total, (8, ROWS))
        return 0

    lax.fori_loop(0, 4, per_run, 0)


def grads_kernel(half, last, info, qd_ref, st_ref, own, other, *refs):
    if last:
        prev, refs = refs[0], refs[1:]
    dq_ref, out_ref, q_s, do_s, kv_s, sem, dqt_s, acc = refs
    fetch((own.at[:, half], other.at[:, half]), kv_s, sem)

    def zero(i, _):
        acc[i] = jnp.zeros((2, 2, KB, HD), F4)
        return 0

    lax.fori_loop(0, 4, zero, 0)

    def per_run(run, _):
        n_all, block = block_plan(info, half, run)
        load_rows(qd_ref, 0, run, q_s)
        load_rows(qd_ref, 1, run, do_s)
        lse, delta = st_ref[run, 0], st_ref[run, 1]
        if last:
            dqt_s[...] = prev[run]
        else:
            dqt_s[...] = jnp.zeros_like(dqt_s)

        def body(i, _):
            seg, ya, (rel, cols), full, bias = block(i)

            def tile(masked):
                k = kv_s[rel, cols, seg, 0].reshape(KB, HD)
                v = kv_s[rel, cols, seg, 1].reshape(KB, HD)
                s = nt(k, q_s[...]) * EXP_SCALE
                if masked:
                    s = s + bias()
                g3 = nt(v, do_s[...]).reshape(KB // 8, 8, ROWS)
                p3 = jnp.exp2(s.reshape(KB // 8, 8, ROWS) - lse[None])
                pb = p3.reshape(KB, ROWS).astype(BF)
                ds = (p3 * (g3 - delta[None])).reshape(KB, ROWS).astype(BF)
                acc[ya, seg, 1] += nn(pb, do_s[...])
                acc[ya, seg, 0] += nn(ds, q_s[...])
                dqt_s[...] += nn(jnp.transpose(k), ds)

            pl.when(full)(functools.partial(tile, False))
            pl.when(jnp.logical_not(full))(functools.partial(tile, True))
            return 0

        lax.fori_loop(0, n_all, body, 0)
        if last:
            dq = (jnp.transpose(dqt_s[...]) * SCALE).astype(BF)
            for j in range(HEADS):
                for zh in range(2):
                    rows = dq[j * PART + zh * SUB : j * PART + (zh + 1) * SUB]
                    dq_ref[info[4] ^ (4 * zh + 2 * (run % 2) + run // 2), j] = rows
        else:
            dq_ref[run] = dqt_s[...]
        return 0

    lax.fori_loop(0, 4, per_run, 0)
    for ya in range(4):
        for seg in range(2):
            cols = pl.ds(4 * ya, 4)
            out_ref[cols, seg, 0] = (acc[ya, seg, 0] * SCALE).astype(BF).reshape(4, TOK, HD)
            out_ref[cols, seg, 1] = acc[ya, seg, 1].astype(BF).reshape(4, TOK, HD)


VM = pl.BlockSpec(memory_space=pltpu.VMEM)
SM = pl.BlockSpec(memory_space=pltpu.SMEM)
ANY = pl.BlockSpec(memory_space=pl.ANY)
ROW_SCRATCH = (pltpu.VMEM((ROWS, HD), BF), pltpu.VMEM((ROWS, HD), BF))
PAIRS = 3072 * 3300


def stats_call(info, qd, own, other):
    return pl.pallas_call(
        stats_kernel,
        out_shape=jax.ShapeDtypeStruct((4, 2, 8, ROWS), F4),
        in_specs=[SM, VM, ANY, ANY],
        out_specs=VM,
        scratch_shapes=[
            *ROW_SCRATCH,
            pltpu.VMEM((2, 8, 2, 2, 2, TOK, HD), BF),
            pltpu.SemaphoreType.DMA((2,)),
        ],
        compiler_params=pltpu.CompilerParams(vmem_limit_bytes=26 * 2**20),
        cost_estimate=pl.CostEstimate(flops=8 * PAIRS * HD, bytes_accessed=4 << 20, transcendentals=PAIRS),
        name="stats",
    )(info, qd, own, other)


def grads_call(half, last, info, qd, stats, own, other, prev=None):
    dq_shape = (
        jax.ShapeDtypeStruct((8, HEADS, SUB, HD), BF)
        if last
        else jax.ShapeDtypeStruct((4, HD, ROWS), F4)
    )
    return pl.pallas_call(
        functools.partial(grads_kernel, half, last),
        out_shape=(dq_shape, jax.ShapeDtypeStruct((16, 2, 2, TOK, HD), BF)),
        in_specs=[SM, VM, VM, ANY, ANY] + ([VM] if last else []),
        out_specs=(VM, VM),
        scratch_shapes=[
            *ROW_SCRATCH,
            pltpu.VMEM((2, 8, 2, 2, TOK, HD), BF),
            pltpu.SemaphoreType.DMA((2,)),
            pltpu.VMEM((HD, ROWS), F4),
            pltpu.VMEM((4, 2, 2, KB, HD), F4),
        ],
        compiler_params=pltpu.CompilerParams(vmem_limit_bytes=32 * 2**20),
        cost_estimate=pl.CostEstimate(flops=10 * PAIRS * HD, bytes_accessed=8 << 20, transcendentals=PAIRS // 2),
        name="grads%d" % half,
    )(*([info, qd, stats, own, other] + ([prev] if last else [])))


def place_kernel(info, *refs):
    *pieces, out_ref = refs
    for d, piece in enumerate(pieces):
        out_ref[info[4] ^ d] = piece[...].astype(F4)


def place_call(info, pieces):
    out = pl.pallas_call(
        place_kernel,
        out_shape=jax.ShapeDtypeStruct((8, HEADS, SUB, HD), F4),
        in_specs=[SM] + [VM] * 8,
        out_specs=VM,
        compiler_params=pltpu.CompilerParams(vmem_limit_bytes=8 * 2**20),
        name="place",
    )(info, *pieces)
    return out.reshape(8 * HEADS, SUB, HD)


def across(block, same_z):
    pairs = []
    for z in range(2):
        for p in range(2):
            for c in range(2):
                to = z if same_z else 1 - z
                pairs.append((4 * z + 2 * p + c, 4 * to + 2 * c + p))
    return lax.ppermute(block, ("zl", "yp", "core"), pairs)


def shift_x(block, by):
    return lax.ppermute(block, "x", [((i + by) % 4, i) for i in range(4)])


def spread_column(blocks):
    got = [blocks[0]]
    for d in range(1, 8):
        flip = (d & 1) << 2 | d & 2 | d >> 2
        got.append(lax.ppermute(blocks[d], ("zl", "yp", "zh"), [(i, i ^ flip) for i in range(8)]))
    return got


def reduce_half(blocks):
    return jnp.sum(lax.all_to_all(blocks, PLANE, 0, 0, tiled=True).astype(F4), axis=0)


def shards(query, key_new, value_new, key_old, value_old, offset, windows, grad_out):
    zl, yh, yp, xx, core = (lax.axis_index(a) for a in ("zl", "yh", "yp", "x", "core"))

    wins = lax.ppermute(windows, ("yp", "core"), [(0, 0), (1, 2), (2, 1), (3, 3)])
    win = jnp.where(zl == 0, wins[0], wins[1])

    def rows_of(a):
        return jnp.swapaxes(a, 0, 1).reshape(8, 1, HEADS, SUB, HD)

    qd = jnp.concatenate([rows_of(query), rows_of(grad_out)], axis=1)
    qd = lax.all_to_all(qd, COLUMN, 0, 0, tiled=True).reshape(2, 2, 2, 2, HEADS, SUB, HD)

    kv = jnp.stack([jnp.stack([key_new, value_new]), jnp.stack([key_old, value_old])])
    kv = jnp.moveaxis(kv, 3, 0)
    same = across(jnp.where(zl == 0, kv[0], kv[1]), True)
    other = across(jnp.where(zl == 0, kv[1], kv[0]), False)
    same, other, win = lax.optimization_barrier((same, other, win))
    z0 = jnp.where(zl == 0, same, other)
    z1 = jnp.where(zl == 0, other, same)
    slot = (8 * yh + 4 * core + xx) * TOK + jnp.arange(TOK, dtype=jnp.int32)
    upper = (((slot - offset[0]) & (2 * HALF - 1)) >= HALF)[None, :, None]
    old_hi = jnp.where(upper, z0[1], z1[1])
    old_lo = jnp.where(upper, z1[1], z0[1])
    block = jnp.stack([jnp.stack([z0[0], old_lo]), jnp.stack([z1[0], old_hi])])
    far = lax.ppermute(block, "yh", [(0, 1), (1, 0)])
    pair = jnp.stack([jnp.where(yh == 0, block, far), jnp.where(yh == 0, far, block)])
    parts = jnp.stack([pair] + [shift_x(pair, d) for d in (1, 2, 3)])
    own = jnp.stack([lax.dynamic_index_in_dim(parts, (j - xx) & 3, 0, keepdims=False) for j in range(4)], axis=1)
    own = own.reshape(8, *block.shape)
    own, qd = lax.optimization_barrier((own, qd))
    other = lax.ppermute(own, "core", [(0, 1), (1, 0)])

    rank = 4 * lax.axis_index("zh") + 2 * yp + zl
    info = jnp.stack([offset[0], win, 8 * yh + xx, core, rank]).astype(jnp.int32)

    stats = stats_call(info, qd, own, other)
    dq_part, blocks_hi = grads_call(1, False, info, qd, stats, own, other)
    sum_hi = reduce_half(blocks_hi)
    dq, blocks_lo = grads_call(0, True, info, qd, stats, own, other, dq_part)
    dq, sum_hi = lax.optimization_barrier((dq, sum_hi))
    sum_lo = reduce_half(blocks_lo)

    got = spread_column(dq)
    *ready, sum_lo = lax.optimization_barrier((*got[:6], sum_lo))
    grad_query = jnp.swapaxes(place_call(info, [*ready, *got[6:]]), 0, 1)

    r0 = jnp.stack([sum_lo[0], jnp.where(upper, sum_hi[1], sum_lo[1])]).astype(BF)
    r1 = jnp.stack([sum_hi[0], jnp.where(upper, sum_lo[1], sum_hi[1])]).astype(BF)
    same = across(jnp.where(zl == 0, r0, r1), True).astype(F4)
    other = across(jnp.where(zl == 0, r1, r0), False).astype(F4)
    both = jnp.stack([jnp.where(zl == 0, same, other), jnp.where(zl == 0, other, same)], axis=3)
    return (grad_query, both[0, 0], both[0, 1], both[1, 0], both[1, 1])


def solution(mesh):
    fine = Mesh(mesh.devices.reshape(2, 2, 2, 4, 2, 2), ALL)
    tokens = P(ALL, None, None)
    slots = P(("zl", "yh", "yp", "x"), ("zh", "core"), None)
    return jax.shard_map(
        shards,
        mesh=fine,
        in_specs=(tokens, slots, slots, slots, slots, P(), P(("zh", "core")), tokens),
        out_specs=(tokens, slots, slots, slots, slots),
        check_vma=False,
    )
```

time: 256 us -> 205 us (0.80); the launches traced: 251 us -> 205 us
  blocking collectives: 61.6 us -> 0 us
  waiting for transfers between devices: 79.6 us -> 55.1 us
  starting transfers between devices: 29 us -> 52.2 us
  Pallas kernels: 62.9 us -> 76.5 us
  other arithmetic: 2.92 us -> 6.21 us
    all_to_all x2 -> x0, blocking collectives: 61.6 us -> none  [reduce_half(): lax.all_to_all(blocks, ('y', 'x'), 0, 0, tiled=True).astype(F4)]
    all_to_all x3 -> x2, waiting for transfers between devices: 55.1 us -> 24.3 us  [reduce_half(): lax.all_to_all(blocks, PLANE, 0, 0, tiled=True).astype(F4)]
    ppermute x2 -> x17, waiting for transfers between devices: 2.83 us -> 30.8 us  [the longest x3 21.1 us: shift_x(): return lax.ppermute(block, 'x', [((i + by) % 4, i) for i in range(4)])]
    ppermute x2 -> x17, starting transfers between devices: 4.18 us -> 32 us  [the longest x7 18.7 us: spread_column(): lax.ppermute(blocks[d], ('zl', 'yp', 'zh'), [(i, i ^ flip) for i in range...]
    all_to_all x1, waiting for transfers between devices: 21.6 us -> 0.01 us  [shards(): lax.all_to_all(qd, COLUMN, 0, 0, tiled=True)]
    all_to_all x3 -> x2, starting transfers between devices: 20 us -> 9.05 us  [reduce_half(): lax.all_to_all(blocks, PLANE, 0, 0, tiled=True).astype(F4)]
    pallas_call x2, Pallas kernels: 39.4 us -> 48.2 us  [grads_call(): pl.pallas_call(functools.partial(grads_kernel, half, last), out_shape=(dq...]
    all_to_all x1, starting transfers between devices: 4.84 us -> 11.1 us  [shards(): lax.all_to_all(qd, COLUMN, 0, 0, tiled=True)]
  transfers between devices with their start and end apart: 6 -> 20, of which waited for: 5 -> 7; matrix products, arithmetic and copies ran while one was open for 2% -> 6% of each run, Pallas kernels for 5% -> 12%
where the time goes in v2:
time: 205 us
  Pallas kernels  76.5 us (37%)
  waiting for transfers between devices  55.1 us (27%)
  starting transfers between devices  52.2 us (25%)
  local copies, waits for them, and re-layouts  12.2 us (6%)
  other arithmetic  6.21 us (3%)
  between operations  2.99 us (1%)
    pallas_call x2, Pallas kernels, grads_call(): pl.pallas_call(functools.partial(grads_kernel, half, last), out_shape=(dq...  48.2 us
    pallas_call x1, Pallas kernels, stats_call(): pl.pallas_call(stats_kernel, out_shape=jax.ShapeDtypeStruct((4, 2, 8, ROW...  27.6 us
    all_to_all x2, waiting for transfers between devices, reduce_half(): lax.all_to_all(blocks, PLANE, 0, 0, tiled=True).astype(F4)  24.3 us
    ppermute x3, waiting for transfers between devices, shift_x(): return lax.ppermute(block, 'x', [((i + by) % 4, i) for i in range(4)])  21.1 us
    ppermute x7, starting transfers between devices, spread_column(): lax.ppermute(blocks[d], ('zl', 'yp', 'zh'), [(i, i ^ flip) for i in range...  18.7 us
    all_to_all x1, starting transfers between devices, shards(): lax.all_to_all(qd, COLUMN, 0, 0, tiled=True)  11.1 us
    all_to_all x2, starting transfers between devices, reduce_half(): lax.all_to_all(blocks, PLANE, 0, 0, tiled=True).astype(F4)  9.05 us
    unnamed x14, local copies, waits for them, and re-layouts  5.87 us
  transfers between devices with their start and end apart: 20, of which 7 were waited for; matrix products, arithmetic and copies ran while one was open for 6% of the time, Pallas kernels for 12%

profile of v2, /device:TPU:0, one launch (start us, length us, event | category | flops | bytes accessed | tf_op | source)
XLA Modules:
  0.0 205.1 jit_solution(5211400649154754099)
XLA Ops:
  0.6 1.3 collective-permute-start.2
  1.9 1.0 copy_bitcast_fusion.3
  2.9 0.9 copy_bitcast_fusion.1
  3.9 0.0 copy-start.5
  3.9 2.1 %collective-permute-start.1 = (bf16[2,2,128,128]{3,2,1,0:T(8,128)(2,1)S(1)}, bf16[2,2,128,128]{3,2,1,0:T(8,128)(2,1)S(1)}, u32[]{:S(2)}, u32[]{:S(2)}) collective-permute-start(bf16[2,2,128,128]{3,2,1,0:T(8,128)(2,1)S(1)} %get-tuple-element.71), channel_id=1, source_target_pairs={{0,64},{1,80},{16,65},{17,81},{64,0},{65,16},{80,1},{81,17},{2,66}... | collective-permute-start | bytes 393224 | tf_op jit(solution)/shard_map/ppermute | solution.py:275
  6.0 0.7 collective-permute-start
  7.4 0.0 collective-permute-done.2
  7.4 0.6 fusion.8
  9.2 0.0 collective-permute-done.1
  9.3 0.1 broadcast_select_fusion.5
  9.5 3.3 %collective-permute-start.3 = (bf16[2,2,2,128,128]{4,3,2,1,0:T(8,128)(2,1)S(1)}, bf16[2,2,2,128,128]{4,3,2,1,0:T(8,128)(2,1)S(1)}, u32[]{:S(2)}, u32[]{:S(2)}) collective-permute-start(bf16[2,2,2,128,128]{4,3,2,1,0:T(8,128)(2,1)S(1)} %pad_maximum_fusion.4), channel_id=1, source_target_pairs={{0,32},{32,0},{1,33},{33,1},{2,34},{34,2},{3,35},{35,3},{4,36},{36... | collective-permute-start | bytes 786440 | tf_op jit(solution)/shard_map/ppermute | solution.py:318
  12.8 0.3 copy.34
  13.1 0.3 copy.35
  13.4 0.1 pad_maximum_fusion.2
  13.5 1.4 copy.36
  15.0 11.1 %all-to-all-start = ((bf16[8,2,12,32,128]{4,3,2,1,0:T(8,128)(2,1)}), bf16[8,2,12,32,128]{4,3,2,1,0:T(8,128)(2,1)}, u32[]{:S(2)}, u32[]{:S(2)}) async-start(bf16[8,2,12,32,128]{4,3,2,1,0:T(8,128)(2,1)} %copy.36), calls=%async_computation | async-start | bytes 3145728 | tf_op jit(solution)/shard_map/all_to_all | solution.py:304
  26.1 0.0 collective-permute-done.3
  26.1 0.1 fusion.7
  26.2 3.1 %collective-permute-start.5 = (bf16[2,2,2,2,128,128]{5,4,3,2,1,0:T(8,128)(2,1)S(1)}, bf16[2,2,2,2,128,128]{5,4,3,2,1,0:T(8,128)(2,1)S(1)}, u32[]{:S(2)}, u32[]{:S(2)}) collective-permute-start(bf16[2,2,2,2,128,128]{5,4,3,2,1,0:T(8,128)(2,1)S(1)} %get-tuple-element.58), channel_id=1, source_target_pairs={{8,0},{12,4},{0,8},{4,12},{9,1},{13,5},{1,9},{5,13},{10,2},{14,6},... | collective-permute-start | bytes 1572872 | tf_op jit(solution)/shard_map/ppermute | solution.py:279
  29.3 1.1 collective-permute-start.4
  30.4 0.9 collective-permute-start.6
  31.3 11.4 %collective-permute-done.5 = bf16[2,2,2,2,128,128]{5,4,3,2,1,0:T(8,128)(2,1)S(1)} collective-permute-done((bf16[2,2,2,2,128,128]{5,4,3,2,1,0:T(8,128)(2,1)S(1)}, bf16[2,2,2,2,128,128]{5,4,3,2,1,0:T(8,128)(2,1)S(1)}, u32[]{:S(2)}, u32[]{:S(2)}) %collective-permute-start.5) | collective-permute-done | bytes 524320 | tf_op jit(solution)/shard_map/ppermute | solution.py:279
  42.7 9.8 %collective-permute-done.4 = bf16[2,2,2,2,128,128]{5,4,3,2,1,0:T(8,128)(2,1)S(1)} collective-permute-done((bf16[2,2,2,2,128,128]{5,4,3,2,1,0:T(8,128)(2,1)S(1)}, bf16[2,2,2,2,128,128]{5,4,3,2,1,0:T(8,128)(2,1)S(1)}, u32[]{:S(2)}, u32[]{:S(2)}) %collective-permute-start.4) | collective-permute-done | bytes 524320 | tf_op jit(solution)/shard_map/ppermute | solution.py:279
  52.4 0.3 pad_maximum_fusion
  52.7 0.3 dynamic-slice_bitcast_fusion.3
  53.0 0.3 pad_maximum_fusion.1
  53.3 0.1 collective-permute-start.7
  53.4 0.1 stack.130.info
  53.5 4.2 %collective-permute-done.7.other = bf16[8,2,2,2,128,128]{5,4,3,2,1,0:T(8,128)(2,1)} collective-permute-done((bf16[8,2,2,2,128,128]{5,4,3,2,1,0:T(8,128)(2,1)S(1)}, bf16[8,2,2,2,128,128]{5,4,3,2,1,0:T(8,128)(2,1)}, u32[]{:S(2)}, u32[]{:S(2)}) %collective-permute-start.7) | collective-permute-done | bytes 2097184 | tf_op jit(solution)/shard_map/ppermute | solution.py:324
  57.6 27.6 %stats.1.st_ref = f32[4,2,8,768]{3,2,1,0:T(8,128)S(1)} custom-call(s32[5]{0:T(128)S(1)} %stack.130.info, bf16[2,2,2,2,12,32,128]{6,5,4,3,2,1,0:T(8,128)(2,1)} %bitcast.33.qd_ref, bf16[8,2,2,2,128,128]{5,4,3,2,1,0:T(8,128)(2,1)S(1)} %bitcast.89, bf16[8,2,2,2,128,128]{5,4,3,2,1,0:T(8,128)(2,1)} %collective-permute-done.7.other), custom_call_target="tpu_custom_call" | custom-call | flops 10380902400 | bytes 4194304 | tf_op jit(solution)/shard_map/stats/pallas_call | solution.py:210
  85.2 23.8 %grads1.1 = (f32[4,128,768]{2,1,0:T(8,128)S(1)}, bf16[16,2,2,128,128]{4,3,2,1,0:T(8,128)(2,1)S(1)}) custom-call(s32[5]{0:T(128)S(1)} %stack.130.info, bf16[2,2,2,2,12,32,128]{6,5,4,3,2,1,0:T(8,128)(2,1)} %bitcast.33.qd_ref, f32[4,2,8,768]{3,2,1,0:T(8,128)S(1)} %stats.1.st_ref, bf16[8,2,2,2,128,128]{5,4,3,2,1,0:T(8,128)(2,1)S(1)} %bitcast.90, ...), custom_call_target="tpu_custom_call" | custom-call | flops 12976128000 | bytes 8388608 | tf_op jit(solution)/shard_map/grads1/pallas_call | solution.py:232
  109.1 1.3 copy-done.1
  110.4 1.1 copy-done.2
  111.5 4.6 %all-to-all-start.1 = ((bf16[16,2,2,128,128]{4,3,2,1,0:T(8,128)(2,1)}), bf16[16,2,2,128,128]{4,3,2,1,0:T(8,128)(2,1)}, u32[]{:S(2)}, u32[]{:S(2)}) async-start(bf16[16,2,2,128,128]{4,3,2,1,0:T(8,128)(2,1)} %copy-done.1), calls=%async_computation.1 | async-start | bytes 4194304 | tf_op jit(solution)/shard_map/all_to_all | solution.py:291
  116.1 0.0 copy-start.3
  116.1 1.4 copy-done.3
  117.5 24.4 %grads0.1 = (bf16[8,12,32,128]{3,2,1,0:T(8,128)(2,1)S(1)}, bf16[16,2,2,128,128]{4,3,2,1,0:T(8,128)(2,1)S(1)}) custom-call(s32[5]{0:T(128)S(1)} %stack.130.info, bf16[2,2,2,2,12,32,128]{6,5,4,3,2,1,0:T(8,128)(2,1)} %bitcast.33.qd_ref, f32[4,2,8,768]{3,2,1,0:T(8,128)S(1)} %stats.1.st_ref, bf16[8,2,2,2,128,128]{5,4,3,2,1,0:T(8,128)(2,1)S(1)} %bitcast.91, ...), custom_call_target="tpu_custom_call" | custom-call | flops 12976128000 | bytes 8388608 | tf_op jit(solution)/shard_map/grads0/pallas_call | solution.py:232
  142.0 1.4 copy-done
  143.3 3.7 %all-to-all-done.1 = bf16[16,2,2,128,128]{4,3,2,1,0:T(8,128)(2,1)} async-done(((bf16[16,2,2,128,128]{4,3,2,1,0:T(8,128)(2,1)}), bf16[16,2,2,128,128]{4,3,2,1,0:T(8,128)(2,1)}, u32[]{:S(2)}, u32[]{:S(2)}) %all-to-all-start.1) | async-done | bytes 2097184 | tf_op jit(solution)/shard_map/all_to_all | solution.py:291
  147.0 4.4 %all-to-all-start.2 = ((bf16[16,2,2,128,128]{4,3,2,1,0:T(8,128)(2,1)}), bf16[16,2,2,128,128]{4,3,2,1,0:T(8,128)(2,1)}, u32[]{:S(2)}, u32[]{:S(2)}) async-start(bf16[16,2,2,128,128]{4,3,2,1,0:T(8,128)(2,1)} %copy-done), calls=%async_computation.2 | async-start | bytes 4194304 | tf_op jit(solution)/shard_map/all_to_all | solution.py:291
  151.5 1.9 convert_reduce_fusion.1
  153.4 0.1 slice_bitcast_fusion
  153.5 3.0 %collective-permute-start.12 = (bf16[12,32,128]{2,1,0:T(8,128)(2,1)S(1)}, bf16[12,32,128]{2,1,0:T(8,128)(2,1)S(1)}, u32[]{:S(2)}, u32[]{:S(2)}) collective-permute-start(bf16[12,32,128]{2,1,0:T(8,128)(2,1)S(1)} %get-tuple-element.47), channel_id=1, source_target_pairs={{0,66},{2,64},{16,82},{18,80},{64,2},{66,0},{80,18},{82,16},{1,67}... | collective-permute-start | bytes 294920 | tf_op jit(solution)/shard_map/ppermute | solution.py:286
  156.5 4.3 %collective-permute-start.10 = (bf16[12,32,128]{2,1,0:T(8,128)(2,1)S(1)}, bf16[12,32,128]{2,1,0:T(8,128)(2,1)S(1)}, u32[]{:S(2)}, u32[]{:S(2)}) collective-permute-start(bf16[12,32,128]{2,1,0:T(8,128)(2,1)S(1)} %get-tuple-element.49), channel_id=1, source_target_pairs={{0,80},{2,82},{16,64},{18,66},{64,16},{66,18},{80,0},{82,2},{1,81}... | collective-permute-start | bytes 294920 | tf_op jit(solution)/shard_map/ppermute | solution.py:286
  160.8 0.0 collective-permute-start.9
  160.9 1.1 collective-permute-start.8
  161.9 20.6 %all-to-all-done.2 = bf16[16,2,2,128,128]{4,3,2,1,0:T(8,128)(2,1)} async-done(((bf16[16,2,2,128,128]{4,3,2,1,0:T(8,128)(2,1)}), bf16[16,2,2,128,128]{4,3,2,1,0:T(8,128)(2,1)}, u32[]{:S(2)}, u32[]{:S(2)}) %all-to-all-start.2) | async-done | bytes 2097184 | tf_op jit(solution)/shard_map/all_to_all | solution.py:291
  182.6 1.9 convert_reduce_fusion
  184.5 0.0 collective-permute-done.12.refs_5_
  184.5 0.0 collective-permute-done.11.refs_4_
  184.5 0.0 collective-permute-done.9.refs_2_
  184.5 0.0 collective-permute-done.8.refs_1_
  184.5 0.1 select_convert_fusion.1
  184.7 0.7 collective-permute-start.15
  185.3 0.1 collective-permute-start.16
  185.4 7.7 %collective-permute-start.14 = (bf16[12,32,128]{2,1,0:T(8,128)(2,1)S(1)}, bf16[12,32,128]{2,1,0:T(8,128)(2,1)S(1)}, u32[]{:S(2)}, u32[]{:S(2)}) collective-permute-start(bf16[12,32,128]{2,1,0:T(8,128)(2,1)S(1)} %get-tuple-element.45), channel_id=1, source_target_pairs={{0,82},{2,80},{16,66},{18,64},{64,18},{66,16},{80,2},{82,0},{1,83}... | collective-permute-start | bytes 294920 | tf_op jit(solution)/shard_map/ppermute | solution.py:286
  193.1 2.5 %collective-permute-start.13 = (bf16[12,32,128]{2,1,0:T(8,128)(2,1)S(1)}, bf16[12,32,128]{2,1,0:T(8,128)(2,1)S(1)}, u32[]{:S(2)}, u32[]{:S(2)}) collective-permute-start(bf16[12,32,128]{2,1,0:T(8,128)(2,1)S(1)} %get-tuple-element.46), channel_id=1, source_target_pairs={{0,18},{2,16},{16,2},{18,0},{64,82},{66,80},{80,66},{82,64},{1,19}... | collective-permute-start | bytes 294920 | tf_op jit(solution)/shard_map/ppermute | solution.py:286
  195.7 4.9 %collective-permute-done.14.refs_7_ = bf16[12,32,128]{2,1,0:T(8,128)(2,1)S(1)} collective-permute-done((bf16[12,32,128]{2,1,0:T(8,128)(2,1)S(1)}, bf16[12,32,128]{2,1,0:T(8,128)(2,1)S(1)}, u32[]{:S(2)}, u32[]{:S(2)}) %collective-permute-start.14) | collective-permute-done | bytes 98336 | tf_op jit(solution)/shard_map/ppermute | solution.py:286
  200.6 0.6 collective-permute-done.13.refs_6_
  201.2 0.6 place.1
  201.8 2.1 %copy.44 = f32[96,32,128]{2,0,1:T(8,128)} copy(f32[96,32,128]{2,1,0:T(8,128)S(1)} %bitcast.87) | data formatting | bytes 3145728 | tf_op jit(solution)/shard_map/reshape | solution.py:265
  203.9 0.0 collective-permute-done.15
  203.9 0.0 collective-permute-done.16
  203.9 1.2 fusion.3
  (23 shorter events, 0.3 us)
Async XLA Ops:
  0.6 6.7 %collective-permute-start.2 = (s32[2]{0:T(128)}, s32[2]{0:T(128)S(1)}, u32[]{:S(2)}, u32[]{:S(2)}) collective-permute-start(s32[2]{0:T(128)} %param.14), channel_id=1, source_target_pairs={{0,0},{1,16},{16,1},{17,17},{2,2},{3,18},{18,3},{19,19},{4,4},{5,2... | collective-permute-start | bytes 32 | tf_op jit(solution)/shard_map/ppermute | solution.py:297
  1.9 10.8 %copy-start.4 = (bf16[32,96,128]{2,1,0:T(8,128)(2,1)S(1)}, bf16[32,96,128]{2,1,0:T(8,128)(2,1)}, u32[]{:S(2)}) copy-start(bf16[32,96,128]{2,1,0:T(8,128)(2,1)} %param.8) | copy-start | bytes 2359300
  3.9 9.2 %copy-start.5 = (bf16[32,96,128]{2,1,0:T(8,128)(2,1)S(1)}, bf16[32,96,128]{2,1,0:T(8,128)(2,1)}, u32[]{:S(2)}) copy-start(bf16[32,96,128]{2,1,0:T(8,128)(2,1)} %param.15) | copy-start | bytes 2359300
  3.9 5.3 %collective-permute-start.1 = (bf16[2,2,128,128]{3,2,1,0:T(8,128)(2,1)S(1)}, bf16[2,2,128,128]{3,2,1,0:T(8,128)(2,1)S(1)}, u32[]{:S(2)}, u32[]{:S(2)}) collective-permute-start(bf16[2,2,128,128]{3,2,1,0:T(8,128)(2,1)S(1)} %get-tuple-element.71), channel_id=1, source_target_pairs={{0,64},{1,80},{16,65},{17,81},{64,0},{65,16},{80,1},{81,17},{2,66}... | collective-permute-start | bytes 393224 | tf_op jit(solution)/shard_map/ppermute | solution.py:275
  6.0 3.2 %collective-permute-start = (bf16[2,2,128,128]{3,2,1,0:T(8,128)(2,1)S(1)}, bf16[2,2,128,128]{3,2,1,0:T(8,128)(2,1)S(1)}, u32[]{:S(2)}, u32[]{:S(2)}) collective-permute-start(bf16[2,2,128,128]{3,2,1,0:T(8,128)(2,1)S(1)} %get-tuple-element.72), channel_id=1, source_target_pairs={{0,0},{1,16},{16,1},{17,17},{64,64},{65,80},{80,65},{81,81},{2,2},... | collective-permute-start | bytes 393224 | tf_op jit(solution)/shard_map/ppermute | solution.py:275
  9.5 16.6 %collective-permute-start.3 = (bf16[2,2,2,128,128]{4,3,2,1,0:T(8,128)(2,1)S(1)}, bf16[2,2,2,128,128]{4,3,2,1,0:T(8,128)(2,1)S(1)}, u32[]{:S(2)}, u32[]{:S(2)}) collective-permute-start(bf16[2,2,2,128,128]{4,3,2,1,0:T(8,128)(2,1)S(1)} %pad_maximum_fusion.4), channel_id=1, source_target_pairs={{0,32},{32,0},{1,33},{33,1},{2,34},{34,2},{3,35},{35,3},{4,36},{36... | collective-permute-start | bytes 786440 | tf_op jit(solution)/shard_map/ppermute | solution.py:318
  15.0 38.3 %all-to-all-start = ((bf16[8,2,12,32,128]{4,3,2,1,0:T(8,128)(2,1)}), bf16[8,2,12,32,128]{4,3,2,1,0:T(8,128)(2,1)}, u32[]{:S(2)}, u32[]{:S(2)}) async-start(bf16[8,2,12,32,128]{4,3,2,1,0:T(8,128)(2,1)} %copy.36), calls=%async_computation | async-start | bytes 3145728 | tf_op jit(solution)/shard_map/all_to_all | solution.py:304
  26.2 16.5 %collective-permute-start.5 = (bf16[2,2,2,2,128,128]{5,4,3,2,1,0:T(8,128)(2,1)S(1)}, bf16[2,2,2,2,128,128]{5,4,3,2,1,0:T(8,128)(2,1)S(1)}, u32[]{:S(2)}, u32[]{:S(2)}) collective-permute-start(bf16[2,2,2,2,128,128]{5,4,3,2,1,0:T(8,128)(2,1)S(1)} %get-tuple-element.58), channel_id=1, source_target_pairs={{8,0},{12,4},{0,8},{4,12},{9,1},{13,5},{1,9},{5,13},{10,2},{14,6},... | collective-permute-start | bytes 1572872 | tf_op jit(solution)/shard_map/ppermute | solution.py:279
  29.3 23.1 %collective-permute-start.4 = (bf16[2,2,2,2,128,128]{5,4,3,2,1,0:T(8,128)(2,1)S(1)}, bf16[2,2,2,2,128,128]{5,4,3,2,1,0:T(8,128)(2,1)S(1)}, u32[]{:S(2)}, u32[]{:S(2)}) collective-permute-start(bf16[2,2,2,2,128,128]{5,4,3,2,1,0:T(8,128)(2,1)S(1)} %get-tuple-element.58), channel_id=1, source_target_pairs={{4,0},{8,4},{12,8},{0,12},{5,1},{9,5},{13,9},{1,13},{6,2},{10,6},{... | collective-permute-start | bytes 1572872 | tf_op jit(solution)/shard_map/ppermute | solution.py:279
  30.4 22.0 %collective-permute-start.6 = (bf16[2,2,2,2,128,128]{5,4,3,2,1,0:T(8,128)(2,1)S(1)}, bf16[2,2,2,2,128,128]{5,4,3,2,1,0:T(8,128)(2,1)S(1)}, u32[]{:S(2)}, u32[]{:S(2)}) collective-permute-start(bf16[2,2,2,2,128,128]{5,4,3,2,1,0:T(8,128)(2,1)S(1)} %get-tuple-element.58), channel_id=1, source_target_pairs={{12,0},{0,4},{4,8},{8,12},{13,1},{1,5},{5,9},{9,13},{14,2},{2,6},{... | collective-permute-start | bytes 1572872 | tf_op jit(solution)/shard_map/ppermute | solution.py:279
  53.3 4.4 %collective-permute-start.7 = (bf16[8,2,2,2,128,128]{5,4,3,2,1,0:T(8,128)(2,1)S(1)}, bf16[8,2,2,2,128,128]{5,4,3,2,1,0:T(8,128)(2,1)}, u32[]{:S(2)}, u32[]{:S(2)}) collective-permute-start(bf16[8,2,2,2,128,128]{5,4,3,2,1,0:T(8,128)(2,1)S(1)} %bitcast.88), channel_id=1, source_target_pairs={{0,1},{1,0},{2,3},{3,2},{4,5},{5,4},{6,7},{7,6},{8,9},{9,8},{10,11... | collective-permute-start | bytes 6291464 | tf_op jit(solution)/shard_map/ppermute | solution.py:324
  109.1 1.3 copy-start.1
  110.4 1.1 copy-start.2
  111.5 35.5 %all-to-all-start.1 = ((bf16[16,2,2,128,128]{4,3,2,1,0:T(8,128)(2,1)}), bf16[16,2,2,128,128]{4,3,2,1,0:T(8,128)(2,1)}, u32[]{:S(2)}, u32[]{:S(2)}) async-start(bf16[16,2,2,128,128]{4,3,2,1,0:T(8,128)(2,1)} %copy-done.1), calls=%async_computation.1 | async-start | bytes 4194304 | tf_op jit(solution)/shard_map/all_to_all | solution.py:291
  116.1 1.4 copy-start.3
  142.0 1.4 copy-start
  147.0 35.5 %all-to-all-start.2 = ((bf16[16,2,2,128,128]{4,3,2,1,0:T(8,128)(2,1)}), bf16[16,2,2,128,128]{4,3,2,1,0:T(8,128)(2,1)}, u32[]{:S(2)}, u32[]{:S(2)}) async-start(bf16[16,2,2,128,128]{4,3,2,1,0:T(8,128)(2,1)} %copy-done), calls=%async_computation.2 | async-start | bytes 4194304 | tf_op jit(solution)/shard_map/all_to_all | solution.py:291
  153.5 31.0 %collective-permute-start.12 = (bf16[12,32,128]{2,1,0:T(8,128)(2,1)S(1)}, bf16[12,32,128]{2,1,0:T(8,128)(2,1)S(1)}, u32[]{:S(2)}, u32[]{:S(2)}) collective-permute-start(bf16[12,32,128]{2,1,0:T(8,128)(2,1)S(1)} %get-tuple-element.47), channel_id=1, source_target_pairs={{0,66},{2,64},{16,82},{18,80},{64,2},{66,0},{80,18},{82,16},{1,67}... | collective-permute-start | bytes 294920 | tf_op jit(solution)/shard_map/ppermute | solution.py:286
  156.5 28.0 %collective-permute-start.11 = (bf16[12,32,128]{2,1,0:T(8,128)(2,1)S(1)}, bf16[12,32,128]{2,1,0:T(8,128)(2,1)S(1)}, u32[]{:S(2)}, u32[]{:S(2)}) collective-permute-start(bf16[12,32,128]{2,1,0:T(8,128)(2,1)S(1)} %get-tuple-element.48), channel_id=1, source_target_pairs={{0,2},{2,0},{16,18},{18,16},{64,66},{66,64},{80,82},{82,80},{1,3},... | collective-permute-start | bytes 294920 | tf_op jit(solution)/shard_map/ppermute | solution.py:286
  156.5 28.0 %collective-permute-start.10 = (bf16[12,32,128]{2,1,0:T(8,128)(2,1)S(1)}, bf16[12,32,128]{2,1,0:T(8,128)(2,1)S(1)}, u32[]{:S(2)}, u32[]{:S(2)}) collective-permute-start(bf16[12,32,128]{2,1,0:T(8,128)(2,1)S(1)} %get-tuple-element.49), channel_id=1, source_target_pairs={{0,80},{2,82},{16,64},{18,66},{64,16},{66,18},{80,0},{82,2},{1,81}... | collective-permute-start | bytes 294920 | tf_op jit(solution)/shard_map/ppermute | solution.py:286
  160.8 23.7 %collective-permute-start.9 = (bf16[12,32,128]{2,1,0:T(8,128)(2,1)S(1)}, bf16[12,32,128]{2,1,0:T(8,128)(2,1)S(1)}, u32[]{:S(2)}, u32[]{:S(2)}) collective-permute-start(bf16[12,32,128]{2,1,0:T(8,128)(2,1)S(1)} %get-tuple-element.50), channel_id=1, source_target_pairs={{0,16},{2,18},{16,0},{18,2},{64,80},{66,82},{80,64},{82,66},{1,17}... | collective-permute-start | bytes 294920 | tf_op jit(solution)/shard_map/ppermute | solution.py:286
  160.9 23.7 %collective-permute-start.8 = (bf16[12,32,128]{2,1,0:T(8,128)(2,1)S(1)}, bf16[12,32,128]{2,1,0:T(8,128)(2,1)S(1)}, u32[]{:S(2)}, u32[]{:S(2)}) collective-permute-start(bf16[12,32,128]{2,1,0:T(8,128)(2,1)S(1)} %get-tuple-element.51), channel_id=1, source_target_pairs={{0,64},{2,66},{16,80},{18,82},{64,0},{66,2},{80,16},{82,18},{1,65}... | collective-permute-start | bytes 294920 | tf_op jit(solution)/shard_map/ppermute | solution.py:286
  184.7 19.2 %collective-permute-start.15 = (bf16[2,2,128,128]{3,2,1,0:T(8,128)(2,1)S(1)}, bf16[2,2,128,128]{3,2,1,0:T(8,128)(2,1)S(1)}, u32[]{:S(2)}, u32[]{:S(2)}) collective-permute-start(bf16[2,2,128,128]{3,2,1,0:T(8,128)(2,1)S(1)} %get-tuple-element.67), channel_id=1, source_target_pairs={{0,0},{1,16},{16,1},{17,17},{64,64},{65,80},{80,65},{81,81},{2,2},... | collective-permute-start | bytes 393224 | tf_op jit(solution)/shard_map/ppermute | solution.py:275
  185.3 18.5 %collective-permute-start.16 = (bf16[2,2,128,128]{3,2,1,0:T(8,128)(2,1)S(1)}, bf16[2,2,128,128]{3,2,1,0:T(8,128)(2,1)S(1)}, u32[]{:S(2)}, u32[]{:S(2)}) collective-permute-start(bf16[2,2,128,128]{3,2,1,0:T(8,128)(2,1)S(1)} %get-tuple-element.68), channel_id=1, source_target_pairs={{0,64},{1,80},{16,65},{17,81},{64,0},{65,16},{80,1},{81,17},{2,66}... | collective-permute-start | bytes 393224 | tf_op jit(solution)/shard_map/ppermute | solution.py:275
  185.4 15.1 %collective-permute-start.14 = (bf16[12,32,128]{2,1,0:T(8,128)(2,1)S(1)}, bf16[12,32,128]{2,1,0:T(8,128)(2,1)S(1)}, u32[]{:S(2)}, u32[]{:S(2)}) collective-permute-start(bf16[12,32,128]{2,1,0:T(8,128)(2,1)S(1)} %get-tuple-element.45), channel_id=1, source_target_pairs={{0,82},{2,80},{16,66},{18,64},{64,18},{66,16},{80,2},{82,0},{1,83}... | collective-permute-start | bytes 294920 | tf_op jit(solution)/shard_map/ppermute | solution.py:286
  193.1 8.0 %collective-permute-start.13 = (bf16[12,32,128]{2,1,0:T(8,128)(2,1)S(1)}, bf16[12,32,128]{2,1,0:T(8,128)(2,1)S(1)}, u32[]{:S(2)}, u32[]{:S(2)}) collective-permute-start(bf16[12,32,128]{2,1,0:T(8,128)(2,1)S(1)} %get-tuple-element.46), channel_id=1, source_target_pairs={{0,18},{2,16},{16,2},{18,0},{64,82},{66,80},{80,66},{82,64},{1,19}... | collective-permute-start | bytes 294920 | tf_op jit(solution)/shard_map/ppermute | solution.py:286

commit v3 on v2

--- a/solution.py
+++ b/solution.py
@@ -140,7 +140,7 @@
 def grads_kernel(half, last, info, qd_ref, st_ref, own, other, *refs):
     if last:
         prev, refs = refs[0], refs[1:]
-    dq_ref, out_ref, q_s, do_s, kv_s, sem, dqt_s, acc = refs
+    dq_ref, *out_refs, q_s, do_s, kv_s, sem, dqt_s, acc = refs
     fetch((own.at[:, half], other.at[:, half]), kv_s, sem)
 
     def zero(i, _):
@@ -192,11 +192,16 @@
         return 0
 
     lax.fori_loop(0, 4, per_run, 0)
-    for ya in range(4):
+    for i in range(4):
         for seg in range(2):
-            cols = pl.ds(4 * ya, 4)
-            out_ref[cols, seg, 0] = (acc[ya, seg, 0] * SCALE).astype(BF).reshape(4, TOK, HD)
-            out_ref[cols, seg, 1] = acc[ya, seg, 1].astype(BF).reshape(4, TOK, HD)
+            if last:
+                out_ref, cols = out_refs[i % 2], pl.ds(4 * (i // 2), 4)
+                ya = 2 * (i // 2) + ((i % 2) ^ info[3])
+            else:
+                out_ref, cols, ya = out_refs[0], pl.ds(4 * i, 4), i
+            keys, values = acc[ya, seg, 0] * SCALE, acc[ya, seg, 1]
+            out_ref[cols, seg, 0] = keys.astype(out_ref.dtype).reshape(4, TOK, HD)
+            out_ref[cols, seg, 1] = values.astype(out_ref.dtype).reshape(4, TOK, HD)
 
 
 VM = pl.BlockSpec(memory_space=pltpu.VMEM)
@@ -229,11 +234,16 @@
         if last
         else jax.ShapeDtypeStruct((4, HD, ROWS), F4)
     )
+    sums = (
+        [jax.ShapeDtypeStruct((8, 2, 2, TOK, HD), F4)] * 2
+        if last
+        else [jax.ShapeDtypeStruct((16, 2, 2, TOK, HD), BF)]
+    )
     return pl.pallas_call(
         functools.partial(grads_kernel, half, last),
-        out_shape=(dq_shape, jax.ShapeDtypeStruct((16, 2, 2, TOK, HD), BF)),
+        out_shape=(dq_shape, *sums),
         in_specs=[SM, VM, VM, ANY, ANY] + ([VM] if last else []),
-        out_specs=(VM, VM),
+        out_specs=(VM,) * (1 + len(sums)),
         scratch_shapes=[
             *ROW_SCRATCH,
             pltpu.VMEM((2, 8, 2, 2, TOK, HD), BF),
@@ -280,11 +290,11 @@
 
 
 def spread_column(blocks):
-    got = [blocks[0]]
-    for d in range(1, 8):
+    def swap(d, block):
         flip = (d & 1) << 2 | d & 2 | d >> 2
-        got.append(lax.ppermute(blocks[d], ("zl", "yp", "zh"), [(i, i ^ flip) for i in range(8)]))
-    return got
+        return lax.ppermute(block, ("zl", "yp", "zh"), [(i, i ^ flip) for i in range(8)])
+
+    return [blocks[0]] + [swap(d, blocks[d]) for d in range(1, 8)]
 
 
 def reduce_half(blocks):
@@ -329,13 +339,15 @@
     stats = stats_call(info, qd, own, other)
     dq_part, blocks_hi = grads_call(1, False, info, qd, stats, own, other)
     sum_hi = reduce_half(blocks_hi)
-    dq, blocks_lo = grads_call(0, True, info, qd, stats, own, other, dq_part)
-    dq, sum_hi = lax.optimization_barrier((dq, sum_hi))
-    sum_lo = reduce_half(blocks_lo)
-
+    dq, share, others = grads_call(0, True, info, qd, stats, own, other, dq_part)
+    others, sum_hi = lax.optimization_barrier((others, sum_hi))
+    share = (share + lax.ppermute(others, "core", [(0, 1), (1, 0)])).astype(BF)
     got = spread_column(dq)
-    *ready, sum_lo = lax.optimization_barrier((*got[:6], sum_lo))
-    grad_query = jnp.swapaxes(place_call(info, [*ready, *got[6:]]), 0, 1)
+    *some, share = lax.optimization_barrier((*got[1:5], share))
+    got[1:5] = some
+    sum_lo = jnp.sum(lax.all_to_all(share, ("yh", "x"), 0, 0, tiled=True).astype(F4), axis=0)
+
+    grad_query = jnp.swapaxes(place_call(info, got), 0, 1)
 
     r0 = jnp.stack([sum_lo[0], jnp.where(upper, sum_hi[1], sum_lo[1])]).astype(BF)
     r1 = jnp.stack([sum_hi[0], jnp.where(upper, sum_lo[1], sum_hi[1])]).astype(BF)

time: 205 us -> 209 us (1.020)
  blocking collectives: 0 us -> 23.2 us
  Pallas kernels: 76.5 us -> 58.7 us
  waiting for transfers between devices: 55.1 us -> 45.7 us
  starting transfers between devices: 52.2 us -> 58 us
    all_to_all x0 -> x1, blocking collectives: none -> 23.2 us  [shards(): lax.all_to_all(share, ('yh', 'x'), 0, 0, tiled=True).astype(F4)]
    all_to_all x2 -> x1, waiting for transfers between devices: 24.3 us -> 7.83 us  [reduce_half(): lax.all_to_all(blocks, PLANE, 0, 0, tiled=True).astype(F4)]
    pallas_call x2, Pallas kernels: 48.2 us -> 37.1 us  [grads_call(): pl.pallas_call(functools.partial(grads_kernel, half, last), out_shape=(dq...]
    ppermute x7 -> x8, starting transfers between devices: 18.7 us -> 26.7 us  [the longest x7 26.6 us: swap(): lax.ppermute(block, ('zl', 'yp', 'zh'), [(i, i ^ flip) for i in range(8)])]
    ppermute x7 -> x8, waiting for transfers between devices: 5.51 us -> 12.6 us  [the longest x7 12.6 us: swap(): lax.ppermute(block, ('zl', 'yp', 'zh'), [(i, i ^ flip) for i in range(8)])]
    pallas_call x1, Pallas kernels: 27.6 us -> 20.9 us  [stats_call(): pl.pallas_call(stats_kernel, out_shape=jax.ShapeDtypeStruct((4, 2, 8, ROW...]
    all_to_all x2 -> x1, starting transfers between devices: 9.05 us -> 4.62 us  [reduce_half(): lax.all_to_all(blocks, PLANE, 0, 0, tiled=True).astype(F4)]
    ppermute x4, starting transfers between devices: 3.49 us -> 5.7 us  [across(): return lax.ppermute(block, ('zl', 'yp', 'core'), pairs)]
  transfers between devices with their start and end apart: 20 -> 20, of which waited for: 7 -> 9; matrix products, arithmetic and copies ran while one was open for 6% -> 4% of each run, Pallas kernels for 12% -> 9%
where the time goes in v3:
time: 209 us; the launch traced here: 207 us
  Pallas kernels  58.7 us (28%)
  starting transfers between devices  58 us (28%)
  waiting for transfers between devices  45.7 us (22%)
  blocking collectives  23.2 us (11%)
  local copies, waits for them, and re-layouts  13.6 us (7%)
  other arithmetic  4.92 us (2%)
  between operations  2.97 us (1%)
    pallas_call x2, Pallas kernels, grads_call(): pl.pallas_call(functools.partial(grads_kernel, half, last), out_shape=(dq...  37.1 us
    ppermute x7, starting transfers between devices, swap(): lax.ppermute(block, ('zl', 'yp', 'zh'), [(i, i ^ flip) for i in range(8)])  26.6 us
    all_to_all x1, blocking collectives, shards(): lax.all_to_all(share, ('yh', 'x'), 0, 0, tiled=True).astype(F4)  23.2 us
    ppermute x3, waiting for transfers between devices, shift_x(): return lax.ppermute(block, 'x', [((i + by) % 4, i) for i in range(4)])  21.1 us
    pallas_call x1, Pallas kernels, stats_call(): pl.pallas_call(stats_kernel, out_shape=jax.ShapeDtypeStruct((4, 2, 8, ROW...  20.9 us
    ppermute x7, waiting for transfers between devices, swap(): lax.ppermute(block, ('zl', 'yp', 'zh'), [(i, i ^ flip) for i in range(8)])  12.6 us
    all_to_all x1, starting transfers between devices, shards(): lax.all_to_all(qd, COLUMN, 0, 0, tiled=True)  11.1 us
    all_to_all x1, waiting for transfers between devices, reduce_half(): lax.all_to_all(blocks, PLANE, 0, 0, tiled=True).astype(F4)  7.83 us
  transfers between devices with their start and end apart: 20, of which 9 were waited for; matrix products, arithmetic and copies ran while one was open for 4% of the time, Pallas kernels for 9%

profile of v3, /device:TPU:0, one launch (start us, length us, event | category | flops | bytes accessed | tf_op | source)
XLA Modules:
  0.0 207.1 jit_solution(3447891603902496842)
XLA Ops:
  0.6 1.3 collective-permute-start.2
  1.9 1.0 copy_bitcast_fusion.3
  2.9 0.9 copy_bitcast_fusion.1
  3.9 0.0 copy-start.7
  3.9 2.1 %collective-permute-start.1 = (bf16[2,2,128,128]{3,2,1,0:T(8,128)(2,1)S(1)}, bf16[2,2,128,128]{3,2,1,0:T(8,128)(2,1)S(1)}, u32[]{:S(2)}, u32[]{:S(2)}) collective-permute-start(bf16[2,2,128,128]{3,2,1,0:T(8,128)(2,1)S(1)} %get-tuple-element.69), channel_id=1, source_target_pairs={{0,64},{1,80},{16,65},{17,81},{64,0},{65,16},{80,1},{81,17},{2,66}... | collective-permute-start | bytes 393224 | tf_op jit(solution)/shard_map/ppermute | solution.py:285
  6.0 0.7 collective-permute-start
  7.4 0.0 collective-permute-done.2
  7.4 0.6 fusion.8
  9.3 0.1 broadcast_select_fusion.5
  9.5 3.3 %collective-permute-start.3 = (bf16[2,2,2,128,128]{4,3,2,1,0:T(8,128)(2,1)S(1)}, bf16[2,2,2,128,128]{4,3,2,1,0:T(8,128)(2,1)S(1)}, u32[]{:S(2)}, u32[]{:S(2)}) collective-permute-start(bf16[2,2,2,128,128]{4,3,2,1,0:T(8,128)(2,1)S(1)} %pad_maximum_fusion.4), channel_id=1, source_target_pairs={{0,32},{32,0},{1,33},{33,1},{2,34},{34,2},{3,35},{35,3},{4,36},{36... | collective-permute-start | bytes 786440 | tf_op jit(solution)/shard_map/ppermute | solution.py:328
  12.8 0.3 copy.34
  13.1 0.3 copy.35
  13.4 0.1 pad_maximum_fusion.2
  13.5 1.4 copy.36
  15.0 11.1 %all-to-all-start = ((bf16[8,2,12,32,128]{4,3,2,1,0:T(8,128)(2,1)}), bf16[8,2,12,32,128]{4,3,2,1,0:T(8,128)(2,1)}, u32[]{:S(2)}, u32[]{:S(2)}) async-start(bf16[8,2,12,32,128]{4,3,2,1,0:T(8,128)(2,1)} %copy.36), calls=%async_computation | async-start | bytes 3145728 | tf_op jit(solution)/shard_map/all_to_all | solution.py:314
  26.1 0.0 collective-permute-done.3
  26.1 0.1 fusion.7
  26.2 3.1 %collective-permute-start.5 = (bf16[2,2,2,2,128,128]{5,4,3,2,1,0:T(8,128)(2,1)S(1)}, bf16[2,2,2,2,128,128]{5,4,3,2,1,0:T(8,128)(2,1)S(1)}, u32[]{:S(2)}, u32[]{:S(2)}) collective-permute-start(bf16[2,2,2,2,128,128]{5,4,3,2,1,0:T(8,128)(2,1)S(1)} %get-tuple-element.56), channel_id=1, source_target_pairs={{8,0},{12,4},{0,8},{4,12},{9,1},{13,5},{1,9},{5,13},{10,2},{14,6},... | collective-permute-start | bytes 1572872 | tf_op jit(solution)/shard_map/ppermute | solution.py:289
  29.3 1.1 collective-permute-start.4
  30.4 0.9 collective-permute-start.6
  31.3 11.4 %collective-permute-done.5 = bf16[2,2,2,2,128,128]{5,4,3,2,1,0:T(8,128)(2,1)S(1)} collective-permute-done((bf16[2,2,2,2,128,128]{5,4,3,2,1,0:T(8,128)(2,1)S(1)}, bf16[2,2,2,2,128,128]{5,4,3,2,1,0:T(8,128)(2,1)S(1)}, u32[]{:S(2)}, u32[]{:S(2)}) %collective-permute-start.5) | collective-permute-done | bytes 524320 | tf_op jit(solution)/shard_map/ppermute | solution.py:289
  42.7 9.8 %collective-permute-done.4 = bf16[2,2,2,2,128,128]{5,4,3,2,1,0:T(8,128)(2,1)S(1)} collective-permute-done((bf16[2,2,2,2,128,128]{5,4,3,2,1,0:T(8,128)(2,1)S(1)}, bf16[2,2,2,2,128,128]{5,4,3,2,1,0:T(8,128)(2,1)S(1)}, u32[]{:S(2)}, u32[]{:S(2)}) %collective-permute-start.4) | collective-permute-done | bytes 524320 | tf_op jit(solution)/shard_map/ppermute | solution.py:289
  52.4 0.0 collective-permute-done.6
  52.4 0.3 pad_maximum_fusion
  52.7 0.3 dynamic-slice_bitcast_fusion.3
  53.0 0.3 pad_maximum_fusion.1
  53.3 0.1 collective-permute-start.7
  53.4 0.1 stack.130.info
  53.5 4.2 %collective-permute-done.7.other = bf16[8,2,2,2,128,128]{5,4,3,2,1,0:T(8,128)(2,1)} collective-permute-done((bf16[8,2,2,2,128,128]{5,4,3,2,1,0:T(8,128)(2,1)S(1)}, bf16[8,2,2,2,128,128]{5,4,3,2,1,0:T(8,128)(2,1)}, u32[]{:S(2)}, u32[]{:S(2)}) %collective-permute-start.7) | collective-permute-done | bytes 2097184 | tf_op jit(solution)/shard_map/ppermute | solution.py:334
  57.6 20.9 %stats.1.st_ref = f32[4,2,8,768]{3,2,1,0:T(8,128)S(1)} custom-call(s32[5]{0:T(128)S(1)} %stack.130.info, bf16[2,2,2,2,12,32,128]{6,5,4,3,2,1,0:T(8,128)(2,1)} %bitcast.33.qd_ref, bf16[8,2,2,2,128,128]{5,4,3,2,1,0:T(8,128)(2,1)S(1)} %bitcast.89, bf16[8,2,2,2,128,128]{5,4,3,2,1,0:T(8,128)(2,1)} %collective-permute-done.7.other), custom_call_target="tpu_custom_call" | custom-call | flops 10380902400 | bytes 4194304 | tf_op jit(solution)/shard_map/stats/pallas_call | solution.py:215
  78.6 18.2 %grads1.1 = (f32[4,128,768]{2,1,0:T(8,128)S(1)}, bf16[16,2,2,128,128]{4,3,2,1,0:T(8,128)(2,1)S(1)}) custom-call(s32[5]{0:T(128)S(1)} %stack.130.info, bf16[2,2,2,2,12,32,128]{6,5,4,3,2,1,0:T(8,128)(2,1)} %bitcast.33.qd_ref, f32[4,2,8,768]{3,2,1,0:T(8,128)S(1)} %stats.1.st_ref, bf16[8,2,2,2,128,128]{5,4,3,2,1,0:T(8,128)(2,1)S(1)} %bitcast.90, ...), custom_call_target="tpu_custom_call" | custom-call | flops 12976128000 | bytes 8388608 | tf_op jit(solution)/shard_map/grads1/pallas_call | solution.py:242
  96.8 1.3 copy-done.2
  98.1 1.1 copy-done.4
  99.3 4.6 %all-to-all-start.1 = ((bf16[16,2,2,128,128]{4,3,2,1,0:T(8,128)(2,1)}), bf16[16,2,2,128,128]{4,3,2,1,0:T(8,128)(2,1)}, u32[]{:S(2)}, u32[]{:S(2)}) async-start(bf16[16,2,2,128,128]{4,3,2,1,0:T(8,128)(2,1)} %copy-done.2), calls=%async_computation.1 | async-start | bytes 4194304 | tf_op jit(solution)/shard_map/all_to_all | solution.py:301
  103.9 0.0 copy-start.5
  103.9 1.4 copy-done.5
  105.3 18.9 %grads0.1 = (bf16[8,12,32,128]{3,2,1,0:T(8,128)(2,1)S(1)}, f32[8,2,2,128,128]{4,3,2,1,0:T(8,128)S(1)}, f32[8,2,2,128,128]{4,3,2,1,0:T(8,128)S(1)}) custom-call(s32[5]{0:T(128)S(1)} %stack.130.info, bf16[2,2,2,2,12,32,128]{6,5,4,3,2,1,0:T(8,128)(2,1)} %bitcast.33.qd_ref, f32[4,2,8,768]{3,2,1,0:T(8,128)S(1)} %stats.1.st_ref, ...), custom_call_target="tpu_custom_call" | custom-call | flops 12976128000 | bytes 8388608 | tf_op jit(solution)/shard_map/grads0/pallas_call | solution.py:242
  124.2 1.4 copy-done
  125.6 1.4 copy-done.3
  127.0 7.8 %all-to-all-done.1 = bf16[16,2,2,128,128]{4,3,2,1,0:T(8,128)(2,1)} async-done(((bf16[16,2,2,128,128]{4,3,2,1,0:T(8,128)(2,1)}), bf16[16,2,2,128,128]{4,3,2,1,0:T(8,128)(2,1)}, u32[]{:S(2)}, u32[]{:S(2)}) %all-to-all-start.1) | async-done | bytes 2097184 | tf_op jit(solution)/shard_map/all_to_all | solution.py:301
  134.8 2.1 convert_reduce_fusion
  136.9 0.1 collective-permute-start.12
  137.0 0.1 slice_bitcast_fusion
  137.1 0.1 collective-permute-start.11
  137.1 19.4 %collective-permute-start.10 = (bf16[12,32,128]{2,1,0:T(8,128)(2,1)S(1)}, bf16[12,32,128]{2,1,0:T(8,128)(2,1)S(1)}, u32[]{:S(2)}, u32[]{:S(2)}) collective-permute-start(bf16[12,32,128]{2,1,0:T(8,128)(2,1)S(1)} %get-tuple-element.47), channel_id=1, source_target_pairs={{0,80},{2,82},{16,64},{18,66},{64,16},{66,18},{80,0},{82,2},{1,81}... | collective-permute-start | bytes 294920 | tf_op jit(solution)/shard_map/ppermute | solution.py:295
  156.6 2.7 %collective-permute-start.9 = (bf16[12,32,128]{2,1,0:T(8,128)(2,1)S(1)}, bf16[12,32,128]{2,1,0:T(8,128)(2,1)S(1)}, u32[]{:S(2)}, u32[]{:S(2)}) collective-permute-start(bf16[12,32,128]{2,1,0:T(8,128)(2,1)S(1)} %get-tuple-element.48), channel_id=1, source_target_pairs={{0,16},{2,18},{16,0},{18,2},{64,80},{66,82},{80,64},{82,66},{1,17}... | collective-permute-start | bytes 294920 | tf_op jit(solution)/shard_map/ppermute | solution.py:295
  159.3 0.0 collective-permute-start.8
  159.3 0.0 collective-permute-done.12
  159.3 0.3 add_convert_fusion
  159.6 0.2 collective-permute-done.10.refs_3_
  159.8 4.4 %collective-permute-done.9.refs_2_ = bf16[12,32,128]{2,1,0:T(8,128)(2,1)S(1)} collective-permute-done((bf16[12,32,128]{2,1,0:T(8,128)(2,1)S(1)}, bf16[12,32,128]{2,1,0:T(8,128)(2,1)S(1)}, u32[]{:S(2)}, u32[]{:S(2)}) %collective-permute-start.9) | collective-permute-done | bytes 98336 | tf_op jit(solution)/shard_map/ppermute | solution.py:295
  164.3 23.2 %all_to_all.15 = bf16[8,2,2,128,128]{4,3,2,1,0:T(8,128)(2,1)S(1)} all-to-all(bf16[8,2,2,128,128]{4,3,2,1,0:T(8,128)(2,1)S(1)} %add_convert_fusion), channel_id=1, replica_groups=mesh['zl'=2,'yh'=2,'yp'=2,'x'=4,'zh'=2,'core'=2] {'yh','x'}, dimensions={0} | all-to-all | bytes 2097152 | tf_op jit(solution)/shard_map/all_to_all | solution.py:348
  187.5 0.1 convert_reduce_fusion.1
  187.7 0.1 select_convert_fusion.1
  187.8 0.7 collective-permute-start.16
  188.5 2.3 %collective-permute-start.17 = (bf16[2,2,128,128]{3,2,1,0:T(8,128)(2,1)S(1)}, bf16[2,2,128,128]{3,2,1,0:T(8,128)(2,1)S(1)}, u32[]{:S(2)}, u32[]{:S(2)}) collective-permute-start(bf16[2,2,128,128]{3,2,1,0:T(8,128)(2,1)S(1)} %get-tuple-element.66), channel_id=1, source_target_pairs={{0,64},{1,80},{16,65},{17,81},{64,0},{65,16},{80,1},{81,17},{2,66}... | collective-permute-start | bytes 393224 | tf_op jit(solution)/shard_map/ppermute | solution.py:285
  190.8 3.3 %collective-permute-start.15 = (bf16[12,32,128]{2,1,0:T(8,128)(2,1)S(1)}, bf16[12,32,128]{2,1,0:T(8,128)(2,1)S(1)}, u32[]{:S(2)}, u32[]{:S(2)}) collective-permute-start(bf16[12,32,128]{2,1,0:T(8,128)(2,1)S(1)} %get-tuple-element.43), channel_id=1, source_target_pairs={{0,82},{2,80},{16,66},{18,64},{64,18},{66,16},{80,2},{82,0},{1,83}... | collective-permute-start | bytes 294920 | tf_op jit(solution)/shard_map/ppermute | solution.py:295
  194.0 1.1 collective-permute-start.13
  195.2 4.9 %collective-permute-done.15.refs_7_ = bf16[12,32,128]{2,1,0:T(8,128)(2,1)S(1)} collective-permute-done((bf16[12,32,128]{2,1,0:T(8,128)(2,1)S(1)}, bf16[12,32,128]{2,1,0:T(8,128)(2,1)S(1)}, u32[]{:S(2)}, u32[]{:S(2)}) %collective-permute-start.15) | collective-permute-done | bytes 98336 | tf_op jit(solution)/shard_map/ppermute | solution.py:295
  200.1 1.1 collective-permute-done.14.refs_6_
  201.1 2.0 collective-permute-done.13.refs_5_
  203.1 0.6 place.1
  203.8 2.1 copy.44
  205.9 1.2 fusion.3
  (29 shorter events, 0.3 us)
Async XLA Ops:
  0.6 6.7 %collective-permute-start.2 = (s32[2]{0:T(128)}, s32[2]{0:T(128)S(1)}, u32[]{:S(2)}, u32[]{:S(2)}) collective-permute-start(s32[2]{0:T(128)} %param.14), channel_id=1, source_target_pairs={{0,0},{1,16},{16,1},{17,17},{2,2},{3,18},{18,3},{19,19},{4,4},{5,2... | collective-permute-start | bytes 32 | tf_op jit(solution)/shard_map/ppermute | solution.py:307
  1.9 10.8 %copy-start.6 = (bf16[32,96,128]{2,1,0:T(8,128)(2,1)S(1)}, bf16[32,96,128]{2,1,0:T(8,128)(2,1)}, u32[]{:S(2)}) copy-start(bf16[32,96,128]{2,1,0:T(8,128)(2,1)} %param.8) | copy-start | bytes 2359300
  3.9 9.2 %copy-start.7 = (bf16[32,96,128]{2,1,0:T(8,128)(2,1)S(1)}, bf16[32,96,128]{2,1,0:T(8,128)(2,1)}, u32[]{:S(2)}) copy-start(bf16[32,96,128]{2,1,0:T(8,128)(2,1)} %param.15) | copy-start | bytes 2359300
  3.9 5.3 %collective-permute-start.1 = (bf16[2,2,128,128]{3,2,1,0:T(8,128)(2,1)S(1)}, bf16[2,2,128,128]{3,2,1,0:T(8,128)(2,1)S(1)}, u32[]{:S(2)}, u32[]{:S(2)}) collective-permute-start(bf16[2,2,128,128]{3,2,1,0:T(8,128)(2,1)S(1)} %get-tuple-element.69), channel_id=1, source_target_pairs={{0,64},{1,80},{16,65},{17,81},{64,0},{65,16},{80,1},{81,17},{2,66}... | collective-permute-start | bytes 393224 | tf_op jit(solution)/shard_map/ppermute | solution.py:285
  6.0 3.2 %collective-permute-start = (bf16[2,2,128,128]{3,2,1,0:T(8,128)(2,1)S(1)}, bf16[2,2,128,128]{3,2,1,0:T(8,128)(2,1)S(1)}, u32[]{:S(2)}, u32[]{:S(2)}) collective-permute-start(bf16[2,2,128,128]{3,2,1,0:T(8,128)(2,1)S(1)} %get-tuple-element.70), channel_id=1, source_target_pairs={{0,0},{1,16},{16,1},{17,17},{64,64},{65,80},{80,65},{81,81},{2,2},... | collective-permute-start | bytes 393224 | tf_op jit(solution)/shard_map/ppermute | solution.py:285
  9.5 16.6 %collective-permute-start.3 = (bf16[2,2,2,128,128]{4,3,2,1,0:T(8,128)(2,1)S(1)}, bf16[2,2,2,128,128]{4,3,2,1,0:T(8,128)(2,1)S(1)}, u32[]{:S(2)}, u32[]{:S(2)}) collective-permute-start(bf16[2,2,2,128,128]{4,3,2,1,0:T(8,128)(2,1)S(1)} %pad_maximum_fusion.4), channel_id=1, source_target_pairs={{0,32},{32,0},{1,33},{33,1},{2,34},{34,2},{3,35},{35,3},{4,36},{36... | collective-permute-start | bytes 786440 | tf_op jit(solution)/shard_map/ppermute | solution.py:328
  15.0 38.3 %all-to-all-start = ((bf16[8,2,12,32,128]{4,3,2,1,0:T(8,128)(2,1)}), bf16[8,2,12,32,128]{4,3,2,1,0:T(8,128)(2,1)}, u32[]{:S(2)}, u32[]{:S(2)}) async-start(bf16[8,2,12,32,128]{4,3,2,1,0:T(8,128)(2,1)} %copy.36), calls=%async_computation | async-start | bytes 3145728 | tf_op jit(solution)/shard_map/all_to_all | solution.py:314
  26.2 16.5 %collective-permute-start.5 = (bf16[2,2,2,2,128,128]{5,4,3,2,1,0:T(8,128)(2,1)S(1)}, bf16[2,2,2,2,128,128]{5,4,3,2,1,0:T(8,128)(2,1)S(1)}, u32[]{:S(2)}, u32[]{:S(2)}) collective-permute-start(bf16[2,2,2,2,128,128]{5,4,3,2,1,0:T(8,128)(2,1)S(1)} %get-tuple-element.56), channel_id=1, source_target_pairs={{8,0},{12,4},{0,8},{4,12},{9,1},{13,5},{1,9},{5,13},{10,2},{14,6},... | collective-permute-start | bytes 1572872 | tf_op jit(solution)/shard_map/ppermute | solution.py:289
  29.3 23.1 %collective-permute-start.4 = (bf16[2,2,2,2,128,128]{5,4,3,2,1,0:T(8,128)(2,1)S(1)}, bf16[2,2,2,2,128,128]{5,4,3,2,1,0:T(8,128)(2,1)S(1)}, u32[]{:S(2)}, u32[]{:S(2)}) collective-permute-start(bf16[2,2,2,2,128,128]{5,4,3,2,1,0:T(8,128)(2,1)S(1)} %get-tuple-element.56), channel_id=1, source_target_pairs={{4,0},{8,4},{12,8},{0,12},{5,1},{9,5},{13,9},{1,13},{6,2},{10,6},{... | collective-permute-start | bytes 1572872 | tf_op jit(solution)/shard_map/ppermute | solution.py:289
  30.4 22.0 %collective-permute-start.6 = (bf16[2,2,2,2,128,128]{5,4,3,2,1,0:T(8,128)(2,1)S(1)}, bf16[2,2,2,2,128,128]{5,4,3,2,1,0:T(8,128)(2,1)S(1)}, u32[]{:S(2)}, u32[]{:S(2)}) collective-permute-start(bf16[2,2,2,2,128,128]{5,4,3,2,1,0:T(8,128)(2,1)S(1)} %get-tuple-element.56), channel_id=1, source_target_pairs={{12,0},{0,4},{4,8},{8,12},{13,1},{1,5},{5,9},{9,13},{14,2},{2,6},{... | collective-permute-start | bytes 1572872 | tf_op jit(solution)/shard_map/ppermute | solution.py:289
  53.3 4.4 %collective-permute-start.7 = (bf16[8,2,2,2,128,128]{5,4,3,2,1,0:T(8,128)(2,1)S(1)}, bf16[8,2,2,2,128,128]{5,4,3,2,1,0:T(8,128)(2,1)}, u32[]{:S(2)}, u32[]{:S(2)}) collective-permute-start(bf16[8,2,2,2,128,128]{5,4,3,2,1,0:T(8,128)(2,1)S(1)} %bitcast.88), channel_id=1, source_target_pairs={{0,1},{1,0},{2,3},{3,2},{4,5},{5,4},{6,7},{7,6},{8,9},{9,8},{10,11... | collective-permute-start | bytes 6291464 | tf_op jit(solution)/shard_map/ppermute | solution.py:334
  96.8 1.3 copy-start.2
  98.1 1.1 copy-start.4
  99.3 35.5 %all-to-all-start.1 = ((bf16[16,2,2,128,128]{4,3,2,1,0:T(8,128)(2,1)}), bf16[16,2,2,128,128]{4,3,2,1,0:T(8,128)(2,1)}, u32[]{:S(2)}, u32[]{:S(2)}) async-start(bf16[16,2,2,128,128]{4,3,2,1,0:T(8,128)(2,1)} %copy-done.2), calls=%async_computation.1 | async-start | bytes 4194304 | tf_op jit(solution)/shard_map/all_to_all | solution.py:301
  103.9 1.4 copy-start.5
  124.2 1.4 copy-start
  125.6 1.4 copy-start.3
  134.8 24.5 %copy-start.1 = (f32[8,2,2,128,128]{4,3,2,1,0:T(8,128)S(1)}, f32[8,2,2,128,128]{4,3,2,1,0:T(8,128)}, u32[]{:S(2)}) copy-start(f32[8,2,2,128,128]{4,3,2,1,0:T(8,128)} %copy-done) | copy-start | bytes 6291460
  136.9 22.4 %collective-permute-start.12 = (f32[8,2,2,128,128]{4,3,2,1,0:T(8,128)}, f32[8,2,2,128,128]{4,3,2,1,0:T(8,128)S(1)}, u32[]{:S(2)}, u32[]{:S(2)}) collective-permute-start(f32[8,2,2,128,128]{4,3,2,1,0:T(8,128)} %copy-done.3), channel_id=1, source_target_pairs={{0,1},{1,0},{2,3},{3,2},{4,5},{5,4},{6,7},{7,6},{8,9},{9,8},{10,11... | collective-permute-start | bytes 6291464 | tf_op jit(solution)/shard_map/ppermute | solution.py:344
  137.1 22.6 %collective-permute-start.11 = (bf16[12,32,128]{2,1,0:T(8,128)(2,1)S(1)}, bf16[12,32,128]{2,1,0:T(8,128)(2,1)S(1)}, u32[]{:S(2)}, u32[]{:S(2)}) collective-permute-start(bf16[12,32,128]{2,1,0:T(8,128)(2,1)S(1)} %get-tuple-element.46), channel_id=1, source_target_pairs={{0,2},{2,0},{16,18},{18,16},{64,66},{66,64},{80,82},{82,80},{1,3},... | collective-permute-start | bytes 294920 | tf_op jit(solution)/shard_map/ppermute | solution.py:295
  137.1 22.7 %collective-permute-start.10 = (bf16[12,32,128]{2,1,0:T(8,128)(2,1)S(1)}, bf16[12,32,128]{2,1,0:T(8,128)(2,1)S(1)}, u32[]{:S(2)}, u32[]{:S(2)}) collective-permute-start(bf16[12,32,128]{2,1,0:T(8,128)(2,1)S(1)} %get-tuple-element.47), channel_id=1, source_target_pairs={{0,80},{2,82},{16,64},{18,66},{64,16},{66,18},{80,0},{82,2},{1,81}... | collective-permute-start | bytes 294920 | tf_op jit(solution)/shard_map/ppermute | solution.py:295
  156.6 7.7 %collective-permute-start.9 = (bf16[12,32,128]{2,1,0:T(8,128)(2,1)S(1)}, bf16[12,32,128]{2,1,0:T(8,128)(2,1)S(1)}, u32[]{:S(2)}, u32[]{:S(2)}) collective-permute-start(bf16[12,32,128]{2,1,0:T(8,128)(2,1)S(1)} %get-tuple-element.48), channel_id=1, source_target_pairs={{0,16},{2,18},{16,0},{18,2},{64,80},{66,82},{80,64},{82,66},{1,17}... | collective-permute-start | bytes 294920 | tf_op jit(solution)/shard_map/ppermute | solution.py:295
  159.3 5.0 %collective-permute-start.8 = (bf16[12,32,128]{2,1,0:T(8,128)(2,1)S(1)}, bf16[12,32,128]{2,1,0:T(8,128)(2,1)S(1)}, u32[]{:S(2)}, u32[]{:S(2)}) collective-permute-start(bf16[12,32,128]{2,1,0:T(8,128)(2,1)S(1)} %get-tuple-element.49), channel_id=1, source_target_pairs={{0,64},{2,66},{16,80},{18,82},{64,0},{66,2},{80,16},{82,18},{1,65}... | collective-permute-start | bytes 294920 | tf_op jit(solution)/shard_map/ppermute | solution.py:295
  187.8 18.0 %collective-permute-start.16 = (bf16[2,2,128,128]{3,2,1,0:T(8,128)(2,1)S(1)}, bf16[2,2,128,128]{3,2,1,0:T(8,128)(2,1)S(1)}, u32[]{:S(2)}, u32[]{:S(2)}) collective-permute-start(bf16[2,2,128,128]{3,2,1,0:T(8,128)(2,1)S(1)} %get-tuple-element.65), channel_id=1, source_target_pairs={{0,0},{1,16},{16,1},{17,17},{64,64},{65,80},{80,65},{81,81},{2,2},... | collective-permute-start | bytes 393224 | tf_op jit(solution)/shard_map/ppermute | solution.py:285
  188.5 17.4 %collective-permute-start.17 = (bf16[2,2,128,128]{3,2,1,0:T(8,128)(2,1)S(1)}, bf16[2,2,128,128]{3,2,1,0:T(8,128)(2,1)S(1)}, u32[]{:S(2)}, u32[]{:S(2)}) collective-permute-start(bf16[2,2,128,128]{3,2,1,0:T(8,128)(2,1)S(1)} %get-tuple-element.66), channel_id=1, source_target_pairs={{0,64},{1,80},{16,65},{17,81},{64,0},{65,16},{80,1},{81,17},{2,66}... | collective-permute-start | bytes 393224 | tf_op jit(solution)/shard_map/ppermute | solution.py:285
  190.8 9.3 %collective-permute-start.15 = (bf16[12,32,128]{2,1,0:T(8,128)(2,1)S(1)}, bf16[12,32,128]{2,1,0:T(8,128)(2,1)S(1)}, u32[]{:S(2)}, u32[]{:S(2)}) collective-permute-start(bf16[12,32,128]{2,1,0:T(8,128)(2,1)S(1)} %get-tuple-element.43), channel_id=1, source_target_pairs={{0,82},{2,80},{16,66},{18,64},{64,18},{66,16},{80,2},{82,0},{1,83}... | collective-permute-start | bytes 294920 | tf_op jit(solution)/shard_map/ppermute | solution.py:295
  194.0 7.1 %collective-permute-start.14 = (bf16[12,32,128]{2,1,0:T(8,128)(2,1)S(1)}, bf16[12,32,128]{2,1,0:T(8,128)(2,1)S(1)}, u32[]{:S(2)}, u32[]{:S(2)}) collective-permute-start(bf16[12,32,128]{2,1,0:T(8,128)(2,1)S(1)} %get-tuple-element.44), channel_id=1, source_target_pairs={{0,18},{2,16},{16,2},{18,0},{64,82},{66,80},{80,66},{82,64},{1,19}... | collective-permute-start | bytes 294920 | tf_op jit(solution)/shard_map/ppermute | solution.py:295
  194.0 9.1 %collective-permute-start.13 = (bf16[12,32,128]{2,1,0:T(8,128)(2,1)S(1)}, bf16[12,32,128]{2,1,0:T(8,128)(2,1)S(1)}, u32[]{:S(2)}, u32[]{:S(2)}) collective-permute-start(bf16[12,32,128]{2,1,0:T(8,128)(2,1)S(1)} %get-tuple-element.45), channel_id=1, source_target_pairs={{0,66},{2,64},{16,82},{18,80},{64,2},{66,0},{80,18},{82,16},{1,67}... | collective-permute-start | bytes 294920 | tf_op jit(solution)/shard_map/ppermute | solution.py:295

commit v4 on v3

--- a/solution.py
+++ b/solution.py
@@ -186,7 +186,7 @@
             for j in range(HEADS):
                 for zh in range(2):
                     rows = dq[j * PART + zh * SUB : j * PART + (zh + 1) * SUB]
-                    dq_ref[info[4] ^ (4 * zh + 2 * (run % 2) + run // 2), j] = rows
+                    dq_ref[4 * zh + 2 * (run % 2) + run // 2, j] = rows
         else:
             dq_ref[run] = dqt_s[...]
         return 0
@@ -257,24 +257,6 @@
     )(*([info, qd, stats, own, other] + ([prev] if last else [])))
 
 
-def place_kernel(info, *refs):
-    *pieces, out_ref = refs
-    for d, piece in enumerate(pieces):
-        out_ref[info[4] ^ d] = piece[...].astype(F4)
-
-
-def place_call(info, pieces):
-    out = pl.pallas_call(
-        place_kernel,
-        out_shape=jax.ShapeDtypeStruct((8, HEADS, SUB, HD), F4),
-        in_specs=[SM] + [VM] * 8,
-        out_specs=VM,
-        compiler_params=pltpu.CompilerParams(vmem_limit_bytes=8 * 2**20),
-        name="place",
-    )(info, *pieces)
-    return out.reshape(8 * HEADS, SUB, HD)
-
-
 def across(block, same_z):
     pairs = []
     for z in range(2):
@@ -287,14 +269,6 @@
 
 def shift_x(block, by):
     return lax.ppermute(block, "x", [((i + by) % 4, i) for i in range(4)])
-
-
-def spread_column(blocks):
-    def swap(d, block):
-        flip = (d & 1) << 2 | d & 2 | d >> 2
-        return lax.ppermute(block, ("zl", "yp", "zh"), [(i, i ^ flip) for i in range(8)])
-
-    return [blocks[0]] + [swap(d, blocks[d]) for d in range(1, 8)]
 
 
 def reduce_half(blocks):
@@ -333,8 +307,7 @@
     own, qd = lax.optimization_barrier((own, qd))
     other = lax.ppermute(own, "core", [(0, 1), (1, 0)])
 
-    rank = 4 * lax.axis_index("zh") + 2 * yp + zl
-    info = jnp.stack([offset[0], win, 8 * yh + xx, core, rank]).astype(jnp.int32)
+    info = jnp.stack([offset[0], win, 8 * yh + xx, core]).astype(jnp.int32)
 
     stats = stats_call(info, qd, own, other)
     dq_part, blocks_hi = grads_call(1, False, info, qd, stats, own, other)
@@ -342,12 +315,11 @@
     dq, share, others = grads_call(0, True, info, qd, stats, own, other, dq_part)
     others, sum_hi = lax.optimization_barrier((others, sum_hi))
     share = (share + lax.ppermute(others, "core", [(0, 1), (1, 0)])).astype(BF)
-    got = spread_column(dq)
-    *some, share = lax.optimization_barrier((*got[1:5], share))
-    got[1:5] = some
+    dq = lax.all_to_all(dq, COLUMN, 0, 0, tiled=True)
+    dq, share = lax.optimization_barrier((dq, share))
     sum_lo = jnp.sum(lax.all_to_all(share, ("yh", "x"), 0, 0, tiled=True).astype(F4), axis=0)
 
-    grad_query = jnp.swapaxes(place_call(info, got), 0, 1)
+    grad_query = jnp.swapaxes(dq.reshape(8 * HEADS, SUB, HD), 0, 1).astype(F4)
 
     r0 = jnp.stack([sum_lo[0], jnp.where(upper, sum_hi[1], sum_lo[1])]).astype(BF)
     r1 = jnp.stack([sum_hi[0], jnp.where(upper, sum_lo[1], sum_hi[1])]).astype(BF)

time: 209 us -> 205 us (0.981)
  starting transfers between devices: 58 us -> 36.7 us
  Pallas kernels: 58.7 us -> 76.8 us
  waiting for transfers between devices: 45.7 us -> 41.7 us
  other arithmetic: 4.92 us -> 7.91 us
    ppermute x7 -> x0, starting transfers between devices: 26.6 us -> none  [swap(): lax.ppermute(block, ('zl', 'yp', 'zh'), [(i, i ^ flip) for i in range(8)])]
    all_to_all x0 -> x1, waiting for transfers between devices: none -> 13.5 us  [shards(): dq = lax.all_to_all(dq, COLUMN, 0, 0, tiled=True)]
    ppermute x7 -> x0, waiting for transfers between devices: 12.6 us -> none  [swap(): lax.ppermute(block, ('zl', 'yp', 'zh'), [(i, i ^ flip) for i in range(8)])]
    pallas_call x2, Pallas kernels: 37.1 us -> 49.3 us  [grads_call(): pl.pallas_call(functools.partial(grads_kernel, half, last), out_shape=(dq...]
    all_to_all x0 -> x1, starting transfers between devices: none -> 7.62 us  [shards(): dq = lax.all_to_all(dq, COLUMN, 0, 0, tiled=True)]
    pallas_call x1, Pallas kernels: 20.9 us -> 27.6 us  [stats_call(): pl.pallas_call(stats_kernel, out_shape=jax.ShapeDtypeStruct((4, 2, 8, ROW...]
    all_to_all x1, waiting for transfers between devices: 7.83 us -> 1.35 us  [reduce_half(): lax.all_to_all(blocks, PLANE, 0, 0, tiled=True).astype(F4)]
    ppermute x4, starting transfers between devices: 5.7 us -> 3.49 us  [across(): return lax.ppermute(block, ('zl', 'yp', 'core'), pairs)]
  transfers between devices with their start and end apart: 20 -> 14, of which waited for: 9 -> 6; matrix products, arithmetic and copies ran while one was open for 4% -> 5% of each run, Pallas kernels for 9% -> 13%
where the time goes in v4:
time: 205 us; the launch traced here: 202 us
  Pallas kernels  76.8 us (37%)
  waiting for transfers between devices  41.7 us (20%)
  starting transfers between devices  36.7 us (18%)
  blocking collectives  22.7 us (11%)
  local copies, waits for them, and re-layouts  13.4 us (7%)
  other arithmetic  7.91 us (4%)
  between operations  2.94 us (1%)
    pallas_call x2, Pallas kernels, grads_call(): pl.pallas_call(functools.partial(grads_kernel, half, last), out_shape=(dq...  49.3 us
    pallas_call x1, Pallas kernels, stats_call(): pl.pallas_call(stats_kernel, out_shape=jax.ShapeDtypeStruct((4, 2, 8, ROW...  27.6 us
    all_to_all x1, blocking collectives, shards(): lax.all_to_all(share, ('yh', 'x'), 0, 0, tiled=True).astype(F4)  22.7 us
    ppermute x3, waiting for transfers between devices, shift_x(): return lax.ppermute(block, 'x', [((i + by) % 4, i) for i in range(4)])  21.1 us
    all_to_all x1, waiting for transfers between devices, shards(): dq = lax.all_to_all(dq, COLUMN, 0, 0, tiled=True)  13.5 us
    all_to_all x1, starting transfers between devices, shards(): lax.all_to_all(qd, COLUMN, 0, 0, tiled=True)  11.1 us
    all_to_all x1, starting transfers between devices, shards(): dq = lax.all_to_all(dq, COLUMN, 0, 0, tiled=True)  7.62 us
    unnamed x18, local copies, waits for them, and re-layouts  7.28 us
  transfers between devices with their start and end apart: 14, of which 6 were waited for; matrix products, arithmetic and copies ran while one was open for 5% of the time, Pallas kernels for 13%

profile of v4, /device:TPU:0, one launch (start us, length us, event | category | flops | bytes accessed | tf_op | source)
XLA Modules:
  0.0 202.3 jit_solution(15846373491216047131)
XLA Ops:
  0.6 1.3 collective-permute-start.2
  1.9 1.0 copy_bitcast_fusion.3
  2.9 0.9 copy_bitcast_fusion.1
  3.9 0.0 copy-start.7
  3.9 2.1 %collective-permute-start.1 = (bf16[2,2,128,128]{3,2,1,0:T(8,128)(2,1)S(1)}, bf16[2,2,128,128]{3,2,1,0:T(8,128)(2,1)S(1)}, u32[]{:S(2)}, u32[]{:S(2)}) collective-permute-start(bf16[2,2,128,128]{3,2,1,0:T(8,128)(2,1)S(1)} %get-tuple-element.55), channel_id=1, source_target_pairs={{0,64},{1,80},{16,65},{17,81},{64,0},{65,16},{80,1},{81,17},{2,66}... | collective-permute-start | bytes 393224 | tf_op jit(solution)/shard_map/ppermute | solution.py:267
  6.0 0.7 collective-permute-start
  7.4 0.0 collective-permute-done.2
  7.4 0.6 fusion.8
  9.2 0.0 collective-permute-done.1
  9.3 0.0 collective-permute-done
  9.3 0.1 broadcast_select_fusion.5
  9.5 3.3 %collective-permute-start.3 = (bf16[2,2,2,128,128]{4,3,2,1,0:T(8,128)(2,1)S(1)}, bf16[2,2,2,128,128]{4,3,2,1,0:T(8,128)(2,1)S(1)}, u32[]{:S(2)}, u32[]{:S(2)}) collective-permute-start(bf16[2,2,2,128,128]{4,3,2,1,0:T(8,128)(2,1)S(1)} %pad_maximum_fusion.4), channel_id=1, source_target_pairs={{0,32},{32,0},{1,33},{33,1},{2,34},{34,2},{3,35},{35,3},{4,36},{36... | collective-permute-start | bytes 786440 | tf_op jit(solution)/shard_map/ppermute | solution.py:302
  12.7 0.0 copy-done.6
  12.8 0.3 copy.34
  13.1 0.0 copy-done.7
  13.1 0.3 copy.35
  13.4 0.1 pad_maximum_fusion.2
  13.5 1.4 copy.36
  15.0 11.1 %all-to-all-start = ((bf16[8,2,12,32,128]{4,3,2,1,0:T(8,128)(2,1)}), bf16[8,2,12,32,128]{4,3,2,1,0:T(8,128)(2,1)}, u32[]{:S(2)}, u32[]{:S(2)}) async-start(bf16[8,2,12,32,128]{4,3,2,1,0:T(8,128)(2,1)} %copy.36), calls=%async_computation | async-start | bytes 3145728 | tf_op jit(solution)/shard_map/all_to_all | solution.py:288
  26.1 0.0 collective-permute-done.3
  26.1 0.1 fusion.7
  26.2 3.1 %collective-permute-start.5 = (bf16[2,2,2,2,128,128]{5,4,3,2,1,0:T(8,128)(2,1)S(1)}, bf16[2,2,2,2,128,128]{5,4,3,2,1,0:T(8,128)(2,1)S(1)}, u32[]{:S(2)}, u32[]{:S(2)}) collective-permute-start(bf16[2,2,2,2,128,128]{5,4,3,2,1,0:T(8,128)(2,1)S(1)} %get-tuple-element.42), channel_id=1, source_target_pairs={{8,0},{12,4},{0,8},{4,12},{9,1},{13,5},{1,9},{5,13},{10,2},{14,6},... | collective-permute-start | bytes 1572872 | tf_op jit(solution)/shard_map/ppermute | solution.py:271
  29.3 1.1 collective-permute-start.4
  30.4 0.9 collective-permute-start.6
  31.3 11.4 %collective-permute-done.5 = bf16[2,2,2,2,128,128]{5,4,3,2,1,0:T(8,128)(2,1)S(1)} collective-permute-done((bf16[2,2,2,2,128,128]{5,4,3,2,1,0:T(8,128)(2,1)S(1)}, bf16[2,2,2,2,128,128]{5,4,3,2,1,0:T(8,128)(2,1)S(1)}, u32[]{:S(2)}, u32[]{:S(2)}) %collective-permute-start.5) | collective-permute-done | bytes 524320 | tf_op jit(solution)/shard_map/ppermute | solution.py:271
  42.7 9.7 %collective-permute-done.4 = bf16[2,2,2,2,128,128]{5,4,3,2,1,0:T(8,128)(2,1)S(1)} collective-permute-done((bf16[2,2,2,2,128,128]{5,4,3,2,1,0:T(8,128)(2,1)S(1)}, bf16[2,2,2,2,128,128]{5,4,3,2,1,0:T(8,128)(2,1)S(1)}, u32[]{:S(2)}, u32[]{:S(2)}) %collective-permute-start.4) | collective-permute-done | bytes 524320 | tf_op jit(solution)/shard_map/ppermute | solution.py:271
  52.4 0.0 collective-permute-done.6
  52.4 0.3 pad_maximum_fusion
  52.7 0.3 dynamic-slice_bitcast_fusion.3
  53.0 0.3 pad_maximum_fusion.1
  53.2 0.0 all-to-all-done
  53.3 0.1 collective-permute-start.7
  53.4 0.1 pad_add_fusion.info
  53.4 4.2 %collective-permute-done.7.other = bf16[8,2,2,2,128,128]{5,4,3,2,1,0:T(8,128)(2,1)} collective-permute-done((bf16[8,2,2,2,128,128]{5,4,3,2,1,0:T(8,128)(2,1)S(1)}, bf16[8,2,2,2,128,128]{5,4,3,2,1,0:T(8,128)(2,1)}, u32[]{:S(2)}, u32[]{:S(2)}) %collective-permute-start.7) | collective-permute-done | bytes 2097184 | tf_op jit(solution)/shard_map/ppermute | solution.py:308
  57.6 27.6 %stats.1.st_ref = f32[4,2,8,768]{3,2,1,0:T(8,128)S(1)} custom-call(s32[4]{0:T(128)S(1)} %pad_add_fusion.info, bf16[2,2,2,2,12,32,128]{6,5,4,3,2,1,0:T(8,128)(2,1)} %bitcast.32.qd_ref, bf16[8,2,2,2,128,128]{5,4,3,2,1,0:T(8,128)(2,1)S(1)} %bitcast.73, bf16[8,2,2,2,128,128]{5,4,3,2,1,0:T(8,128)(2,1)} %collective-permute-done.7.other), custom_call_target="tpu_custom_call" | custom-call | flops 10380902400 | bytes 4194304 | tf_op jit(solution)/shard_map/stats/pallas_call | solution.py:215
  85.2 23.9 %grads1.1 = (f32[4,128,768]{2,1,0:T(8,128)S(1)}, bf16[16,2,2,128,128]{4,3,2,1,0:T(8,128)(2,1)S(1)}) custom-call(s32[4]{0:T(128)S(1)} %pad_add_fusion.info, bf16[2,2,2,2,12,32,128]{6,5,4,3,2,1,0:T(8,128)(2,1)} %bitcast.32.qd_ref, f32[4,2,8,768]{3,2,1,0:T(8,128)S(1)} %stats.1.st_ref, bf16[8,2,2,2,128,128]{5,4,3,2,1,0:T(8,128)(2,1)S(1)} %bitcast.74, ...), custom_call_target="tpu_custom_call" | custom-call | flops 12976128000 | bytes 8388608 | tf_op jit(solution)/shard_map/grads1/pallas_call | solution.py:242
  109.1 0.0 copy-start.2
  109.1 1.4 copy-done.2
  110.5 1.1 copy-done.4
  111.6 4.6 %all-to-all-start.2 = ((bf16[16,2,2,128,128]{4,3,2,1,0:T(8,128)(2,1)}), bf16[16,2,2,128,128]{4,3,2,1,0:T(8,128)(2,1)}, u32[]{:S(2)}, u32[]{:S(2)}) async-start(bf16[16,2,2,128,128]{4,3,2,1,0:T(8,128)(2,1)} %copy-done.2), calls=%async_computation.2 | async-start | bytes 4194304 | tf_op jit(solution)/shard_map/all_to_all | solution.py:275
  116.2 0.0 copy-start.5
  116.2 1.4 copy-done.5
  117.6 25.4 %grads0.1 = (bf16[8,12,32,128]{3,2,1,0:T(8,128)(2,1)}, f32[8,2,2,128,128]{4,3,2,1,0:T(8,128)S(1)}, f32[8,2,2,128,128]{4,3,2,1,0:T(8,128)S(1)}) custom-call(s32[4]{0:T(128)S(1)} %pad_add_fusion.info, bf16[2,2,2,2,12,32,128]{6,5,4,3,2,1,0:T(8,128)(2,1)} %bitcast.32.qd_ref, f32[4,2,8,768]{3,2,1,0:T(8,128)S(1)} %stats.1.st_ref, ...), custom_call_target="tpu_custom_call" | custom-call | flops 12976128000 | bytes 8388608 | tf_op jit(solution)/shard_map/grads0/pallas_call | solution.py:242
  143.0 0.0 copy-start
  143.0 1.3 copy-done
  144.4 1.4 copy-done.3
  145.8 1.4 all-to-all-done.2
  147.1 2.1 %convert_reduce_fusion = bf16[2,2,128,128]{3,2,1,0:T(8,128)(2,1)S(1)} fusion(bf16[16,2,2,128,128]{4,3,2,1,0:T(8,128)(2,1)} %all-to-all-done.2), kind=kLoop, calls=%fused_computation | loop fusion | flops 2031616 | bytes 2228224 | tf_op jit(solution)/shard_map/reduce_sum | solution.py:275
  149.2 0.1 collective-permute-start.8
  149.3 7.6 %all-to-all-start.1 = ((bf16[8,12,32,128]{3,2,1,0:T(8,128)(2,1)}), bf16[8,12,32,128]{3,2,1,0:T(8,128)(2,1)}, u32[]{:S(2)}, u32[]{:S(2)}) async-start(bf16[8,12,32,128]{3,2,1,0:T(8,128)(2,1)} %get-tuple-element.25), calls=%async_computation.1 | async-start | bytes 1572864 | tf_op jit(solution)/shard_map/all_to_all | solution.py:318
  156.9 0.0 collective-permute-done.8
  156.9 0.0 copy-done.1
  156.9 1.9 add_convert_fusion
  158.8 13.5 %all-to-all-done.1 = bf16[8,12,32,128]{3,2,1,0:T(8,128)(2,1)} async-done(((bf16[8,12,32,128]{3,2,1,0:T(8,128)(2,1)}), bf16[8,12,32,128]{3,2,1,0:T(8,128)(2,1)}, u32[]{:S(2)}, u32[]{:S(2)}) %all-to-all-start.1) | async-done | bytes 786464 | tf_op jit(solution)/shard_map/all_to_all | solution.py:318
  172.3 22.7 %all_to_all.20 = bf16[8,2,2,128,128]{4,3,2,1,0:T(8,128)(2,1)S(1)} all-to-all(bf16[8,2,2,128,128]{4,3,2,1,0:T(8,128)(2,1)S(1)} %add_convert_fusion), channel_id=1, replica_groups=mesh['zl'=2,'yh'=2,'yp'=2,'x'=4,'zh'=2,'core'=2] {'yh','x'}, dimensions={0} | all-to-all | bytes 2097152 | tf_op jit(solution)/shard_map/all_to_all | solution.py:320
  195.0 0.1 convert_reduce_fusion.1
  195.2 0.1 select_convert_fusion.1
  195.3 0.7 collective-permute-start.9
  196.0 0.1 collective-permute-start.10
  196.1 1.3 bitcast_convert_fusion
  197.4 2.1 %copy.44 = f32[96,32,128]{2,0,1:T(8,128)} copy(f32[96,32,128]{2,1,0:T(8,128)S(1)} %bitcast_convert_fusion) | data formatting | bytes 3145728 | tf_op jit(solution)/shard_map/convert_element_type | solution.py:322
  199.5 0.0 collective-permute-done.9
  199.5 1.5 collective-permute-done.10
  201.1 1.2 fusion.3
  (16 shorter events, 0.3 us)
Async XLA Ops:
  0.6 6.7 %collective-permute-start.2 = (s32[2]{0:T(128)}, s32[2]{0:T(128)S(1)}, u32[]{:S(2)}, u32[]{:S(2)}) collective-permute-start(s32[2]{0:T(128)} %param.14), channel_id=1, source_target_pairs={{0,0},{1,16},{16,1},{17,17},{2,2},{3,18},{18,3},{19,19},{4,4},{5,2... | collective-permute-start | bytes 32 | tf_op jit(solution)/shard_map/ppermute | solution.py:281
  1.9 10.8 %copy-start.6 = (bf16[32,96,128]{2,1,0:T(8,128)(2,1)S(1)}, bf16[32,96,128]{2,1,0:T(8,128)(2,1)}, u32[]{:S(2)}) copy-start(bf16[32,96,128]{2,1,0:T(8,128)(2,1)} %param.8) | copy-start | bytes 2359300
  3.9 9.2 %copy-start.7 = (bf16[32,96,128]{2,1,0:T(8,128)(2,1)S(1)}, bf16[32,96,128]{2,1,0:T(8,128)(2,1)}, u32[]{:S(2)}) copy-start(bf16[32,96,128]{2,1,0:T(8,128)(2,1)} %param.15) | copy-start | bytes 2359300
  3.9 5.3 %collective-permute-start.1 = (bf16[2,2,128,128]{3,2,1,0:T(8,128)(2,1)S(1)}, bf16[2,2,128,128]{3,2,1,0:T(8,128)(2,1)S(1)}, u32[]{:S(2)}, u32[]{:S(2)}) collective-permute-start(bf16[2,2,128,128]{3,2,1,0:T(8,128)(2,1)S(1)} %get-tuple-element.55), channel_id=1, source_target_pairs={{0,64},{1,80},{16,65},{17,81},{64,0},{65,16},{80,1},{81,17},{2,66}... | collective-permute-start | bytes 393224 | tf_op jit(solution)/shard_map/ppermute | solution.py:267
  6.0 3.2 %collective-permute-start = (bf16[2,2,128,128]{3,2,1,0:T(8,128)(2,1)S(1)}, bf16[2,2,128,128]{3,2,1,0:T(8,128)(2,1)S(1)}, u32[]{:S(2)}, u32[]{:S(2)}) collective-permute-start(bf16[2,2,128,128]{3,2,1,0:T(8,128)(2,1)S(1)} %get-tuple-element.56), channel_id=1, source_target_pairs={{0,0},{1,16},{16,1},{17,17},{64,64},{65,80},{80,65},{81,81},{2,2},... | collective-permute-start | bytes 393224 | tf_op jit(solution)/shard_map/ppermute | solution.py:267
  9.5 16.6 %collective-permute-start.3 = (bf16[2,2,2,128,128]{4,3,2,1,0:T(8,128)(2,1)S(1)}, bf16[2,2,2,128,128]{4,3,2,1,0:T(8,128)(2,1)S(1)}, u32[]{:S(2)}, u32[]{:S(2)}) collective-permute-start(bf16[2,2,2,128,128]{4,3,2,1,0:T(8,128)(2,1)S(1)} %pad_maximum_fusion.4), channel_id=1, source_target_pairs={{0,32},{32,0},{1,33},{33,1},{2,34},{34,2},{3,35},{35,3},{4,36},{36... | collective-permute-start | bytes 786440 | tf_op jit(solution)/shard_map/ppermute | solution.py:302
  15.0 38.3 %all-to-all-start = ((bf16[8,2,12,32,128]{4,3,2,1,0:T(8,128)(2,1)}), bf16[8,2,12,32,128]{4,3,2,1,0:T(8,128)(2,1)}, u32[]{:S(2)}, u32[]{:S(2)}) async-start(bf16[8,2,12,32,128]{4,3,2,1,0:T(8,128)(2,1)} %copy.36), calls=%async_computation | async-start | bytes 3145728 | tf_op jit(solution)/shard_map/all_to_all | solution.py:288
  26.2 16.5 %collective-permute-start.5 = (bf16[2,2,2,2,128,128]{5,4,3,2,1,0:T(8,128)(2,1)S(1)}, bf16[2,2,2,2,128,128]{5,4,3,2,1,0:T(8,128)(2,1)S(1)}, u32[]{:S(2)}, u32[]{:S(2)}) collective-permute-start(bf16[2,2,2,2,128,128]{5,4,3,2,1,0:T(8,128)(2,1)S(1)} %get-tuple-element.42), channel_id=1, source_target_pairs={{8,0},{12,4},{0,8},{4,12},{9,1},{13,5},{1,9},{5,13},{10,2},{14,6},... | collective-permute-start | bytes 1572872 | tf_op jit(solution)/shard_map/ppermute | solution.py:271
  29.3 23.1 %collective-permute-start.4 = (bf16[2,2,2,2,128,128]{5,4,3,2,1,0:T(8,128)(2,1)S(1)}, bf16[2,2,2,2,128,128]{5,4,3,2,1,0:T(8,128)(2,1)S(1)}, u32[]{:S(2)}, u32[]{:S(2)}) collective-permute-start(bf16[2,2,2,2,128,128]{5,4,3,2,1,0:T(8,128)(2,1)S(1)} %get-tuple-element.42), channel_id=1, source_target_pairs={{4,0},{8,4},{12,8},{0,12},{5,1},{9,5},{13,9},{1,13},{6,2},{10,6},{... | collective-permute-start | bytes 1572872 | tf_op jit(solution)/shard_map/ppermute | solution.py:271
  30.4 22.0 %collective-permute-start.6 = (bf16[2,2,2,2,128,128]{5,4,3,2,1,0:T(8,128)(2,1)S(1)}, bf16[2,2,2,2,128,128]{5,4,3,2,1,0:T(8,128)(2,1)S(1)}, u32[]{:S(2)}, u32[]{:S(2)}) collective-permute-start(bf16[2,2,2,2,128,128]{5,4,3,2,1,0:T(8,128)(2,1)S(1)} %get-tuple-element.42), channel_id=1, source_target_pairs={{12,0},{0,4},{4,8},{8,12},{13,1},{1,5},{5,9},{9,13},{14,2},{2,6},{... | collective-permute-start | bytes 1572872 | tf_op jit(solution)/shard_map/ppermute | solution.py:271
  53.3 4.4 %collective-permute-start.7 = (bf16[8,2,2,2,128,128]{5,4,3,2,1,0:T(8,128)(2,1)S(1)}, bf16[8,2,2,2,128,128]{5,4,3,2,1,0:T(8,128)(2,1)}, u32[]{:S(2)}, u32[]{:S(2)}) collective-permute-start(bf16[8,2,2,2,128,128]{5,4,3,2,1,0:T(8,128)(2,1)S(1)} %bitcast.72), channel_id=1, source_target_pairs={{0,1},{1,0},{2,3},{3,2},{4,5},{5,4},{6,7},{7,6},{8,9},{9,8},{10,11... | collective-permute-start | bytes 6291464 | tf_op jit(solution)/shard_map/ppermute | solution.py:308
  109.1 1.4 copy-start.2
  110.5 1.1 copy-start.4
  111.6 35.5 %all-to-all-start.2 = ((bf16[16,2,2,128,128]{4,3,2,1,0:T(8,128)(2,1)}), bf16[16,2,2,128,128]{4,3,2,1,0:T(8,128)(2,1)}, u32[]{:S(2)}, u32[]{:S(2)}) async-start(bf16[16,2,2,128,128]{4,3,2,1,0:T(8,128)(2,1)} %copy-done.2), calls=%async_computation.2 | async-start | bytes 4194304 | tf_op jit(solution)/shard_map/all_to_all | solution.py:275
  116.2 1.4 copy-start.5
  143.0 1.4 copy-start
  144.4 1.4 copy-start.3
  147.1 9.8 %copy-start.1 = (f32[8,2,2,128,128]{4,3,2,1,0:T(8,128)S(1)}, f32[8,2,2,128,128]{4,3,2,1,0:T(8,128)}, u32[]{:S(2)}) copy-start(f32[8,2,2,128,128]{4,3,2,1,0:T(8,128)} %copy-done) | copy-start | bytes 6291460
  149.2 7.7 %collective-permute-start.8 = (f32[8,2,2,128,128]{4,3,2,1,0:T(8,128)}, f32[8,2,2,128,128]{4,3,2,1,0:T(8,128)}, u32[]{:S(2)}, u32[]{:S(2)}) collective-permute-start(f32[8,2,2,128,128]{4,3,2,1,0:T(8,128)} %copy-done.3), channel_id=1, source_target_pairs={{0,1},{1,0},{2,3},{3,2},{4,5},{5,4},{6,7},{7,6},{8,9},{9,8},{10,11... | collective-permute-start | bytes 6291464 | tf_op jit(solution)/shard_map/ppermute | solution.py:317
  149.3 23.1 %all-to-all-start.1 = ((bf16[8,12,32,128]{3,2,1,0:T(8,128)(2,1)}), bf16[8,12,32,128]{3,2,1,0:T(8,128)(2,1)}, u32[]{:S(2)}, u32[]{:S(2)}) async-start(bf16[8,12,32,128]{3,2,1,0:T(8,128)(2,1)} %get-tuple-element.25), calls=%async_computation.1 | async-start | bytes 1572864 | tf_op jit(solution)/shard_map/all_to_all | solution.py:318
  195.3 4.2 %collective-permute-start.9 = (bf16[2,2,128,128]{3,2,1,0:T(8,128)(2,1)S(1)}, bf16[2,2,128,128]{3,2,1,0:T(8,128)(2,1)S(1)}, u32[]{:S(2)}, u32[]{:S(2)}) collective-permute-start(bf16[2,2,128,128]{3,2,1,0:T(8,128)(2,1)S(1)} %get-tuple-element.51), channel_id=1, source_target_pairs={{0,0},{1,16},{16,1},{17,17},{64,64},{65,80},{80,65},{81,81},{2,2},... | collective-permute-start | bytes 393224 | tf_op jit(solution)/shard_map/ppermute | solution.py:267
  196.0 5.0 %collective-permute-start.10 = (bf16[2,2,128,128]{3,2,1,0:T(8,128)(2,1)S(1)}, bf16[2,2,128,128]{3,2,1,0:T(8,128)(2,1)S(1)}, u32[]{:S(2)}, u32[]{:S(2)}) collective-permute-start(bf16[2,2,128,128]{3,2,1,0:T(8,128)(2,1)S(1)} %get-tuple-element.52), channel_id=1, source_target_pairs={{0,64},{1,80},{16,65},{17,81},{64,0},{65,16},{80,1},{81,17},{2,66}... | collective-permute-start | bytes 393224 | tf_op jit(solution)/shard_map/ppermute | solution.py:267

commit v5 on v4

--- a/solution.py
+++ b/solution.py
@@ -140,7 +140,10 @@
 def grads_kernel(half, last, info, qd_ref, st_ref, own, other, *refs):
     if last:
         prev, refs = refs[0], refs[1:]
-    dq_ref, *out_refs, q_s, do_s, kv_s, sem, dqt_s, acc = refs
+    dq_ref, *out_refs, q_s, do_s, kv_s, sem, dq_s, acc, out_s, out_sem, dq_sem = refs
+    if last:
+        before = pltpu.make_async_copy(prev, dq_s, dq_sem.at[0])
+        before.start()
     fetch((own.at[:, half], other.at[:, half]), kv_s, sem)
 
     def zero(i, _):
@@ -148,16 +151,16 @@
         return 0
 
     lax.fori_loop(0, 4, zero, 0)
+    if last:
+        before.wait()
 
     def per_run(run, _):
         n_all, block = block_plan(info, half, run)
         load_rows(qd_ref, 0, run, q_s)
         load_rows(qd_ref, 1, run, do_s)
         lse, delta = st_ref[run, 0], st_ref[run, 1]
-        if last:
-            dqt_s[...] = prev[run]
-        else:
-            dqt_s[...] = jnp.zeros_like(dqt_s)
+        if not last:
+            dq_s[run] = jnp.zeros((HD, ROWS), F4)
 
         def body(i, _):
             seg, ya, (rel, cols), full, bias = block(i)
@@ -174,7 +177,7 @@
                 ds = (p3 * (g3 - delta[None])).reshape(KB, ROWS).astype(BF)
                 acc[ya, seg, 1] += nn(pb, do_s[...])
                 acc[ya, seg, 0] += nn(ds, q_s[...])
-                dqt_s[...] += nn(jnp.transpose(k), ds)
+                dq_s[run] += nn(jnp.transpose(k), ds)
 
             pl.when(full)(functools.partial(tile, False))
             pl.when(jnp.logical_not(full))(functools.partial(tile, True))
@@ -182,26 +185,31 @@
 
         lax.fori_loop(0, n_all, body, 0)
         if last:
-            dq = (jnp.transpose(dqt_s[...]) * SCALE).astype(BF)
+            dq = (jnp.transpose(dq_s[run]) * SCALE).astype(BF)
             for j in range(HEADS):
                 for zh in range(2):
                     rows = dq[j * PART + zh * SUB : j * PART + (zh + 1) * SUB]
                     dq_ref[4 * zh + 2 * (run % 2) + run // 2, j] = rows
+        return 0
+
+    lax.fori_loop(0, 4, per_run, 0)
+    copies = [] if last else [pltpu.make_async_copy(dq_s, dq_ref, dq_sem.at[0])]
+    for c in copies:
+        c.start()
+    for i in range(4):
+        if last:
+            out_ref, cols = out_refs[i % 2], pl.ds(4 * (i // 2), 4)
+            ya = 2 * (i // 2) + ((i % 2) ^ info[3])
         else:
-            dq_ref[run] = dqt_s[...]
-        return 0
-
-    lax.fori_loop(0, 4, per_run, 0)
-    for i in range(4):
+            out_ref, cols, ya = out_refs[0], pl.ds(4 * i, 4), i
         for seg in range(2):
-            if last:
-                out_ref, cols = out_refs[i % 2], pl.ds(4 * (i // 2), 4)
-                ya = 2 * (i // 2) + ((i % 2) ^ info[3])
-            else:
-                out_ref, cols, ya = out_refs[0], pl.ds(4 * i, 4), i
             keys, values = acc[ya, seg, 0] * SCALE, acc[ya, seg, 1]
-            out_ref[cols, seg, 0] = keys.astype(out_ref.dtype).reshape(4, TOK, HD)
-            out_ref[cols, seg, 1] = values.astype(out_ref.dtype).reshape(4, TOK, HD)
+            out_s[i, :, seg, 0] = keys.astype(out_s.dtype).reshape(4, TOK, HD)
+            out_s[i, :, seg, 1] = values.astype(out_s.dtype).reshape(4, TOK, HD)
+        copies.append(pltpu.make_async_copy(out_s.at[i], out_ref.at[cols], out_sem.at[i]))
+        copies[-1].start()
+    for c in copies:
+        c.wait()
 
 
 VM = pl.BlockSpec(memory_space=pltpu.VMEM)
@@ -242,14 +250,17 @@
     return pl.pallas_call(
         functools.partial(grads_kernel, half, last),
         out_shape=(dq_shape, *sums),
-        in_specs=[SM, VM, VM, ANY, ANY] + ([VM] if last else []),
-        out_specs=(VM,) * (1 + len(sums)),
+        in_specs=[SM, VM, VM, ANY, ANY] + ([ANY] if last else []),
+        out_specs=(VM if last else ANY,) + (ANY,) * len(sums),
         scratch_shapes=[
             *ROW_SCRATCH,
             pltpu.VMEM((2, 8, 2, 2, TOK, HD), BF),
             pltpu.SemaphoreType.DMA((2,)),
-            pltpu.VMEM((HD, ROWS), F4),
+            pltpu.VMEM((4, HD, ROWS), F4),
             pltpu.VMEM((4, 2, 2, KB, HD), F4),
+            pltpu.VMEM((4, 4, 2, 2, TOK, HD), F4 if last else BF),
+            pltpu.SemaphoreType.DMA((4,)),
+            pltpu.SemaphoreType.DMA((1,)),
         ],
         compiler_params=pltpu.CompilerParams(vmem_limit_bytes=32 * 2**20),
         cost_estimate=pl.CostEstimate(flops=10 * PAIRS * HD, bytes_accessed=8 << 20, transcendentals=PAIRS // 2),

time: 205 us -> 206 us (level)
  Pallas kernels: 76.8 us -> 81 us
  starting transfers between devices: 36.7 us -> 34.2 us
    all_to_all x1, starting transfers between devices: 7.62 us -> 4.41 us  [shards(): dq = lax.all_to_all(dq, COLUMN, 0, 0, tiled=True)]
    pallas_call x2, Pallas kernels: 49.3 us -> 52.1 us  [grads_call(): pl.pallas_call(functools.partial(grads_kernel, half, last), out_shape=(dq...]
where the time goes in v5:
time: 206 us; the launch traced here: 203 us
  Pallas kernels  81 us (39%)
  waiting for transfers between devices  40 us (19%)
  starting transfers between devices  34.2 us (17%)
  blocking collectives  23.4 us (11%)
  local copies, waits for them, and re-layouts  13.4 us (7%)
  other arithmetic  7.91 us (4%)
  between operations  2.93 us (1%)
    pallas_call x2, Pallas kernels, grads_call(): pl.pallas_call(functools.partial(grads_kernel, half, last), out_shape=(dq...  52.1 us
    pallas_call x1, Pallas kernels, stats_call(): pl.pallas_call(stats_kernel, out_shape=jax.ShapeDtypeStruct((4, 2, 8, ROW...  28.9 us
    all_to_all x1, blocking collectives, shards(): lax.all_to_all(share, ('yh', 'x'), 0, 0, tiled=True).astype(F4)  23.4 us
    ppermute x3, waiting for transfers between devices, shift_x(): return lax.ppermute(block, 'x', [((i + by) % 4, i) for i in range(4)])  21.1 us
    all_to_all x1, waiting for transfers between devices, shards(): dq = lax.all_to_all(dq, COLUMN, 0, 0, tiled=True)  13 us
    all_to_all x1, starting transfers between devices, shards(): lax.all_to_all(qd, COLUMN, 0, 0, tiled=True)  11.1 us
    unnamed x18, local copies, waits for them, and re-layouts  7.28 us
    ppermute x3, starting transfers between devices, shift_x(): return lax.ppermute(block, 'x', [((i + by) % 4, i) for i in range(4)])  5.13 us
  transfers between devices with their start and end apart: 14, of which 6 were waited for; matrix products, arithmetic and copies ran while one was open for 5% of the time, Pallas kernels for 13%

profile of v5, /device:TPU:0, one launch (start us, length us, event | category | flops | bytes accessed | tf_op | source)
XLA Modules:
  0.0 202.9 jit_solution(13626317642756127670)
XLA Ops:
  0.6 1.3 collective-permute-start.2
  1.9 1.0 copy_bitcast_fusion.3
  2.9 0.9 copy_bitcast_fusion.1
  3.9 0.0 copy-start.7
  3.9 2.1 %collective-permute-start.1 = (bf16[2,2,128,128]{3,2,1,0:T(8,128)(2,1)S(1)}, bf16[2,2,128,128]{3,2,1,0:T(8,128)(2,1)S(1)}, u32[]{:S(2)}, u32[]{:S(2)}) collective-permute-start(bf16[2,2,128,128]{3,2,1,0:T(8,128)(2,1)S(1)} %get-tuple-element.55), channel_id=1, source_target_pairs={{0,64},{1,80},{16,65},{17,81},{64,0},{65,16},{80,1},{81,17},{2,66}... | collective-permute-start | bytes 393224 | tf_op jit(solution)/shard_map/ppermute | solution.py:278
  6.0 0.7 collective-permute-start
  7.4 0.0 collective-permute-done.2
  7.4 0.6 fusion.8
  9.2 0.0 collective-permute-done.1
  9.3 0.0 collective-permute-done
  9.3 0.1 broadcast_select_fusion.5
  9.5 3.3 %collective-permute-start.3 = (bf16[2,2,2,128,128]{4,3,2,1,0:T(8,128)(2,1)S(1)}, bf16[2,2,2,128,128]{4,3,2,1,0:T(8,128)(2,1)S(1)}, u32[]{:S(2)}, u32[]{:S(2)}) collective-permute-start(bf16[2,2,2,128,128]{4,3,2,1,0:T(8,128)(2,1)S(1)} %pad_maximum_fusion.4), channel_id=1, source_target_pairs={{0,32},{32,0},{1,33},{33,1},{2,34},{34,2},{3,35},{35,3},{4,36},{36... | collective-permute-start | bytes 786440 | tf_op jit(solution)/shard_map/ppermute | solution.py:313
  12.7 0.0 copy-done.6
  12.8 0.3 copy.34
  13.1 0.0 copy-done.7
  13.1 0.3 copy.35
  13.4 0.1 pad_maximum_fusion.2
  13.5 1.4 copy.36
  15.0 11.1 %all-to-all-start = ((bf16[8,2,12,32,128]{4,3,2,1,0:T(8,128)(2,1)}), bf16[8,2,12,32,128]{4,3,2,1,0:T(8,128)(2,1)}, u32[]{:S(2)}, u32[]{:S(2)}) async-start(bf16[8,2,12,32,128]{4,3,2,1,0:T(8,128)(2,1)} %copy.36), calls=%async_computation | async-start | bytes 3145728 | tf_op jit(solution)/shard_map/all_to_all | solution.py:299
  26.1 0.0 collective-permute-done.3
  26.1 0.1 fusion.7
  26.2 3.1 %collective-permute-start.5 = (bf16[2,2,2,2,128,128]{5,4,3,2,1,0:T(8,128)(2,1)S(1)}, bf16[2,2,2,2,128,128]{5,4,3,2,1,0:T(8,128)(2,1)S(1)}, u32[]{:S(2)}, u32[]{:S(2)}) collective-permute-start(bf16[2,2,2,2,128,128]{5,4,3,2,1,0:T(8,128)(2,1)S(1)} %get-tuple-element.42), channel_id=1, source_target_pairs={{8,0},{12,4},{0,8},{4,12},{9,1},{13,5},{1,9},{5,13},{10,2},{14,6},... | collective-permute-start | bytes 1572872 | tf_op jit(solution)/shard_map/ppermute | solution.py:282
  29.3 1.1 collective-permute-start.4
  30.4 0.9 collective-permute-start.6
  31.3 11.4 %collective-permute-done.5 = bf16[2,2,2,2,128,128]{5,4,3,2,1,0:T(8,128)(2,1)S(1)} collective-permute-done((bf16[2,2,2,2,128,128]{5,4,3,2,1,0:T(8,128)(2,1)S(1)}, bf16[2,2,2,2,128,128]{5,4,3,2,1,0:T(8,128)(2,1)S(1)}, u32[]{:S(2)}, u32[]{:S(2)}) %collective-permute-start.5) | collective-permute-done | bytes 524320 | tf_op jit(solution)/shard_map/ppermute | solution.py:282
  42.7 9.7 %collective-permute-done.4 = bf16[2,2,2,2,128,128]{5,4,3,2,1,0:T(8,128)(2,1)S(1)} collective-permute-done((bf16[2,2,2,2,128,128]{5,4,3,2,1,0:T(8,128)(2,1)S(1)}, bf16[2,2,2,2,128,128]{5,4,3,2,1,0:T(8,128)(2,1)S(1)}, u32[]{:S(2)}, u32[]{:S(2)}) %collective-permute-start.4) | collective-permute-done | bytes 524320 | tf_op jit(solution)/shard_map/ppermute | solution.py:282
  52.4 0.0 collective-permute-done.6
  52.4 0.3 pad_maximum_fusion
  52.7 0.3 dynamic-slice_bitcast_fusion.3
  53.0 0.3 pad_maximum_fusion.1
  53.2 0.0 all-to-all-done
  53.3 0.1 collective-permute-start.7
  53.4 0.1 pad_add_fusion.info
  53.4 4.2 %collective-permute-done.7.other = bf16[8,2,2,2,128,128]{5,4,3,2,1,0:T(8,128)(2,1)} collective-permute-done((bf16[8,2,2,2,128,128]{5,4,3,2,1,0:T(8,128)(2,1)S(1)}, bf16[8,2,2,2,128,128]{5,4,3,2,1,0:T(8,128)(2,1)}, u32[]{:S(2)}, u32[]{:S(2)}) %collective-permute-start.7) | collective-permute-done | bytes 2097184 | tf_op jit(solution)/shard_map/ppermute | solution.py:319
  57.6 28.9 %stats.1.st_ref = f32[4,2,8,768]{3,2,1,0:T(8,128)S(1)} custom-call(s32[4]{0:T(128)S(1)} %pad_add_fusion.info, bf16[2,2,2,2,12,32,128]{6,5,4,3,2,1,0:T(8,128)(2,1)} %bitcast.32.qd_ref, bf16[8,2,2,2,128,128]{5,4,3,2,1,0:T(8,128)(2,1)S(1)} %bitcast.73, bf16[8,2,2,2,128,128]{5,4,3,2,1,0:T(8,128)(2,1)} %collective-permute-done.7.other), custom_call_target="tpu_custom_call" | custom-call | flops 10380902400 | bytes 4194304 | tf_op jit(solution)/shard_map/stats/pallas_call | solution.py:223
  86.6 25.2 %grads1.1 = (f32[4,128,768]{2,1,0:T(8,128)S(1)}, bf16[16,2,2,128,128]{4,3,2,1,0:T(8,128)(2,1)S(1)}) custom-call(s32[4]{0:T(128)S(1)} %pad_add_fusion.info, bf16[2,2,2,2,12,32,128]{6,5,4,3,2,1,0:T(8,128)(2,1)} %bitcast.32.qd_ref, f32[4,2,8,768]{3,2,1,0:T(8,128)S(1)} %stats.1.st_ref, bf16[8,2,2,2,128,128]{5,4,3,2,1,0:T(8,128)(2,1)S(1)} %bitcast.74, ...), custom_call_target="tpu_custom_call" | custom-call | flops 12976128000 | bytes 8388608 | tf_op jit(solution)/shard_map/grads1/pallas_call | solution.py:250
  111.8 0.0 copy-start.2
  111.8 1.4 copy-done.2
  113.2 1.1 copy-done.4
  114.3 5.1 %all-to-all-start.2 = ((bf16[16,2,2,128,128]{4,3,2,1,0:T(8,128)(2,1)}), bf16[16,2,2,128,128]{4,3,2,1,0:T(8,128)(2,1)}, u32[]{:S(2)}, u32[]{:S(2)}) async-start(bf16[16,2,2,128,128]{4,3,2,1,0:T(8,128)(2,1)} %copy-done.2), calls=%async_computation.2 | async-start | bytes 4194304 | tf_op jit(solution)/shard_map/all_to_all | solution.py:286
  119.4 0.0 copy-start.5
  119.4 1.4 copy-done.5
  120.8 26.8 %grads0.1 = (bf16[8,12,32,128]{3,2,1,0:T(8,128)(2,1)}, f32[8,2,2,128,128]{4,3,2,1,0:T(8,128)S(1)}, f32[8,2,2,128,128]{4,3,2,1,0:T(8,128)S(1)}) custom-call(s32[4]{0:T(128)S(1)} %pad_add_fusion.info, bf16[2,2,2,2,12,32,128]{6,5,4,3,2,1,0:T(8,128)(2,1)} %bitcast.32.qd_ref, f32[4,2,8,768]{3,2,1,0:T(8,128)S(1)} %stats.1.st_ref, ...), custom_call_target="tpu_custom_call" | custom-call | flops 12976128000 | bytes 8388608 | tf_op jit(solution)/shard_map/grads0/pallas_call | solution.py:250
  147.7 0.0 copy-start
  147.7 1.3 copy-done
  149.0 1.4 copy-done.3
  150.4 0.1 all-to-all-done.2
  150.5 2.1 %convert_reduce_fusion = bf16[2,2,128,128]{3,2,1,0:T(8,128)(2,1)S(1)} fusion(bf16[16,2,2,128,128]{4,3,2,1,0:T(8,128)(2,1)} %all-to-all-done.2), kind=kLoop, calls=%fused_computation | loop fusion | flops 2031616 | bytes 2228224 | tf_op jit(solution)/shard_map/reduce_sum | solution.py:286
  152.6 0.3 collective-permute-start.8
  152.9 4.4 %all-to-all-start.1 = ((bf16[8,12,32,128]{3,2,1,0:T(8,128)(2,1)}), bf16[8,12,32,128]{3,2,1,0:T(8,128)(2,1)}, u32[]{:S(2)}, u32[]{:S(2)}) async-start(bf16[8,12,32,128]{3,2,1,0:T(8,128)(2,1)} %get-tuple-element.25), calls=%async_computation.1 | async-start | bytes 1572864 | tf_op jit(solution)/shard_map/all_to_all | solution.py:329
  157.3 0.0 collective-permute-done.8
  157.3 0.0 copy-done.1
  157.3 1.9 add_convert_fusion
  159.2 13.0 %all-to-all-done.1 = bf16[8,12,32,128]{3,2,1,0:T(8,128)(2,1)} async-done(((bf16[8,12,32,128]{3,2,1,0:T(8,128)(2,1)}), bf16[8,12,32,128]{3,2,1,0:T(8,128)(2,1)}, u32[]{:S(2)}, u32[]{:S(2)}) %all-to-all-start.1) | async-done | bytes 786464 | tf_op jit(solution)/shard_map/all_to_all | solution.py:329
  172.2 23.4 %all_to_all.20 = bf16[8,2,2,128,128]{4,3,2,1,0:T(8,128)(2,1)S(1)} all-to-all(bf16[8,2,2,128,128]{4,3,2,1,0:T(8,128)(2,1)S(1)} %add_convert_fusion), channel_id=1, replica_groups=mesh['zl'=2,'yh'=2,'yp'=2,'x'=4,'zh'=2,'core'=2] {'yh','x'}, dimensions={0} | all-to-all | bytes 2097152 | tf_op jit(solution)/shard_map/all_to_all | solution.py:331
  195.6 0.1 convert_reduce_fusion.1
  195.8 0.1 select_convert_fusion.1
  195.9 0.7 collective-permute-start.9
  196.6 0.1 collective-permute-start.10
  196.7 1.3 bitcast_convert_fusion
  198.0 2.1 %copy.44 = f32[96,32,128]{2,0,1:T(8,128)} copy(f32[96,32,128]{2,1,0:T(8,128)S(1)} %bitcast_convert_fusion) | data formatting | bytes 3145728 | tf_op jit(solution)/shard_map/convert_element_type | solution.py:333
  200.1 0.0 collective-permute-done.9
  200.1 1.5 collective-permute-done.10
  201.7 1.2 fusion.3
  (16 shorter events, 0.3 us)
Async XLA Ops:
  0.6 6.7 %collective-permute-start.2 = (s32[2]{0:T(128)}, s32[2]{0:T(128)S(1)}, u32[]{:S(2)}, u32[]{:S(2)}) collective-permute-start(s32[2]{0:T(128)} %param.14), channel_id=1, source_target_pairs={{0,0},{1,16},{16,1},{17,17},{2,2},{3,18},{18,3},{19,19},{4,4},{5,2... | collective-permute-start | bytes 32 | tf_op jit(solution)/shard_map/ppermute | solution.py:292
  1.9 10.8 %copy-start.6 = (bf16[32,96,128]{2,1,0:T(8,128)(2,1)S(1)}, bf16[32,96,128]{2,1,0:T(8,128)(2,1)}, u32[]{:S(2)}) copy-start(bf16[32,96,128]{2,1,0:T(8,128)(2,1)} %param.8) | copy-start | bytes 2359300
  3.9 9.2 %copy-start.7 = (bf16[32,96,128]{2,1,0:T(8,128)(2,1)S(1)}, bf16[32,96,128]{2,1,0:T(8,128)(2,1)}, u32[]{:S(2)}) copy-start(bf16[32,96,128]{2,1,0:T(8,128)(2,1)} %param.15) | copy-start | bytes 2359300
  3.9 5.3 %collective-permute-start.1 = (bf16[2,2,128,128]{3,2,1,0:T(8,128)(2,1)S(1)}, bf16[2,2,128,128]{3,2,1,0:T(8,128)(2,1)S(1)}, u32[]{:S(2)}, u32[]{:S(2)}) collective-permute-start(bf16[2,2,128,128]{3,2,1,0:T(8,128)(2,1)S(1)} %get-tuple-element.55), channel_id=1, source_target_pairs={{0,64},{1,80},{16,65},{17,81},{64,0},{65,16},{80,1},{81,17},{2,66}... | collective-permute-start | bytes 393224 | tf_op jit(solution)/shard_map/ppermute | solution.py:278
  6.0 3.2 %collective-permute-start = (bf16[2,2,128,128]{3,2,1,0:T(8,128)(2,1)S(1)}, bf16[2,2,128,128]{3,2,1,0:T(8,128)(2,1)S(1)}, u32[]{:S(2)}, u32[]{:S(2)}) collective-permute-start(bf16[2,2,128,128]{3,2,1,0:T(8,128)(2,1)S(1)} %get-tuple-element.56), channel_id=1, source_target_pairs={{0,0},{1,16},{16,1},{17,17},{64,64},{65,80},{80,65},{81,81},{2,2},... | collective-permute-start | bytes 393224 | tf_op jit(solution)/shard_map/ppermute | solution.py:278
  9.5 16.6 %collective-permute-start.3 = (bf16[2,2,2,128,128]{4,3,2,1,0:T(8,128)(2,1)S(1)}, bf16[2,2,2,128,128]{4,3,2,1,0:T(8,128)(2,1)S(1)}, u32[]{:S(2)}, u32[]{:S(2)}) collective-permute-start(bf16[2,2,2,128,128]{4,3,2,1,0:T(8,128)(2,1)S(1)} %pad_maximum_fusion.4), channel_id=1, source_target_pairs={{0,32},{32,0},{1,33},{33,1},{2,34},{34,2},{3,35},{35,3},{4,36},{36... | collective-permute-start | bytes 786440 | tf_op jit(solution)/shard_map/ppermute | solution.py:313
  15.0 38.3 %all-to-all-start = ((bf16[8,2,12,32,128]{4,3,2,1,0:T(8,128)(2,1)}), bf16[8,2,12,32,128]{4,3,2,1,0:T(8,128)(2,1)}, u32[]{:S(2)}, u32[]{:S(2)}) async-start(bf16[8,2,12,32,128]{4,3,2,1,0:T(8,128)(2,1)} %copy.36), calls=%async_computation | async-start | bytes 3145728 | tf_op jit(solution)/shard_map/all_to_all | solution.py:299
  26.2 16.5 %collective-permute-start.5 = (bf16[2,2,2,2,128,128]{5,4,3,2,1,0:T(8,128)(2,1)S(1)}, bf16[2,2,2,2,128,128]{5,4,3,2,1,0:T(8,128)(2,1)S(1)}, u32[]{:S(2)}, u32[]{:S(2)}) collective-permute-start(bf16[2,2,2,2,128,128]{5,4,3,2,1,0:T(8,128)(2,1)S(1)} %get-tuple-element.42), channel_id=1, source_target_pairs={{8,0},{12,4},{0,8},{4,12},{9,1},{13,5},{1,9},{5,13},{10,2},{14,6},... | collective-permute-start | bytes 1572872 | tf_op jit(solution)/shard_map/ppermute | solution.py:282
  29.3 23.1 %collective-permute-start.4 = (bf16[2,2,2,2,128,128]{5,4,3,2,1,0:T(8,128)(2,1)S(1)}, bf16[2,2,2,2,128,128]{5,4,3,2,1,0:T(8,128)(2,1)S(1)}, u32[]{:S(2)}, u32[]{:S(2)}) collective-permute-start(bf16[2,2,2,2,128,128]{5,4,3,2,1,0:T(8,128)(2,1)S(1)} %get-tuple-element.42), channel_id=1, source_target_pairs={{4,0},{8,4},{12,8},{0,12},{5,1},{9,5},{13,9},{1,13},{6,2},{10,6},{... | collective-permute-start | bytes 1572872 | tf_op jit(solution)/shard_map/ppermute | solution.py:282
  30.4 22.0 %collective-permute-start.6 = (bf16[2,2,2,2,128,128]{5,4,3,2,1,0:T(8,128)(2,1)S(1)}, bf16[2,2,2,2,128,128]{5,4,3,2,1,0:T(8,128)(2,1)S(1)}, u32[]{:S(2)}, u32[]{:S(2)}) collective-permute-start(bf16[2,2,2,2,128,128]{5,4,3,2,1,0:T(8,128)(2,1)S(1)} %get-tuple-element.42), channel_id=1, source_target_pairs={{12,0},{0,4},{4,8},{8,12},{13,1},{1,5},{5,9},{9,13},{14,2},{2,6},{... | collective-permute-start | bytes 1572872 | tf_op jit(solution)/shard_map/ppermute | solution.py:282
  53.3 4.4 %collective-permute-start.7 = (bf16[8,2,2,2,128,128]{5,4,3,2,1,0:T(8,128)(2,1)S(1)}, bf16[8,2,2,2,128,128]{5,4,3,2,1,0:T(8,128)(2,1)}, u32[]{:S(2)}, u32[]{:S(2)}) collective-permute-start(bf16[8,2,2,2,128,128]{5,4,3,2,1,0:T(8,128)(2,1)S(1)} %bitcast.72), channel_id=1, source_target_pairs={{0,1},{1,0},{2,3},{3,2},{4,5},{5,4},{6,7},{7,6},{8,9},{9,8},{10,11... | collective-permute-start | bytes 6291464 | tf_op jit(solution)/shard_map/ppermute | solution.py:319
  111.8 1.4 copy-start.2
  113.2 1.1 copy-start.4
  114.3 36.2 %all-to-all-start.2 = ((bf16[16,2,2,128,128]{4,3,2,1,0:T(8,128)(2,1)}), bf16[16,2,2,128,128]{4,3,2,1,0:T(8,128)(2,1)}, u32[]{:S(2)}, u32[]{:S(2)}) async-start(bf16[16,2,2,128,128]{4,3,2,1,0:T(8,128)(2,1)} %copy-done.2), calls=%async_computation.2 | async-start | bytes 4194304 | tf_op jit(solution)/shard_map/all_to_all | solution.py:286
  119.4 1.4 copy-start.5
  147.7 1.4 copy-start
  149.0 1.4 copy-start.3
  150.5 6.8 %copy-start.1 = (f32[8,2,2,128,128]{4,3,2,1,0:T(8,128)S(1)}, f32[8,2,2,128,128]{4,3,2,1,0:T(8,128)}, u32[]{:S(2)}) copy-start(f32[8,2,2,128,128]{4,3,2,1,0:T(8,128)} %copy-done) | copy-start | bytes 6291460
  152.6 4.7 %collective-permute-start.8 = (f32[8,2,2,128,128]{4,3,2,1,0:T(8,128)}, f32[8,2,2,128,128]{4,3,2,1,0:T(8,128)}, u32[]{:S(2)}, u32[]{:S(2)}) collective-permute-start(f32[8,2,2,128,128]{4,3,2,1,0:T(8,128)} %copy-done.3), channel_id=1, source_target_pairs={{0,1},{1,0},{2,3},{3,2},{4,5},{5,4},{6,7},{7,6},{8,9},{9,8},{10,11... | collective-permute-start | bytes 6291464 | tf_op jit(solution)/shard_map/ppermute | solution.py:328
  152.9 19.3 %all-to-all-start.1 = ((bf16[8,12,32,128]{3,2,1,0:T(8,128)(2,1)}), bf16[8,12,32,128]{3,2,1,0:T(8,128)(2,1)}, u32[]{:S(2)}, u32[]{:S(2)}) async-start(bf16[8,12,32,128]{3,2,1,0:T(8,128)(2,1)} %get-tuple-element.25), calls=%async_computation.1 | async-start | bytes 1572864 | tf_op jit(solution)/shard_map/all_to_all | solution.py:329
  195.9 4.2 %collective-permute-start.9 = (bf16[2,2,128,128]{3,2,1,0:T(8,128)(2,1)S(1)}, bf16[2,2,128,128]{3,2,1,0:T(8,128)(2,1)S(1)}, u32[]{:S(2)}, u32[]{:S(2)}) collective-permute-start(bf16[2,2,128,128]{3,2,1,0:T(8,128)(2,1)S(1)} %get-tuple-element.51), channel_id=1, source_target_pairs={{0,0},{1,16},{16,1},{17,17},{64,64},{65,80},{80,65},{81,81},{2,2},... | collective-permute-start | bytes 393224 | tf_op jit(solution)/shard_map/ppermute | solution.py:278
  196.6 5.0 %collective-permute-start.10 = (bf16[2,2,128,128]{3,2,1,0:T(8,128)(2,1)S(1)}, bf16[2,2,128,128]{3,2,1,0:T(8,128)(2,1)S(1)}, u32[]{:S(2)}, u32[]{:S(2)}) collective-permute-start(bf16[2,2,128,128]{3,2,1,0:T(8,128)(2,1)S(1)} %get-tuple-element.52), channel_id=1, source_target_pairs={{0,64},{1,80},{16,65},{17,81},{64,0},{65,16},{80,1},{81,17},{2,66}... | collective-permute-start | bytes 393224 | tf_op jit(solution)/shard_map/ppermute | solution.py:278
